TPU v7x, 512 devices: a whole 4x8x8 slice. The times are simulated.
512 devices in a mesh: seg: 8 (over x, core), blk: 64 (over z, y).
Axes of the slice: x: 4, y: 8, z: 8, core: 2. Of those that a mesh axis runs over, the one named last changes fastest.
Arguments:
- two_site: float32 [8, 64, 128, 128], P('seg', 'blk'), may hold values from -6 to 6
- diag_left: float32 [8, 64, 2, 128, 128], P('seg', 'blk')
- diag_right: float32 [8, 64, 2, 128, 128], P('seg', 'blk')
- hop_left: float32 [8, 64, 16, 128, 128], P('seg', 'blk'), may hold values from -0.125 to 0.125
- hop_right: float32 [8, 64, 16, 128, 128], P('seg', 'blk'), may hold values from -0.125 to 0.125
- sector_sizes: int32 [8, 64], P('seg', 'blk'), may hold values from 1 to 128, 6144 in all within a row
- ranks: int32 [8, 64], P('seg', 'blk'), may hold values from 1 to 128
Outputs:
- new_state: float32 [8, 64, 128, 128], P('seg', 'blk')
- left_boundary: float32 [8, 64, 18, 128, 128], P('seg', 'blk')
- right_boundary: float32 [8, 64, 18, 128, 128], P('seg', 'blk')
- energy: float32 [8], P('seg')
Inputs may be any that keep to these rules, and one draw needn't show every extreme that they name: Each row of sector_sizes sums to 6144; the largest entry of every row is 128.
All inputs are finite; a program needn't handle non-finite values. No bound on the sum of `sector_sizes` on one device may be relied on, other than what follows from the above.
Results may differ from a plain program's by a relative error of at most 0.0003.
Values sent between devices are 32-bit elements; how exact they have to be, the bound alone decides.
No kernel may reach another device: no remote copies, remote signals or barrier semaphores. Data moves between devices by JAX's collectives and lax.ppermute only.
A program may use at most 64 MiB of HBM per device.

v0:
```python
import jax
import jax.numpy as jnp
from jax import lax
from jax.sharding import PartitionSpec as P

ITERS = 4


highest = lax.Precision.HIGHEST
spectral_shift = 20.0


def padded_2(block, sides, width):
    for axis, dim in sides:
        count = lax.axis_size(axis)
        forward = [(i, i + 1) for i in range(count - 1)]
        backward = [(target, source) for source, target in forward]
        low = lax.ppermute(
            lax.slice_in_dim(block, block.shape[dim] - width, None, axis=dim), axis, forward
        )
        high = lax.ppermute(lax.slice_in_dim(block, 0, width, axis=dim), axis, backward)
        block = jnp.concatenate([low, block, high], axis=dim)
    return block


def passed_along(value, axis, steps):
    count = lax.axis_size(axis)
    leading, last = (max(0, -steps), min(count, count - steps))
    return lax.ppermute(value, axis, [(source, source + steps) for source in range(leading, last)])


def channel_apply(left_ops, vector, right_ops):
    halfway = jnp.einsum("qwij,qjk->qwik", left_ops, vector, precision=highest)
    return jnp.einsum("qwik,qwlk->qil", halfway, right_ops, precision=highest)


def channel_adjoint(left_ops, vector, right_ops):
    halfway = jnp.einsum("qwji,qjk->qwik", left_ops, vector, precision=highest)
    return jnp.einsum("qwik,qwkl->qil", halfway, right_ops, precision=highest)


def left_extend(kept_state, left_ops):
    halfway = jnp.einsum("qwij,qjl->qwil", left_ops, kept_state, precision=highest)
    return jnp.einsum("qik,qwil->qwkl", kept_state, halfway, precision=highest)


def right_extend(kept_state, right_ops):
    halfway = jnp.einsum("qik,qwlk->qwil", kept_state, right_ops, precision=highest)
    return jnp.einsum("qwil,qjl->qwij", halfway, kept_state, precision=highest)


def shards(two_site, diag_left, diag_right, hop_left, hop_right, sector_sizes, ranks):
    block_size = two_site.shape[2]
    positions = jnp.arange(block_size, dtype=jnp.int32)
    sector_size = sector_sizes[0]
    row_live = (positions[None, :] < sector_size[:, None]).astype(jnp.float32)
    live_mask = row_live[:, :, None] * row_live[:, None, :]
    keep_left = diag_left[0]
    keep_right = diag_right[0]
    raise_left = hop_left[0]
    raise_right = hop_right[0]
    vector = live_mask * two_site[0]
    last_vector = vector
    last_applied = vector
    for iteration in range(ITERS):
        own_terms = channel_apply(keep_left, vector, keep_right)
        carried = channel_adjoint(raise_left, vector, raise_right)
        stacked = jnp.stack([vector, carried], 0)
        padded = padded_2(stacked, (("blk", 1),), 1)
        previous = padded[0, :-2]
        following = padded[1, 2:]
        applied = live_mask * (
            own_terms + channel_apply(raise_left, previous, raise_right) + following
        )
        last_vector = vector
        last_applied = applied
        vector = spectral_shift * vector - applied
    quotient_top, quotient_low, final_sq, bond_total = lax.psum(
        (
            jnp.sum(last_vector * last_applied),
            jnp.sum(last_vector * last_vector),
            jnp.sum(vector * vector),
            jnp.sum(sector_size).astype(jnp.float32),
        ),
        "blk",
    )
    energy = quotient_top / quotient_low
    new_state = vector * jnp.sqrt(bond_total * block_size / final_sq)
    kept_count = jnp.minimum(ranks[0], sector_size)
    col_live = (positions[None, :] < kept_count[:, None]).astype(jnp.float32)
    kept_state = new_state * col_live[:, None, :]
    scale = 1.0 / jnp.sqrt(jnp.float32(block_size))
    new_left = (
        jnp.concatenate(
            [left_extend(kept_state, keep_left), left_extend(kept_state, raise_left)], 1
        )
        * scale
    )
    new_right = (
        jnp.concatenate(
            [right_extend(kept_state, keep_right), right_extend(kept_state, raise_right)], 1
        )
        * scale
    )
    left_boundary = passed_along(new_left, "seg", 1)
    right_boundary = passed_along(new_right, "seg", -1)
    return (new_state[None], left_boundary[None], right_boundary[None], jnp.reshape(energy, (1,)))


def solution(mesh):
    return jax.shard_map(
        shards,
        mesh=mesh,
        in_specs=(
            P("seg", "blk", None, None),
            P("seg", "blk", None, None, None),
            P("seg", "blk", None, None, None),
            P("seg", "blk", None, None, None),
            P("seg", "blk", None, None, None),
            P("seg", "blk"),
            P("seg", "blk"),
        ),
        out_specs=(
            P("seg", "blk", None, None),
            P("seg", "blk", None, None, None),
            P("seg", "blk", None, None, None),
            P("seg"),
        ),
        check_vma=False,
    )
```

profile of v0, /device:TPU:1, one launch (start us, length us, event | category | flops | bytes accessed | tf_op | source)
XLA Modules:
  0.0 249.5 jit_solution(16559540481740805035)
XLA Ops:
  1.5 0.9 multiply_multiply_fusion.5
  2.4 1.8 convolution_bitcast_fusion.11
  4.2 1.1 convolution_bitcast_fusion.30
  5.4 1.3 collective-permute-start.1
  6.7 4.7 %collective-permute-start = (f32[2,1,128,128]{3,2,1,0:T(8,128)S(1)}, f32[2,1,128,128]{3,2,1,0:T(8,128)S(1)}, u32[]{:S(2)}, u32[]{:S(2)}) collective-permute-start(f32[2,1,128,128]{3,2,1,0:T(8,128)S(1)} %pad_maximum_fusion), channel_id=1, source_target_pairs={{0,1},{1,2},{2,3},{3,4},{4,5},{5,6},{6,7},{7,8},{8,9},{9,10},{10,1... | collective-permute-start | bytes 393224 | tf_op jit(solution)/shard_map/ppermute | solution.py:18
  12.3 1.0 collective-permute-done
  13.3 1.0 convolution_bitcast_fusion.10
  14.3 1.0 convolution_bitcast_fusion.29
  15.3 0.3 fusion.33
  15.6 1.8 convolution_bitcast_fusion.9
  17.4 1.1 convolution_bitcast_fusion.27
  18.6 1.3 collective-permute-start.3
  19.9 4.6 %collective-permute-start.2 = (f32[2,1,128,128]{3,2,1,0:T(8,128)S(1)}, f32[2,1,128,128]{3,2,1,0:T(8,128)S(1)}, u32[]{:S(2)}, u32[]{:S(2)}) collective-permute-start(f32[2,1,128,128]{3,2,1,0:T(8,128)S(1)} %pad_maximum_fusion.1), channel_id=1, source_target_pairs={{0,1},{1,2},{2,3},{3,4},{4,5},{5,6},{6,7},{7,8},{8,9},{9,10},{10,1... | collective-permute-start | bytes 393224 | tf_op jit(solution)/shard_map/ppermute | solution.py:18
  24.8 1.5 collective-permute-done.2
  26.2 1.0 convolution_bitcast_fusion.8
  27.2 1.0 convolution_bitcast_fusion.26
  28.2 0.3 fusion.34
  28.5 1.8 convolution_bitcast_fusion.7
  30.3 1.1 convolution_bitcast_fusion.24
  31.5 1.3 collective-permute-start.5
  32.8 4.4 %collective-permute-start.4 = (f32[2,1,128,128]{3,2,1,0:T(8,128)S(1)}, f32[2,1,128,128]{3,2,1,0:T(8,128)S(1)}, u32[]{:S(2)}, u32[]{:S(2)}) collective-permute-start(f32[2,1,128,128]{3,2,1,0:T(8,128)S(1)} %pad_maximum_fusion.2), channel_id=1, source_target_pairs={{0,1},{1,2},{2,3},{3,4},{4,5},{5,6},{6,7},{7,8},{8,9},{9,10},{10,1... | collective-permute-start | bytes 393224 | tf_op jit(solution)/shard_map/ppermute | solution.py:18
  37.5 1.7 collective-permute-done.4
  39.1 1.0 convolution_bitcast_fusion.6
  40.1 1.0 convolution_bitcast_fusion.23
  41.1 0.3 fusion.35
  41.4 1.8 convolution_bitcast_fusion.5
  43.2 1.1 convolution_bitcast_fusion.21
  44.4 1.3 collective-permute-start.7
  45.7 4.6 %collective-permute-start.6 = (f32[2,1,128,128]{3,2,1,0:T(8,128)S(1)}, f32[2,1,128,128]{3,2,1,0:T(8,128)S(1)}, u32[]{:S(2)}, u32[]{:S(2)}) collective-permute-start(f32[2,1,128,128]{3,2,1,0:T(8,128)S(1)} %pad_maximum_fusion.3), channel_id=1, source_target_pairs={{0,1},{1,2},{2,3},{3,4},{4,5},{5,6},{6,7},{7,8},{8,9},{9,10},{10,1... | collective-permute-start | bytes 393224 | tf_op jit(solution)/shard_map/ppermute | solution.py:18
  50.6 1.4 collective-permute-done.6
  52.0 1.0 convolution_bitcast_fusion.4
  53.0 1.0 convolution_bitcast_fusion.20
  54.0 0.9 multiply_reduce_fusion
  54.9 128.3 %all-reduce = (f32[]{:T(128)}, f32[]{:T(128)}, f32[]{:T(128)}, f32[]{:T(128)}) all-reduce(f32[]{:T(128)S(6)} %convert_element_type.26, f32[]{:T(128)} %get-tuple-element.16, f32[]{:T(128)} %get-tuple-element.9, f32[]{:T(128)} %get-tuple-element.8), channel_id=1, replica_groups=mesh['seg'=8,'blk'=64] {'blk'}, use_global_device_ids=true, to_apply=%region_0.0 | all-reduce | flops 4 | bytes 32 | tf_op jit(solution)/shard_map/psum | solution.py:78
  184.9 0.3 convolution_bitcast_fusion.15
  185.2 1.0 convolution_bitcast_fusion.1
  186.2 1.1 convolution_bitcast_fusion.3
  187.3 0.3 convolution_bitcast_fusion.12
  187.9 1.1 convolution_bitcast_fusion
  189.0 1.0 convolution_bitcast_fusion.2
  190.1 36.7 %collective-permute-start.8 = (f32[1,18,128,128]{2,3,1,0:T(8,128)S(1)}, f32[1,18,128,128]{2,3,1,0:T(8,128)}, u32[]{:S(2)}, u32[]{:S(2)}) collective-permute-start(f32[1,18,128,128]{2,3,1,0:T(8,128)S(1)} %maximum_multiply_fusion), channel_id=1, source_target_pairs={{0,64},{64,128},{128,192},{192,256},{256,320},{320,384},{384,448},... | collective-permute-start | bytes 3538952 | tf_op jit(solution)/shard_map/ppermute | solution.py:29
  226.8 1.1 maximum_multiply_fusion.1
  227.9 1.9 collective-permute-start.9
  231.2 0.6 multiply_bitcast_fusion
  231.8 8.1 %collective-permute-done.8 = f32[1,18,128,128]{2,3,1,0:T(8,128)} collective-permute-done((f32[1,18,128,128]{2,3,1,0:T(8,128)S(1)}, f32[1,18,128,128]{2,3,1,0:T(8,128)}, u32[]{:S(2)}, u32[]{:S(2)}) %collective-permute-start.8) | collective-permute-done | bytes 1179680 | tf_op jit(solution)/shard_map/ppermute | solution.py:29
  239.9 2.7 %copy.13 = f32[1,1,18,128,128]{4,3,2,1,0:T(8,128)} copy(f32[1,1,18,128,128]{3,4,2,1,0:T(8,128)} %bitcast.68) | data formatting | bytes 2359296
  242.6 3.2 %collective-permute-done.9 = f32[1,18,128,128]{2,3,1,0:T(8,128)} collective-permute-done((f32[1,18,128,128]{2,3,1,0:T(8,128)}, f32[1,18,128,128]{2,3,1,0:T(8,128)}, u32[]{:S(2)}, u32[]{:S(2)}) %collective-permute-start.9) | collective-permute-done | bytes 1179680 | tf_op jit(solution)/shard_map/ppermute | solution.py:29
  245.8 2.7 %copy.14 = f32[1,1,18,128,128]{4,3,2,1,0:T(8,128)} copy(f32[1,1,18,128,128]{3,4,2,1,0:T(8,128)} %bitcast.79) | data formatting | bytes 2359296
  (27 shorter events, 1.8 us)
Async XLA Ops:
  0.6 1.8 copy-start
  0.6 3.6 %copy-start.1 = (f32[1,1,16,128,128]{4,3,2,1,0:T(8,128)S(1)}, f32[1,1,16,128,128]{4,3,2,1,0:T(8,128)}, u32[]{:S(2)}) copy-start(f32[1,1,16,128,128]{4,3,2,1,0:T(8,128)} %param.11) | copy-start | bytes 3145732
  4.2 7.1 %copy-start.2 = (f32[1,1,2,128,128]{4,3,2,1,0:T(8,128)S(1)}, f32[1,1,2,128,128]{4,3,2,1,0:T(8,128)}, u32[]{:S(2)}) copy-start(f32[1,1,2,128,128]{4,3,2,1,0:T(8,128)} %param.8) | copy-start | bytes 393220
  5.4 9.9 %collective-permute-start.1 = (f32[2,1,128,128]{3,2,1,0:T(8,128)S(1)}, f32[2,1,128,128]{3,2,1,0:T(8,128)S(1)}, u32[]{:S(2)}, u32[]{:S(2)}) collective-permute-start(f32[2,1,128,128]{3,2,1,0:T(8,128)S(1)} %pad_maximum_fusion), channel_id=1, source_target_pairs={{1,0},{2,1},{3,2},{4,3},{5,4},{6,5},{7,6},{8,7},{9,8},{10,9},{11,1... | collective-permute-start | bytes 393224 | tf_op jit(solution)/shard_map/ppermute | solution.py:21
  6.7 6.6 %collective-permute-start = (f32[2,1,128,128]{3,2,1,0:T(8,128)S(1)}, f32[2,1,128,128]{3,2,1,0:T(8,128)S(1)}, u32[]{:S(2)}, u32[]{:S(2)}) collective-permute-start(f32[2,1,128,128]{3,2,1,0:T(8,128)S(1)} %pad_maximum_fusion), channel_id=1, source_target_pairs={{0,1},{1,2},{2,3},{3,4},{4,5},{5,6},{6,7},{7,8},{8,9},{9,10},{10,1... | collective-permute-start | bytes 393224 | tf_op jit(solution)/shard_map/ppermute | solution.py:18
  14.3 1.0 copy-start.3
  14.3 1.0 copy-start.4
  18.6 9.6 %collective-permute-start.3 = (f32[2,1,128,128]{3,2,1,0:T(8,128)S(1)}, f32[2,1,128,128]{3,2,1,0:T(8,128)S(1)}, u32[]{:S(2)}, u32[]{:S(2)}) collective-permute-start(f32[2,1,128,128]{3,2,1,0:T(8,128)S(1)} %pad_maximum_fusion.1), channel_id=1, source_target_pairs={{1,0},{2,1},{3,2},{4,3},{5,4},{6,5},{7,6},{8,7},{9,8},{10,9},{11,1... | collective-permute-start | bytes 393224 | tf_op jit(solution)/shard_map/ppermute | solution.py:21
  19.9 6.3 %collective-permute-start.2 = (f32[2,1,128,128]{3,2,1,0:T(8,128)S(1)}, f32[2,1,128,128]{3,2,1,0:T(8,128)S(1)}, u32[]{:S(2)}, u32[]{:S(2)}) collective-permute-start(f32[2,1,128,128]{3,2,1,0:T(8,128)S(1)} %pad_maximum_fusion.1), channel_id=1, source_target_pairs={{0,1},{1,2},{2,3},{3,4},{4,5},{5,6},{6,7},{7,8},{8,9},{9,10},{10,1... | collective-permute-start | bytes 393224 | tf_op jit(solution)/shard_map/ppermute | solution.py:18
  31.5 9.6 %collective-permute-start.5 = (f32[2,1,128,128]{3,2,1,0:T(8,128)S(1)}, f32[2,1,128,128]{3,2,1,0:T(8,128)S(1)}, u32[]{:S(2)}, u32[]{:S(2)}) collective-permute-start(f32[2,1,128,128]{3,2,1,0:T(8,128)S(1)} %pad_maximum_fusion.2), channel_id=1, source_target_pairs={{1,0},{2,1},{3,2},{4,3},{5,4},{6,5},{7,6},{8,7},{9,8},{10,9},{11,1... | collective-permute-start | bytes 393224 | tf_op jit(solution)/shard_map/ppermute | solution.py:21
  32.8 6.3 %collective-permute-start.4 = (f32[2,1,128,128]{3,2,1,0:T(8,128)S(1)}, f32[2,1,128,128]{3,2,1,0:T(8,128)S(1)}, u32[]{:S(2)}, u32[]{:S(2)}) collective-permute-start(f32[2,1,128,128]{3,2,1,0:T(8,128)S(1)} %pad_maximum_fusion.2), channel_id=1, source_target_pairs={{0,1},{1,2},{2,3},{3,4},{4,5},{5,6},{6,7},{7,8},{8,9},{9,10},{10,1... | collective-permute-start | bytes 393224 | tf_op jit(solution)/shard_map/ppermute | solution.py:18
  44.4 9.6 %collective-permute-start.7 = (f32[2,1,128,128]{3,2,1,0:T(8,128)S(1)}, f32[2,1,128,128]{3,2,1,0:T(8,128)S(1)}, u32[]{:S(2)}, u32[]{:S(2)}) collective-permute-start(f32[2,1,128,128]{3,2,1,0:T(8,128)S(1)} %pad_maximum_fusion.3), channel_id=1, source_target_pairs={{1,0},{2,1},{3,2},{4,3},{5,4},{6,5},{7,6},{8,7},{9,8},{10,9},{11,1... | collective-permute-start | bytes 393224 | tf_op jit(solution)/shard_map/ppermute | solution.py:21
  45.7 6.3 %collective-permute-start.6 = (f32[2,1,128,128]{3,2,1,0:T(8,128)S(1)}, f32[2,1,128,128]{3,2,1,0:T(8,128)S(1)}, u32[]{:S(2)}, u32[]{:S(2)}) collective-permute-start(f32[2,1,128,128]{3,2,1,0:T(8,128)S(1)} %pad_maximum_fusion.3), channel_id=1, source_target_pairs={{0,1},{1,2},{2,3},{3,4},{4,5},{5,6},{6,7},{7,8},{8,9},{9,10},{10,1... | collective-permute-start | bytes 393224 | tf_op jit(solution)/shard_map/ppermute | solution.py:18
  190.1 49.9 %collective-permute-start.8 = (f32[1,18,128,128]{2,3,1,0:T(8,128)S(1)}, f32[1,18,128,128]{2,3,1,0:T(8,128)}, u32[]{:S(2)}, u32[]{:S(2)}) collective-permute-start(f32[1,18,128,128]{2,3,1,0:T(8,128)S(1)} %maximum_multiply_fusion), channel_id=1, source_target_pairs={{0,64},{64,128},{128,192},{192,256},{256,320},{320,384},{384,448},... | collective-permute-start | bytes 3538952 | tf_op jit(solution)/shard_map/ppermute | solution.py:29
  227.9 17.8 %collective-permute-start.9 = (f32[1,18,128,128]{2,3,1,0:T(8,128)}, f32[1,18,128,128]{2,3,1,0:T(8,128)}, u32[]{:S(2)}, u32[]{:S(2)}) collective-permute-start(f32[1,18,128,128]{2,3,1,0:T(8,128)} %maximum_multiply_fusion.1), channel_id=1, source_target_pairs={{64,0},{128,64},{192,128},{256,192},{320,256},{384,320},{448,384},... | collective-permute-start | bytes 3538952 | tf_op jit(solution)/shard_map/ppermute | solution.py:29
where the time goes:
time: 250 us
  blocking collectives  128 us (51%)
  starting transfers between devices  62.1 us (25%)
  matrix products  27.7 us (11%)
  waiting for transfers between devices  16.8 us (7%)
  between operations  6.41 us (3%)
  local copies, waits for them, and re-layouts  5.34 us (2%)
  other arithmetic  2.86 us (1%)
    psum x1, blocking collectives, shards(): lax.psum((jnp.sum(last_vector * last_applied), jnp.sum(last_vector * last...  128 us
    ppermute x2, starting transfers between devices, passed_along(): lax.ppermute(value, axis, [(source, source + steps) for source in range(l...  38.6 us
    ppermute x4, starting transfers between devices, padded_2(): lax.ppermute(lax.slice_in_dim(block, block.shape[dim] - width, None, axis...  18.3 us
    ppermute x2, waiting for transfers between devices, passed_along(): lax.ppermute(value, axis, [(source, source + steps) for source in range(l...  11.3 us
    dot_general x4, matrix products, channel_adjoint(): halfway = jnp.einsum('qwji,qjk->qwik', left_ops, vector, precision=highest)  7.22 us
    dot_general x8, matrix products, channel_apply(): return jnp.einsum('qwik,qwlk->qil', halfway, right_ops, precision=highest)  5.73 us
    ppermute x4, waiting for transfers between devices, padded_2(): lax.ppermute(lax.slice_in_dim(block, block.shape[dim] - width, None, axis...  5.54 us
    unnamed x12, local copies, waits for them, and re-layouts  5.34 us
  transfers between devices with their start and end apart: 10, of which 6 were waited for; matrix products, arithmetic and copies ran while one was open for 5% of the time, Pallas kernels for 0%

commit v1 on v0

v1 whole, which is shorter than its diff:
```python
import functools
import math

import jax
import jax.numpy as jnp
from jax import lax
from jax.experimental import pallas as pl
from jax.experimental.pallas import tpu as pltpu
from jax.sharding import PartitionSpec as P

ITERS = 4
SHIFT = 20.0
BOND = 6144.0
f32 = jnp.float32
bf16 = jnp.bfloat16
VMEM = pl.BlockSpec(memory_space=pltpu.VMEM)
SMEM = pl.BlockSpec(memory_space=pltpu.SMEM)
HBM = pl.BlockSpec(memory_space=pl.ANY)
SDS = jax.ShapeDtypeStruct


def dot(a, b):
    return jnp.dot(a, b, preferred_element_type=f32)


def split(x):
    high = x.astype(bf16)
    return high, (x - high.astype(f32)).astype(bf16)


def weight(x):
    high, low = split(x)
    row = jnp.concatenate([high, low], 1)
    return jnp.concatenate([row, row], 0)


def folded(t):
    n = t.shape[1] // 2
    return t[:, :n] + t[:, n:]


def sandwich(p_ref, q_ref, x):
    n = x.shape[0]
    w = weight(x)
    total = None
    for pair in range(p_ref.shape[0] // (2 * n)):
        rows = pl.ds(pair * 2 * n, 2 * n)
        t = folded(dot(p_ref[rows, :], w))
        high, low = split(t)
        lhs = jnp.concatenate(
            [
                jnp.concatenate([high[:n], high[n:]], 1),
                jnp.concatenate([low[:n], low[n:]], 1),
            ],
            0,
        )
        term = dot(lhs, q_ref[rows, :])
        total = term if total is None else total + term
    total = folded(total)
    return total[:n] + total[n:]


def square_mask(size):
    n = size.shape[1]
    size = jnp.broadcast_to(size, (n, n))
    rows = lax.broadcasted_iota(jnp.int32, (n, n), 0).astype(f32)
    cols = lax.broadcasted_iota(jnp.int32, (n, n), 1).astype(f32)
    return (rows < size) & (cols < size)


def where(mask, x):
    return jnp.where(mask, x, 0.0)


def put_parts(out_ref, h, n, x):
    high, low = split(x)
    out_ref[pl.ds(h * n, n), :n] = high
    out_ref[pl.ds(h * n, n), n:] = low


def first_message(size_ref, x_ref, out_ref):
    n = x_ref.shape[0]
    size = jnp.full((1, n), size_ref[0, 0].astype(f32), f32)
    out_ref[:n, :] = where(square_mask(size), x_ref[...])
    out_ref[n:, :] = jnp.broadcast_to(size, (8, n))


def first_adjoint(own_ref, hl_ref, hr_ref, dl_ref, dr_ref, lt_ref, rc_ref, dlt_ref, drc_ref, b_ref):
    n = own_ref.shape[1]
    for h in range(hl_ref.shape[0]):
        put_parts(lt_ref, h, n, hl_ref[h].T)
        put_parts(rc_ref, h, n, hr_ref[h])
    for h in range(dl_ref.shape[0]):
        put_parts(dlt_ref, h, n, dl_ref[h].T)
        put_parts(drc_ref, h, n, dr_ref[h])
    b_ref[...] = sandwich(lt_ref, rc_ref, own_ref[:n, :])


def adjoint(own_ref, a_ref, got_b_ref, lt_ref, rc_ref, v_ref, b_ref):
    n = own_ref.shape[1]
    v = a_ref[...] - where(square_mask(own_ref[n : n + 1, :]), got_b_ref[...])
    v_ref[...] = v
    b_ref[...] = sandwich(lt_ref, rc_ref, v)


def own_part(own_ref, v, below, lt_ref, rc_ref, dlt_ref, drc_ref):
    n = own_ref.shape[1]
    hop = sandwich(rc_ref, lt_ref, below.T)
    diag = sandwich(drc_ref, dlt_ref, v.T)
    return where(square_mask(own_ref[n : n + 1, :]), (hop + diag).T)


def first_apply(own_ref, below_ref, lt_ref, rc_ref, dlt_ref, drc_ref, a_ref):
    n = own_ref.shape[1]
    v = own_ref[:n, :]
    a_ref[...] = SHIFT * v - own_part(own_ref, v, below_ref[:n, :], lt_ref, rc_ref, dlt_ref, drc_ref)


def later_apply(last, own_ref, below_ref, v_ref, got_a_ref, b_ref, lt_ref, rc_ref, dlt_ref, drc_ref, a_ref):
    n = own_ref.shape[1]
    below = where(square_mask(below_ref[n : n + 1, :]), got_a_ref[...] - b_ref[...])
    v = v_ref[...]
    part = own_part(own_ref, v, below, lt_ref, rc_ref, dlt_ref, drc_ref)
    a_ref[...] = part if last else SHIFT * v - part


def total_of(x):
    return jnp.sum(jnp.sum(x, axis=0, keepdims=True), axis=1, keepdims=True)


def finish(rank_ref, own_ref, v_ref, part_ref, got_b_ref, v4_ref, kept_ref):
    n = own_ref.shape[1]
    size = own_ref[n : n + 1, :]
    v = v_ref[...]
    applied = part_ref[...] + where(square_mask(size), got_b_ref[...])
    v4 = SHIFT * v - applied
    v4_ref[...] = v4
    square = total_of(v4 * v4)
    top = total_of(v * applied)
    low = total_of(v * v)
    safe = jnp.maximum(square, 1e-37)
    kept_cols = jnp.minimum(jnp.full((1, n), rank_ref[0, 0].astype(f32), f32), size)
    cols = lax.broadcasted_iota(jnp.int32, (n, n), 1).astype(f32)
    kept = where(cols < jnp.broadcast_to(kept_cols, (n, n)), v4)
    kept_ref[:n, :] = kept * lax.rsqrt(safe)
    lane = lax.broadcasted_iota(jnp.int32, (8, n), 1)
    row = jnp.where(lane == 0, square, 0.0)
    row = jnp.where(lane == 1, top, row)
    row = jnp.where(lane == 2, low, row)
    row = jnp.where(lane == 3, safe, row)
    row = jnp.where(lane == 4, 1.0, row)
    kept_ref[n:, :] = row


def sums_message(own_ref, left_ref, right_ref, out_ref):
    n = own_ref.shape[1]
    lane = lax.broadcasted_iota(jnp.int32, (1, n), 1)

    def pick(ref, j):
        return jnp.sum(jnp.where(lane == j, ref[n : n + 1, :], 0.0), axis=1, keepdims=True)

    row = jnp.where(lane < 3, own_ref[n : n + 1, :], 0.0)
    row = jnp.where(lane == 3, pick(left_ref, 0), row)
    row = jnp.where(lane == 4, pick(right_ref, 0), row)
    out_ref[...] = jnp.broadcast_to(row, out_ref.shape)


def extend(left_ref, right_ref, dl_ref, hl_ref, dr_ref, hr_ref, el_ref, er_ref):
    n = left_ref.shape[1]
    kept = left_ref[:n, :]
    w = weight(kept)
    flip = kept.T
    high, low = split(flip)
    lhs = jnp.concatenate([high, low], 0)
    for c in range(el_ref.shape[0]):
        x = dl_ref[c] if c < dl_ref.shape[0] else hl_ref[c - dl_ref.shape[0]]
        xh, xl = split(x)
        half = folded(dot(jnp.concatenate([xh, xl], 1), w))
        th, tl = split(half)
        out = folded(dot(lhs, jnp.concatenate([th, tl], 1)))
        el_ref[c] = out[:n] + out[n:]
    kept = right_ref[:n, :]
    w = weight(kept.T)
    high, low = split(kept)
    lhs = jnp.concatenate([high, low], 0)
    for c in range(er_ref.shape[0]):
        y = dr_ref[c] if c < dr_ref.shape[0] else hr_ref[c - dr_ref.shape[0]]
        yh, yl = split(y.T)
        half = folded(dot(jnp.concatenate([yh, yl], 1), w))
        th, tl = split(half)
        out = folded(dot(lhs, jnp.concatenate([th, tl], 1)))
        er_ref[c] = out[:n] + out[n:]


def scaled(sums_ref, left_ref, right_ref, v4_ref, el_ref, er_ref, state_ref, lo_ref, ro_ref, energy_ref, state, lo, ro, sems):
    n = v4_ref.shape[1]
    channels = el_ref.shape[0]
    sums = jnp.sum(sums_ref[...], axis=0, keepdims=True)
    lane = lax.broadcasted_iota(jnp.int32, (1, n), 1)

    def pick(row, j):
        return jnp.sum(jnp.where(lane == j, row, 0.0), axis=1, keepdims=True)

    state[...] = v4_ref[...] * jnp.sqrt(BOND * n / pick(sums, 0))
    copies = [pltpu.make_async_copy(state, state_ref, sems.at[0])]
    copies[0].start()
    left_row, right_row = left_ref[n : n + 1, :], right_ref[n : n + 1, :]
    root = BOND * n / math.sqrt(n)
    left_scale = jnp.where(pick(left_row, 4) > 0.0, root * (pick(left_row, 3) / pick(sums, 3)), 0.0)
    right_scale = jnp.where(pick(right_row, 4) > 0.0, root * (pick(right_row, 3) / pick(sums, 4)), 0.0)
    step = 6
    for i in range(channels // step):
        at = pl.ds(i * step, step)
        lo[at] = el_ref[at] * left_scale
        copies.append(pltpu.make_async_copy(lo.at[at], lo_ref.at[at], sems.at[1 + 2 * i]))
        copies[-1].start()
        ro[at] = er_ref[at] * right_scale
        copies.append(pltpu.make_async_copy(ro.at[at], ro_ref.at[at], sems.at[2 + 2 * i]))
        copies[-1].start()
    energy_ref[0] = jnp.sum(pick(sums, 1) / pick(sums, 2))
    for copy in copies:
        copy.wait()


def call(kernel, args, specs, outs, out_specs=None, scratch=(), flops=0, name=None):
    moved = sum(math.prod(a.shape) * a.dtype.itemsize for a in (*args, *outs))
    return pl.pallas_call(
        kernel,
        in_specs=specs,
        out_specs=out_specs or [VMEM] * len(outs),
        out_shape=outs,
        scratch_shapes=list(scratch),
        compiler_params=pltpu.CompilerParams(vmem_limit_bytes=16 << 20),
        cost_estimate=pl.CostEstimate(flops=flops, bytes_accessed=moved, transcendentals=0),
        name=name,
    )(*args)


def shards(two_site, diag_left, diag_right, hop_left, hop_right, sector_sizes, ranks):
    n = two_site.shape[2]
    x0 = two_site[0, 0]
    dl, dr, hl, hr = diag_left[0, 0], diag_right[0, 0], hop_left[0, 0], hop_right[0, 0]
    hops, diags = hl.shape[0], dl.shape[0]
    blocks, segs = lax.axis_size("blk"), lax.axis_size("seg")
    up = [(i, i + 1) for i in range(blocks - 1)]
    down = [(i + 1, i) for i in range(blocks - 1)]
    seg_up = [(i, i + 1) for i in range(segs - 1)]
    seg_down = [(i + 1, i) for i in range(segs - 1)]
    block = SDS((n, n), f32)
    message = SDS((n + 8, n), f32)
    hop_parts = SDS((hops * n, 2 * n), bf16)
    diag_parts = SDS((diags * n, 2 * n), bf16)
    channel = 8 * 2 * n**3

    (own,) = call(first_message, (sector_sizes, x0), [SMEM, VMEM], [message], name="first_message")
    below0 = lax.ppermute(own, "blk", up)
    lt, rc, dlt, drc, b = call(
        first_adjoint,
        (own, hl, hr, dl, dr),
        [VMEM] * 5,
        [hop_parts, hop_parts, diag_parts, diag_parts, block],
        flops=channel * hops,
        name="first_adjoint",
    )
    got_b = lax.ppermute(b, "blk", down)
    dl_in, hl_in = lax.ppermute(dl, "seg", seg_up), lax.ppermute(hl, "seg", seg_up)
    dr_in, hr_in = lax.ppermute(dr, "seg", seg_down), lax.ppermute(hr, "seg", seg_down)
    ops = (lt, rc, dlt, drc)
    (a,) = call(first_apply, (own, below0, *ops), [VMEM] * 6, [block], flops=channel * (hops + diags), name="apply0")
    for k in range(1, ITERS):
        got_a = lax.ppermute(a, "blk", up)
        last_b = b
        v, b = call(
            adjoint, (own, a, got_b, lt, rc), [VMEM] * 5, [block, block], flops=channel * hops, name=f"adjoint{k}"
        )
        got_b = lax.ppermute(b, "blk", down)
        (a,) = call(
            functools.partial(later_apply, k == ITERS - 1),
            (own, below0, v, got_a, last_b, *ops),
            [VMEM] * 9,
            [block],
            flops=channel * (hops + diags),
            name=f"apply{k}",
        )
    v4, kept = call(finish, (ranks, own, v, a, got_b), [SMEM] + [VMEM] * 4, [block, message], name="finish")
    from_left = lax.ppermute(kept, "seg", seg_up)
    from_right = lax.ppermute(kept, "seg", seg_down)
    (sums,) = call(sums_message, (kept, from_left, from_right), [VMEM] * 3, [SDS((blocks, n), f32)], name="sums_message")
    sums = lax.all_to_all(sums, "blk", 0, 0, tiled=True)
    out = SDS((hops + diags, n, n), f32)
    el, er = call(
        extend,
        (from_left, from_right, dl_in, hl_in, dr_in, hr_in),
        [VMEM] * 6,
        [out, out],
        flops=2 * channel * (hops + diags),
        name="extend",
    )
    state, left, right, energy = call(
        scaled,
        (sums, from_left, from_right, v4, el, er),
        [VMEM] * 6,
        [block, out, out, SDS((1,), f32)],
        out_specs=[HBM, HBM, HBM, SMEM],
        scratch=[
            pltpu.VMEM((n, n), f32),
            pltpu.VMEM(out.shape, f32),
            pltpu.VMEM(out.shape, f32),
            pltpu.SemaphoreType.DMA((7,)),
        ],
        name="scaled",
    )
    return state[None, None], left[None, None], right[None, None], energy


def solution(mesh):
    wide = P("seg", "blk", None, None, None)
    return jax.shard_map(
        shards,
        mesh=mesh,
        in_specs=(P("seg", "blk", None, None), wide, wide, wide, wide, P("seg", "blk"), P("seg", "blk")),
        out_specs=(P("seg", "blk", None, None), wide, wide, P("seg")),
        check_vma=False,
    )
```

time: 250 us -> 101 us (0.40)
  blocking collectives: 128 us -> 0 us
  matrix products: 27.7 us -> 0 us
  Pallas kernels: 0 us -> 15.4 us
  waiting for transfers between devices: 16.8 us -> 7.7 us
  local copies, waits for them, and re-layouts: 5.34 us -> 9.48 us
  between operations: 6.41 us -> 2.27 us
  starting transfers between devices: 62.1 us -> 65 us
  other arithmetic: 2.86 us -> 0 us
    psum x1 -> x0, blocking collectives: 128 us -> none  [shards(): lax.psum((jnp.sum(last_vector * last_applied), jnp.sum(last_vector * last...]
    dot_general x32 -> x0, matrix products: 27.7 us -> none  [the longest x4 7.22 us: channel_adjoint(): halfway = jnp.einsum('qwji,qjk->qwik', left_ops, vector, precision=highest)]
    all_to_all x0 -> x1, starting transfers between devices: none -> 24.3 us  [shards(): sums = lax.all_to_all(sums, 'blk', 0, 0, tiled=True)]
    ppermute x10 -> x14, starting transfers between devices: 62.1 us -> 40.7 us  [the longest x3 12 us: shards(): got_a = lax.ppermute(a, 'blk', up)]
    pallas_call x0 -> x13, Pallas kernels: none -> 15.4 us  [call(): pl.pallas_call(kernel, in_specs=specs, out_specs=out_specs or [VMEM] * le...]
    ppermute x10 -> x14, waiting for transfers between devices: 16.8 us -> 5.86 us  [the longest x1 3.7 us: shards(): from_right = lax.ppermute(kept, 'seg', seg_down)]
    unnamed x12 -> x22, local copies, waits for them, and re-layouts: 5.34 us -> 9.48 us
  transfers between devices with their start and end apart: 10 -> 15, of which waited for: 6 -> 3; matrix products, arithmetic and copies ran while one was open for 5% -> 0% of each run, Pallas kernels for 0% -> 13%
where the time goes in v1:
time: 101 us; the launch traced here: 99.9 us
  starting transfers between devices  65 us (64%)
  Pallas kernels  15.4 us (15%)
  local copies, waits for them, and re-layouts  9.48 us (9%)
  waiting for transfers between devices  7.7 us (8%)
  between operations  2.27 us (2%)
    all_to_all x1, starting transfers between devices, shards(): sums = lax.all_to_all(sums, 'blk', 0, 0, tiled=True)  24.3 us
    pallas_call x13, Pallas kernels, call(): pl.pallas_call(kernel, in_specs=specs, out_specs=out_specs or [VMEM] * le...  15.4 us
    ppermute x3, starting transfers between devices, shards(): got_a = lax.ppermute(a, 'blk', up)  12 us
    unnamed x22, local copies, waits for them, and re-layouts  9.48 us
    ppermute x1, starting transfers between devices, shards(): from_left = lax.ppermute(kept, 'seg', seg_up)  5.91 us
    ppermute x1, starting transfers between devices, shards(): lax.ppermute(hr, 'seg', seg_down)  5.64 us
    ppermute x4, starting transfers between devices, shards(): got_b = lax.ppermute(b, 'blk', down)  5.17 us
    ppermute x1, starting transfers between devices, shards(): lax.ppermute(hl, 'seg', seg_up)  4.51 us
  transfers between devices with their start and end apart: 15, of which 3 were waited for; matrix products, arithmetic and copies ran while one was open for 0% of the time, Pallas kernels for 13%

profile of v1, /device:TPU:1, one launch (start us, length us, event | category | flops | bytes accessed | tf_op | source)
XLA Modules:
  0.0 99.9 jit_solution(442682527833059275)
XLA Ops:
  0.6 4.5 %collective-permute-start.11 = (f32[16,128,128]{2,1,0:T(8,128)}, f32[16,128,128]{2,1,0:T(8,128)S(1)}, u32[]{:S(2)}, u32[]{:S(2)}) collective-permute-start(f32[16,128,128]{2,1,0:T(8,128)} %bitcast.12), channel_id=1, source_target_pairs={{0,64},{64,128},{128,192},{192,256},{256,320},{320,384},{384,448},... | collective-permute-start | bytes 3145736 | tf_op jit(solution)/shard_map/ppermute | solution.py:266
  5.1 5.6 %collective-permute-start.13 = (f32[16,128,128]{2,1,0:T(8,128)}, f32[16,128,128]{2,1,0:T(8,128)S(1)}, u32[]{:S(2)}, u32[]{:S(2)}) collective-permute-start(f32[16,128,128]{2,1,0:T(8,128)} %bitcast.14), channel_id=1, source_target_pairs={{64,0},{128,64},{192,128},{256,192},{320,256},{384,320},{448,384},... | collective-permute-start | bytes 3145736 | tf_op jit(solution)/shard_map/ppermute | solution.py:267
  11.4 0.8 copy-done.6
  12.3 1.3 %collective-permute-start = (f32[136,128]{1,0:T(8,128)S(1)}, f32[136,128]{1,0:T(8,128)S(1)}, u32[]{:S(2)}, u32[]{:S(2)}) collective-permute-start(f32[136,128]{1,0:T(8,128)S(1)} %first_message.1.own_ref), channel_id=1, source_target_pairs={{0,1},{1,2},{2,3},{3,4},{4,5},{5,6},{6,7},{7,8},{8,9},{9,10},{10,1... | collective-permute-start | bytes 208904 | tf_op jit(solution)/shard_map/ppermute | solution.py:256
  13.6 0.0 copy-start
  13.6 1.2 %copy-done = f32[1,1,16,128,128]{4,3,2,1,0:T(8,128)S(1)} copy-done((f32[1,1,16,128,128]{4,3,2,1,0:T(8,128)S(1)}, f32[1,1,16,128,128]{4,3,2,1,0:T(8,128)}, u32[]{:S(2)}) %copy-start) | copy-done | bytes 1048600
  14.8 1.2 %copy-done.1 = f32[1,1,16,128,128]{4,3,2,1,0:T(8,128)S(1)} copy-done((f32[1,1,16,128,128]{4,3,2,1,0:T(8,128)S(1)}, f32[1,1,16,128,128]{4,3,2,1,0:T(8,128)}, u32[]{:S(2)}) %copy-start.1) | copy-done | bytes 1048600
  16.1 0.9 copy-done.2
  17.0 0.9 copy-done.4
  17.9 1.0 %first_adjoint.1 = (bf16[2048,256]{1,0:T(8,128)(2,1)S(1)}, bf16[2048,256]{1,0:T(8,128)(2,1)S(1)}, bf16[256,256]{1,0:T(8,128)(2,1)S(1)}, bf16[256,256]{1,0:T(8,128)(2,1)S(1)}, f32[128,128]{1,0:T(8,128)S(1)}) custom-call(f32[136,128]{1,0:T(8,128)S(1)} %first_message.1.own_ref, f32[16,128,128]{2,1,0:T(8,128)S(1)} %bitcast.13, f32[16,128,128]{2,1,0:T(8,128)S(1)} %bitcast.15, ...), custom_call_target="tpu_custom_call" | custom-call | flops 536870912 | bytes 4853760 | tf_op jit(solution)/shard_map/first_adjoint/pallas_call | solution.py:227
  18.9 1.3 %collective-permute-start.1 = (f32[128,128]{1,0:T(8,128)S(1)}, f32[128,128]{1,0:T(8,128)S(1)}, u32[]{:S(2)}, u32[]{:S(2)}) collective-permute-start(f32[128,128]{1,0:T(8,128)S(1)} %get-tuple-element.27.b_ref), channel_id=1, source_target_pairs={{1,0},{2,1},{3,2},{4,3},{5,4},{6,5},{7,6},{8,7},{9,8},{10,9},{11,1... | collective-permute-start | bytes 196616 | tf_op jit(solution)/shard_map/ppermute | solution.py:265
  20.2 0.0 collective-permute-done.below_ref
  20.2 1.0 %apply0.1.a_ref = f32[128,128]{1,0:T(8,128)S(1)} custom-call(f32[136,128]{1,0:T(8,128)S(1)} %first_message.1.own_ref, f32[136,128]{1,0:T(8,128)S(1)} %collective-permute-done.below_ref, bf16[2048,256]{1,0:T(8,128)(2,1)S(1)} %get-tuple-element.23.lt_ref, bf16[2048,256]{1,0:T(8,128)(2,1)S(1)} %get-tuple-element.24.rc_ref, ...), custom_call_target="tpu_custom_call" | custom-call | flops 603979776 | bytes 2564096 | tf_op jit(solution)/shard_map/apply0/pallas_call | solution.py:227
  21.2 4.0 %collective-permute-start.2 = (f32[128,128]{1,0:T(8,128)S(1)}, f32[128,128]{1,0:T(8,128)S(1)}, u32[]{:S(2)}, u32[]{:S(2)}) collective-permute-start(f32[128,128]{1,0:T(8,128)S(1)} %apply0.1.a_ref), channel_id=1, source_target_pairs={{0,1},{1,2},{2,3},{3,4},{4,5},{5,6},{6,7},{7,8},{8,9},{9,10},{10,1... | collective-permute-start | bytes 196616 | tf_op jit(solution)/shard_map/ppermute | solution.py:271
  25.2 0.0 collective-permute-done.1.got_b_ref
  25.2 0.9 adjoint1.1
  26.2 1.3 %collective-permute-start.3 = (f32[128,128]{1,0:T(8,128)S(1)}, f32[128,128]{1,0:T(8,128)S(1)}, u32[]{:S(2)}, u32[]{:S(2)}) collective-permute-start(f32[128,128]{1,0:T(8,128)S(1)} %get-tuple-element.29.b_ref), channel_id=1, source_target_pairs={{1,0},{2,1},{3,2},{4,3},{5,4},{6,5},{7,6},{8,7},{9,8},{10,9},{11,1... | collective-permute-start | bytes 196616 | tf_op jit(solution)/shard_map/ppermute | solution.py:276
  27.5 1.1 %apply1.1.a_ref = f32[128,128]{1,0:T(8,128)S(1)} custom-call(f32[136,128]{1,0:T(8,128)S(1)} %first_message.1.own_ref, f32[136,128]{1,0:T(8,128)S(1)} %collective-permute-done.below_ref, f32[128,128]{1,0:T(8,128)S(1)} %get-tuple-element.28.v_ref, f32[128,128]{1,0:T(8,128)S(1)} %collective-permute-done.2.got_a_ref, f32[128,128]{1,0:T(8,128)S(1)} %get-tuple-element.27.b_ref, ...), custom_call_target="tpu_custom_call" | custom-call | flops 603979776 | bytes 2760704 | tf_op jit(solution)/shard_map/apply1/pallas_call | solution.py:227
  28.6 4.0 %collective-permute-start.4 = (f32[128,128]{1,0:T(8,128)S(1)}, f32[128,128]{1,0:T(8,128)S(1)}, u32[]{:S(2)}, u32[]{:S(2)}) collective-permute-start(f32[128,128]{1,0:T(8,128)S(1)} %apply1.1.a_ref), channel_id=1, source_target_pairs={{0,1},{1,2},{2,3},{3,4},{4,5},{5,6},{6,7},{7,8},{8,9},{9,10},{10,1... | collective-permute-start | bytes 196616 | tf_op jit(solution)/shard_map/ppermute | solution.py:271
  32.6 0.0 collective-permute-done.3.got_b_ref
  32.6 0.9 adjoint2.1
  33.5 1.3 %collective-permute-start.5 = (f32[128,128]{1,0:T(8,128)S(1)}, f32[128,128]{1,0:T(8,128)S(1)}, u32[]{:S(2)}, u32[]{:S(2)}) collective-permute-start(f32[128,128]{1,0:T(8,128)S(1)} %get-tuple-element.31.b_ref), channel_id=1, source_target_pairs={{1,0},{2,1},{3,2},{4,3},{5,4},{6,5},{7,6},{8,7},{9,8},{10,9},{11,1... | collective-permute-start | bytes 196616 | tf_op jit(solution)/shard_map/ppermute | solution.py:276
  34.8 1.0 %apply2.1.a_ref = f32[128,128]{1,0:T(8,128)S(1)} custom-call(f32[136,128]{1,0:T(8,128)S(1)} %first_message.1.own_ref, f32[136,128]{1,0:T(8,128)S(1)} %collective-permute-done.below_ref, f32[128,128]{1,0:T(8,128)S(1)} %get-tuple-element.30.v_ref, f32[128,128]{1,0:T(8,128)S(1)} %collective-permute-done.4.got_a_ref, f32[128,128]{1,0:T(8,128)S(1)} %get-tuple-element.29.b_ref, ...), custom_call_target="tpu_custom_call" | custom-call | flops 603979776 | bytes 2760704 | tf_op jit(solution)/shard_map/apply2/pallas_call | solution.py:227
  35.9 4.0 %collective-permute-start.6 = (f32[128,128]{1,0:T(8,128)S(1)}, f32[128,128]{1,0:T(8,128)S(1)}, u32[]{:S(2)}, u32[]{:S(2)}) collective-permute-start(f32[128,128]{1,0:T(8,128)S(1)} %apply2.1.a_ref), channel_id=1, source_target_pairs={{0,1},{1,2},{2,3},{3,4},{4,5},{5,6},{6,7},{7,8},{8,9},{9,10},{10,1... | collective-permute-start | bytes 196616 | tf_op jit(solution)/shard_map/ppermute | solution.py:271
  39.9 0.0 collective-permute-done.5.got_b_ref
  39.9 0.9 adjoint3.1
  40.8 1.3 %collective-permute-start.7 = (f32[128,128]{1,0:T(8,128)S(1)}, f32[128,128]{1,0:T(8,128)S(1)}, u32[]{:S(2)}, u32[]{:S(2)}) collective-permute-start(f32[128,128]{1,0:T(8,128)S(1)} %get-tuple-element.33), channel_id=1, source_target_pairs={{1,0},{2,1},{3,2},{4,3},{5,4},{6,5},{7,6},{8,7},{9,8},{10,9},{11,1... | collective-permute-start | bytes 196616 | tf_op jit(solution)/shard_map/ppermute | solution.py:276
  42.8 0.0 collective-permute-done.6.got_a_ref
  42.8 0.0 copy-start.3
  42.8 0.0 copy-start.5
  42.8 1.0 %apply3.1.part_ref = f32[128,128]{1,0:T(8,128)S(1)} custom-call(f32[136,128]{1,0:T(8,128)S(1)} %first_message.1.own_ref, f32[136,128]{1,0:T(8,128)S(1)} %collective-permute-done.below_ref, f32[128,128]{1,0:T(8,128)S(1)} %get-tuple-element.32.v_ref, f32[128,128]{1,0:T(8,128)S(1)} %collective-permute-done.6.got_a_ref, f32[128,128]{1,0:T(8,128)S(1)} %get-tuple-element.31.b_ref, ...), custom_call_target="tpu_custom_call" | custom-call | flops 603979776 | bytes 2760704 | tf_op jit(solution)/shard_map/apply3/pallas_call | solution.py:227
  43.9 2.1 %collective-permute-done.7.got_b_ref = f32[128,128]{1,0:T(8,128)S(1)} collective-permute-done((f32[128,128]{1,0:T(8,128)S(1)}, f32[128,128]{1,0:T(8,128)S(1)}, u32[]{:S(2)}, u32[]{:S(2)}) %collective-permute-start.7) | collective-permute-done | bytes 65568 | tf_op jit(solution)/shard_map/ppermute | solution.py:276
  46.0 0.1 finish.1
  46.1 5.9 %collective-permute-start.8 = (f32[136,128]{1,0:T(8,128)S(1)}, f32[136,128]{1,0:T(8,128)S(1)}, u32[]{:S(2)}, u32[]{:S(2)}) collective-permute-start(f32[136,128]{1,0:T(8,128)S(1)} %get-tuple-element.34.own_ref), channel_id=1, source_target_pairs={{0,64},{64,128},{128,192},{192,256},{256,320},{320,384},{384,448},... | collective-permute-start | bytes 208904 | tf_op jit(solution)/shard_map/ppermute | solution.py:286
  52.1 1.9 %collective-permute-start.10 = (f32[2,128,128]{2,1,0:T(8,128)S(1)}, f32[2,128,128]{2,1,0:T(8,128)S(1)}, u32[]{:S(2)}, u32[]{:S(2)}) collective-permute-start(f32[2,128,128]{2,1,0:T(8,128)S(1)} %bitcast.18), channel_id=1, source_target_pairs={{0,64},{64,128},{128,192},{192,256},{256,320},{320,384},{384,448},... | collective-permute-start | bytes 393224 | tf_op jit(solution)/shard_map/ppermute | solution.py:266
  54.0 2.4 %collective-permute-start.12 = (f32[2,128,128]{2,1,0:T(8,128)S(1)}, f32[2,128,128]{2,1,0:T(8,128)S(1)}, u32[]{:S(2)}, u32[]{:S(2)}) collective-permute-start(f32[2,128,128]{2,1,0:T(8,128)S(1)} %bitcast.20), channel_id=1, source_target_pairs={{64,0},{128,64},{192,128},{256,192},{320,256},{384,320},{448,384},... | collective-permute-start | bytes 393224 | tf_op jit(solution)/shard_map/ppermute | solution.py:267
  56.4 1.9 %collective-permute-start.9 = (f32[136,128]{1,0:T(8,128)S(1)}, f32[136,128]{1,0:T(8,128)S(1)}, u32[]{:S(2)}, u32[]{:S(2)}) collective-permute-start(f32[136,128]{1,0:T(8,128)S(1)} %get-tuple-element.34.own_ref), channel_id=1, source_target_pairs={{64,0},{128,64},{192,128},{256,192},{320,256},{384,320},{448,384},... | collective-permute-start | bytes 208904 | tf_op jit(solution)/shard_map/ppermute | solution.py:287
  58.3 3.7 %collective-permute-done.9.right_ref = f32[136,128]{1,0:T(8,128)S(1)} collective-permute-done((f32[136,128]{1,0:T(8,128)S(1)}, f32[136,128]{1,0:T(8,128)S(1)}, u32[]{:S(2)}, u32[]{:S(2)}) %collective-permute-start.9) | collective-permute-done | bytes 69664 | tf_op jit(solution)/shard_map/ppermute | solution.py:287
  62.0 0.7 sums_message.1
  62.7 24.3 %all-to-all-start = ((f32[64,1,128]{2,1,0:T(1,128)}), f32[64,1,128]{2,1,0:T(1,128)S(1)}, u32[]{:S(2)}, u32[]{:S(2)}) async-start(f32[64,1,128]{2,1,0:T(1,128)} %bitcast.6), calls=%async_computation | async-start | bytes 65536 | tf_op jit(solution)/shard_map/all_to_all | solution.py:289
  87.1 0.0 copy-start.7
  87.1 1.0 copy-done.7
  88.0 1.0 copy-done.9
  89.0 1.2 %copy-done.8 = f32[16,128,128]{2,1,0:T(8,128)S(1)} copy-done((f32[16,128,128]{2,1,0:T(8,128)S(1)}, f32[16,128,128]{2,1,0:T(8,128)}, u32[]{:S(2)}) %copy-start.8) | copy-done | bytes 1048600
  90.2 1.2 %copy-done.10 = f32[16,128,128]{2,1,0:T(8,128)S(1)} copy-done((f32[16,128,128]{2,1,0:T(8,128)S(1)}, f32[16,128,128]{2,1,0:T(8,128)}, u32[]{:S(2)}) %copy-start.10) | copy-done | bytes 1048600
  91.5 4.5 %extend.1 = (f32[18,128,128]{2,1,0:T(8,128)S(1)}, f32[18,128,128]{2,1,0:T(8,128)S(1)}) custom-call(f32[136,128]{1,0:T(8,128)S(1)} %collective-permute-done.8.left_ref, f32[136,128]{1,0:T(8,128)S(1)} %collective-permute-done.9.right_ref, f32[2,128,128]{2,1,0:T(8,128)S(1)} %collective-permute-done.10.dl_ref, f32[16,128,128]{2,1,0:T(8,128)S(1)} %copy-done.8, ...), custom_call_target="tpu_custom_call" | custom-call | flops 1207959552 | bytes 4857856 | tf_op jit(solution)/shard_map/extend/pallas_call | solution.py:227
  96.0 1.8 %all-to-all-done = f32[64,1,128]{2,1,0:T(1,128)S(1)} async-done(((f32[64,1,128]{2,1,0:T(1,128)}), f32[64,1,128]{2,1,0:T(1,128)S(1)}, u32[]{:S(2)}, u32[]{:S(2)}) %all-to-all-start) | async-done | bytes 32800 | tf_op jit(solution)/shard_map/all_to_all | solution.py:289
  97.8 2.1 %scaled.1 = (f32[128,128]{1,0:T(8,128)}, f32[18,128,128]{2,1,0:T(8,128)}, f32[18,128,128]{2,1,0:T(8,128)}, f32[1]{0:T(128)}) custom-call(f32[64,128]{1,0:T(8,128)S(1)} %bitcast.16, f32[136,128]{1,0:T(8,128)S(1)} %collective-permute-done.8.left_ref, f32[136,128]{1,0:T(8,128)S(1)} %collective-permute-done.9.right_ref, ...), custom_call_target="tpu_custom_call" | custom-call | bytes 5021700 | tf_op jit(solution)/shard_map/scaled/pallas_call | solution.py:227
  (17 shorter events, 0.0 us)
Async XLA Ops:
  0.6 86.4 %collective-permute-start.11 = (f32[16,128,128]{2,1,0:T(8,128)}, f32[16,128,128]{2,1,0:T(8,128)S(1)}, u32[]{:S(2)}, u32[]{:S(2)}) collective-permute-start(f32[16,128,128]{2,1,0:T(8,128)} %bitcast.12), channel_id=1, source_target_pairs={{0,64},{64,128},{128,192},{192,256},{256,320},{320,384},{384,448},... | collective-permute-start | bytes 3145736 | tf_op jit(solution)/shard_map/ppermute | solution.py:266
  5.1 82.9 %collective-permute-start.13 = (f32[16,128,128]{2,1,0:T(8,128)}, f32[16,128,128]{2,1,0:T(8,128)S(1)}, u32[]{:S(2)}, u32[]{:S(2)}) collective-permute-start(f32[16,128,128]{2,1,0:T(8,128)} %bitcast.14), channel_id=1, source_target_pairs={{64,0},{128,64},{192,128},{256,192},{320,256},{384,320},{448,384},... | collective-permute-start | bytes 3145736 | tf_op jit(solution)/shard_map/ppermute | solution.py:267
  11.4 0.8 copy-start.6
  12.3 7.9 %collective-permute-start = (f32[136,128]{1,0:T(8,128)S(1)}, f32[136,128]{1,0:T(8,128)S(1)}, u32[]{:S(2)}, u32[]{:S(2)}) collective-permute-start(f32[136,128]{1,0:T(8,128)S(1)} %first_message.1.own_ref), channel_id=1, source_target_pairs={{0,1},{1,2},{2,3},{3,4},{4,5},{5,6},{6,7},{7,8},{8,9},{9,10},{10,1... | collective-permute-start | bytes 208904 | tf_op jit(solution)/shard_map/ppermute | solution.py:256
  13.6 1.2 %copy-start = (f32[1,1,16,128,128]{4,3,2,1,0:T(8,128)S(1)}, f32[1,1,16,128,128]{4,3,2,1,0:T(8,128)}, u32[]{:S(2)}) copy-start(f32[1,1,16,128,128]{4,3,2,1,0:T(8,128)} %param.10) | copy-start | bytes 3145732
  14.8 1.2 %copy-start.1 = (f32[1,1,16,128,128]{4,3,2,1,0:T(8,128)S(1)}, f32[1,1,16,128,128]{4,3,2,1,0:T(8,128)}, u32[]{:S(2)}) copy-start(f32[1,1,16,128,128]{4,3,2,1,0:T(8,128)} %param.11) | copy-start | bytes 3145732
  16.1 0.9 copy-start.2
  17.0 0.9 copy-start.4
  18.9 6.4 %collective-permute-start.1 = (f32[128,128]{1,0:T(8,128)S(1)}, f32[128,128]{1,0:T(8,128)S(1)}, u32[]{:S(2)}, u32[]{:S(2)}) collective-permute-start(f32[128,128]{1,0:T(8,128)S(1)} %get-tuple-element.27.b_ref), channel_id=1, source_target_pairs={{1,0},{2,1},{3,2},{4,3},{5,4},{6,5},{7,6},{8,7},{9,8},{10,9},{11,1... | collective-permute-start | bytes 196616 | tf_op jit(solution)/shard_map/ppermute | solution.py:265
  21.2 6.3 %collective-permute-start.2 = (f32[128,128]{1,0:T(8,128)S(1)}, f32[128,128]{1,0:T(8,128)S(1)}, u32[]{:S(2)}, u32[]{:S(2)}) collective-permute-start(f32[128,128]{1,0:T(8,128)S(1)} %apply0.1.a_ref), channel_id=1, source_target_pairs={{0,1},{1,2},{2,3},{3,4},{4,5},{5,6},{6,7},{7,8},{8,9},{9,10},{10,1... | collective-permute-start | bytes 196616 | tf_op jit(solution)/shard_map/ppermute | solution.py:271
  26.2 6.4 %collective-permute-start.3 = (f32[128,128]{1,0:T(8,128)S(1)}, f32[128,128]{1,0:T(8,128)S(1)}, u32[]{:S(2)}, u32[]{:S(2)}) collective-permute-start(f32[128,128]{1,0:T(8,128)S(1)} %get-tuple-element.29.b_ref), channel_id=1, source_target_pairs={{1,0},{2,1},{3,2},{4,3},{5,4},{6,5},{7,6},{8,7},{9,8},{10,9},{11,1... | collective-permute-start | bytes 196616 | tf_op jit(solution)/shard_map/ppermute | solution.py:276
  28.6 6.3 %collective-permute-start.4 = (f32[128,128]{1,0:T(8,128)S(1)}, f32[128,128]{1,0:T(8,128)S(1)}, u32[]{:S(2)}, u32[]{:S(2)}) collective-permute-start(f32[128,128]{1,0:T(8,128)S(1)} %apply1.1.a_ref), channel_id=1, source_target_pairs={{0,1},{1,2},{2,3},{3,4},{4,5},{5,6},{6,7},{7,8},{8,9},{9,10},{10,1... | collective-permute-start | bytes 196616 | tf_op jit(solution)/shard_map/ppermute | solution.py:271
  33.5 6.4 %collective-permute-start.5 = (f32[128,128]{1,0:T(8,128)S(1)}, f32[128,128]{1,0:T(8,128)S(1)}, u32[]{:S(2)}, u32[]{:S(2)}) collective-permute-start(f32[128,128]{1,0:T(8,128)S(1)} %get-tuple-element.31.b_ref), channel_id=1, source_target_pairs={{1,0},{2,1},{3,2},{4,3},{5,4},{6,5},{7,6},{8,7},{9,8},{10,9},{11,1... | collective-permute-start | bytes 196616 | tf_op jit(solution)/shard_map/ppermute | solution.py:276
  35.9 6.9 %collective-permute-start.6 = (f32[128,128]{1,0:T(8,128)S(1)}, f32[128,128]{1,0:T(8,128)S(1)}, u32[]{:S(2)}, u32[]{:S(2)}) collective-permute-start(f32[128,128]{1,0:T(8,128)S(1)} %apply2.1.a_ref), channel_id=1, source_target_pairs={{0,1},{1,2},{2,3},{3,4},{4,5},{5,6},{6,7},{7,8},{8,9},{9,10},{10,1... | collective-permute-start | bytes 196616 | tf_op jit(solution)/shard_map/ppermute | solution.py:271
  40.8 5.2 %collective-permute-start.7 = (f32[128,128]{1,0:T(8,128)S(1)}, f32[128,128]{1,0:T(8,128)S(1)}, u32[]{:S(2)}, u32[]{:S(2)}) collective-permute-start(f32[128,128]{1,0:T(8,128)S(1)} %get-tuple-element.33), channel_id=1, source_target_pairs={{1,0},{2,1},{3,2},{4,3},{5,4},{6,5},{7,6},{8,7},{9,8},{10,9},{11,1... | collective-permute-start | bytes 196616 | tf_op jit(solution)/shard_map/ppermute | solution.py:276
  42.8 9.3 %copy-start.3 = (f32[1,1,2,128,128]{4,3,2,1,0:T(8,128)S(1)}, f32[1,1,2,128,128]{4,3,2,1,0:T(8,128)}, u32[]{:S(2)}) copy-start(f32[1,1,2,128,128]{4,3,2,1,0:T(8,128)} %param.8) | copy-start | bytes 393220
  42.8 11.2 %copy-start.5 = (f32[1,1,2,128,128]{4,3,2,1,0:T(8,128)S(1)}, f32[1,1,2,128,128]{4,3,2,1,0:T(8,128)}, u32[]{:S(2)}) copy-start(f32[1,1,2,128,128]{4,3,2,1,0:T(8,128)} %param.9) | copy-start | bytes 393220
  46.1 10.3 %collective-permute-start.8 = (f32[136,128]{1,0:T(8,128)S(1)}, f32[136,128]{1,0:T(8,128)S(1)}, u32[]{:S(2)}, u32[]{:S(2)}) collective-permute-start(f32[136,128]{1,0:T(8,128)S(1)} %get-tuple-element.34.own_ref), channel_id=1, source_target_pairs={{0,64},{64,128},{128,192},{192,256},{256,320},{320,384},{384,448},... | collective-permute-start | bytes 208904 | tf_op jit(solution)/shard_map/ppermute | solution.py:286
  52.1 35.0 %collective-permute-start.10 = (f32[2,128,128]{2,1,0:T(8,128)S(1)}, f32[2,128,128]{2,1,0:T(8,128)S(1)}, u32[]{:S(2)}, u32[]{:S(2)}) collective-permute-start(f32[2,128,128]{2,1,0:T(8,128)S(1)} %bitcast.18), channel_id=1, source_target_pairs={{0,64},{64,128},{128,192},{192,256},{256,320},{320,384},{384,448},... | collective-permute-start | bytes 393224 | tf_op jit(solution)/shard_map/ppermute | solution.py:266
  54.0 33.1 %collective-permute-start.12 = (f32[2,128,128]{2,1,0:T(8,128)S(1)}, f32[2,128,128]{2,1,0:T(8,128)S(1)}, u32[]{:S(2)}, u32[]{:S(2)}) collective-permute-start(f32[2,128,128]{2,1,0:T(8,128)S(1)} %bitcast.20), channel_id=1, source_target_pairs={{64,0},{128,64},{192,128},{256,192},{320,256},{384,320},{448,384},... | collective-permute-start | bytes 393224 | tf_op jit(solution)/shard_map/ppermute | solution.py:267
  56.4 5.6 %collective-permute-start.9 = (f32[136,128]{1,0:T(8,128)S(1)}, f32[136,128]{1,0:T(8,128)S(1)}, u32[]{:S(2)}, u32[]{:S(2)}) collective-permute-start(f32[136,128]{1,0:T(8,128)S(1)} %get-tuple-element.34.own_ref), channel_id=1, source_target_pairs={{64,0},{128,64},{192,128},{256,192},{320,256},{384,320},{448,384},... | collective-permute-start | bytes 208904 | tf_op jit(solution)/shard_map/ppermute | solution.py:287
  62.7 35.1 %all-to-all-start = ((f32[64,1,128]{2,1,0:T(1,128)}), f32[64,1,128]{2,1,0:T(1,128)S(1)}, u32[]{:S(2)}, u32[]{:S(2)}) async-start(f32[64,1,128]{2,1,0:T(1,128)} %bitcast.6), calls=%async_computation | async-start | bytes 65536 | tf_op jit(solution)/shard_map/all_to_all | solution.py:289
  87.1 1.0 copy-start.7
  88.0 1.0 copy-start.9
  89.0 1.2 %copy-start.8 = (f32[16,128,128]{2,1,0:T(8,128)S(1)}, f32[16,128,128]{2,1,0:T(8,128)}, u32[]{:S(2)}) copy-start(f32[16,128,128]{2,1,0:T(8,128)} %copy-done.7) | copy-start | bytes 3145732
  90.2 1.2 %copy-start.10 = (f32[16,128,128]{2,1,0:T(8,128)S(1)}, f32[16,128,128]{2,1,0:T(8,128)}, u32[]{:S(2)}) copy-start(f32[16,128,128]{2,1,0:T(8,128)} %copy-done.9) | copy-start | bytes 3145732

commit v2 on v1

--- a/solution.py
+++ b/solution.py
@@ -11,11 +11,14 @@
 ITERS = 4
 SHIFT = 20.0
 BOND = 6144.0
+PARTS = 4
+CHUNKS = 3
 f32 = jnp.float32
 bf16 = jnp.bfloat16
 VMEM = pl.BlockSpec(memory_space=pltpu.VMEM)
 SMEM = pl.BlockSpec(memory_space=pltpu.SMEM)
-HBM = pl.BlockSpec(memory_space=pl.ANY)
+HBM = pl.BlockSpec(memory_space=pltpu.HBM)
+ANY = pl.BlockSpec(memory_space=pl.ANY)
 SDS = jax.ShapeDtypeStruct
 
 
@@ -78,21 +81,38 @@
     out_ref[pl.ds(h * n, n), n:] = low
 
 
-def first_message(size_ref, x_ref, out_ref):
-    n = x_ref.shape[0]
-    size = jnp.full((1, n), size_ref[0, 0].astype(f32), f32)
-    out_ref[:n, :] = where(square_mask(size), x_ref[...])
-    out_ref[n:, :] = jnp.broadcast_to(size, (8, n))
-
-
-def first_adjoint(own_ref, hl_ref, hr_ref, dl_ref, dr_ref, lt_ref, rc_ref, dlt_ref, drc_ref, b_ref):
-    n = own_ref.shape[1]
-    for h in range(hl_ref.shape[0]):
-        put_parts(lt_ref, h, n, hl_ref[h].T)
-        put_parts(rc_ref, h, n, hr_ref[h])
-    for h in range(dl_ref.shape[0]):
-        put_parts(dlt_ref, h, n, dl_ref[h].T)
-        put_parts(drc_ref, h, n, dr_ref[h])
+def load(size_ref, x_ref, dl_ref, hl_ref, dr_ref, hr_ref, own_ref, cl_ref, cr_ref, x, sems):
+    n = x.shape[0]
+    diags, hops = dl_ref.shape[0], hl_ref.shape[0]
+    first = pltpu.make_async_copy(x_ref, x, sems.at[0])
+    first.start()
+    rest = [
+        pltpu.make_async_copy(dl_ref, cl_ref.at[pl.ds(0, diags)], sems.at[1]),
+        pltpu.make_async_copy(dr_ref, cr_ref.at[pl.ds(0, diags)], sems.at[2]),
+    ]
+    part = hops // PARTS
+    for i in range(PARTS):
+        source, target = pl.ds(i * part, part), pl.ds(diags + i * part, part)
+        rest.append(pltpu.make_async_copy(hl_ref.at[source], cl_ref.at[target], sems.at[3 + 2 * i]))
+        rest.append(pltpu.make_async_copy(hr_ref.at[source], cr_ref.at[target], sems.at[4 + 2 * i]))
+    for copy in rest:
+        copy.start()
+    first.wait()
+    live = jnp.full((1, n), size_ref[0, 0].astype(f32), f32)
+    own_ref[:n, :] = where(square_mask(live), x[...])
+    own_ref[n:, :] = jnp.broadcast_to(live, (8, n))
+    for copy in rest:
+        copy.wait()
+
+
+def first_adjoint(own_ref, cl_ref, cr_ref, lt_ref, rc_ref, dlt_ref, drc_ref, clt_ref, b_ref):
+    n = own_ref.shape[1]
+    diags = dlt_ref.shape[0] // n
+    for c in range(cl_ref.shape[0]):
+        flip = cl_ref[c].T
+        clt_ref[c] = flip
+        put_parts(dlt_ref if c < diags else lt_ref, c if c < diags else c - diags, n, flip)
+        put_parts(drc_ref if c < diags else rc_ref, c if c < diags else c - diags, n, cr_ref[c])
     b_ref[...] = sandwich(lt_ref, rc_ref, own_ref[:n, :])
 
 
@@ -165,72 +185,71 @@
     out_ref[...] = jnp.broadcast_to(row, out_ref.shape)
 
 
-def extend(left_ref, right_ref, dl_ref, hl_ref, dr_ref, hr_ref, el_ref, er_ref):
-    n = left_ref.shape[1]
-    kept = left_ref[:n, :]
-    w = weight(kept)
-    flip = kept.T
-    high, low = split(flip)
-    lhs = jnp.concatenate([high, low], 0)
-    for c in range(el_ref.shape[0]):
-        x = dl_ref[c] if c < dl_ref.shape[0] else hl_ref[c - dl_ref.shape[0]]
-        xh, xl = split(x)
-        half = folded(dot(jnp.concatenate([xh, xl], 1), w))
-        th, tl = split(half)
-        out = folded(dot(lhs, jnp.concatenate([th, tl], 1)))
-        el_ref[c] = out[:n] + out[n:]
-    kept = right_ref[:n, :]
-    w = weight(kept.T)
-    high, low = split(kept)
-    lhs = jnp.concatenate([high, low], 0)
-    for c in range(er_ref.shape[0]):
-        y = dr_ref[c] if c < dr_ref.shape[0] else hr_ref[c - dr_ref.shape[0]]
-        yh, yl = split(y.T)
-        half = folded(dot(jnp.concatenate([yh, yl], 1), w))
-        th, tl = split(half)
-        out = folded(dot(lhs, jnp.concatenate([th, tl], 1)))
-        er_ref[c] = out[:n] + out[n:]
-
-
-def scaled(sums_ref, left_ref, right_ref, v4_ref, el_ref, er_ref, state_ref, lo_ref, ro_ref, energy_ref, state, lo, ro, sems):
+def twice(x, w):
+    n = x.shape[1]
+    half = folded(dot(jnp.concatenate(split(x), 1), w))
+    flip = jnp.concatenate([half[:n].T, half[n:].T], 0)
+    return folded(dot(jnp.concatenate(split(flip), 1), w))
+
+
+def extend(
+    sums_ref, left_ref, right_ref, v4_ref, xl_ref, xr_ref, state_ref, lo_ref, ro_ref, energy_ref, sums, xl, xr, state, lo, ro, sems
+):
     n = v4_ref.shape[1]
-    channels = el_ref.shape[0]
-    sums = jnp.sum(sums_ref[...], axis=0, keepdims=True)
+    channels = xl.shape[0]
+    step = channels // CHUNKS
+    get_sums = pltpu.make_async_copy(sums_ref, sums, sems.at[0])
+    get_sums.start()
+    loads, copies = [], []
+    for i in range(CHUNKS):
+        at = pl.ds(i * step, step)
+        loads.append(pltpu.make_async_copy(xl_ref.at[at], xl.at[at], sems.at[2 + 4 * i]))
+        loads.append(pltpu.make_async_copy(xr_ref.at[at], xr.at[at], sems.at[3 + 4 * i]))
+    for copy in loads:
+        copy.start()
+    wl = weight(left_ref[:n, :])
+    wr = weight(right_ref[:n, :].T)
+    get_sums.wait()
+    total = jnp.sum(sums[...], axis=0, keepdims=True)
     lane = lax.broadcasted_iota(jnp.int32, (1, n), 1)
 
     def pick(row, j):
         return jnp.sum(jnp.where(lane == j, row, 0.0), axis=1, keepdims=True)
 
-    state[...] = v4_ref[...] * jnp.sqrt(BOND * n / pick(sums, 0))
-    copies = [pltpu.make_async_copy(state, state_ref, sems.at[0])]
+    state[...] = v4_ref[...] * jnp.sqrt(BOND * n / pick(total, 0))
+    copies.append(pltpu.make_async_copy(state, state_ref, sems.at[1]))
     copies[0].start()
+    energy_ref[0] = jnp.sum(pick(total, 1) / pick(total, 2))
     left_row, right_row = left_ref[n : n + 1, :], right_ref[n : n + 1, :]
     root = BOND * n / math.sqrt(n)
-    left_scale = jnp.where(pick(left_row, 4) > 0.0, root * (pick(left_row, 3) / pick(sums, 3)), 0.0)
-    right_scale = jnp.where(pick(right_row, 4) > 0.0, root * (pick(right_row, 3) / pick(sums, 4)), 0.0)
-    step = 6
-    for i in range(channels // step):
+    left_scale = jnp.where(pick(left_row, 4) > 0.0, root * (pick(left_row, 3) / pick(total, 3)), 0.0)
+    right_scale = jnp.where(pick(right_row, 4) > 0.0, root * (pick(right_row, 3) / pick(total, 4)), 0.0)
+    for i in range(CHUNKS):
         at = pl.ds(i * step, step)
-        lo[at] = el_ref[at] * left_scale
-        copies.append(pltpu.make_async_copy(lo.at[at], lo_ref.at[at], sems.at[1 + 2 * i]))
-        copies[-1].start()
-        ro[at] = er_ref[at] * right_scale
-        copies.append(pltpu.make_async_copy(ro.at[at], ro_ref.at[at], sems.at[2 + 2 * i]))
-        copies[-1].start()
-    energy_ref[0] = jnp.sum(pick(sums, 1) / pick(sums, 2))
+        for side, (x, w, scale, out, out_ref) in enumerate(
+            ((xl, wl, left_scale, lo, lo_ref), (xr, wr, right_scale, ro, ro_ref))
+        ):
+            loads[2 * i + side].wait()
+            for c in range(i * step, (i + 1) * step, 2):
+                y = twice(x[pl.ds(c, 2)].reshape(2 * n, n), w) * scale
+                out[c] = y[:n]
+                out[c + 1] = y[n:]
+            copies.append(pltpu.make_async_copy(out.at[at], out_ref.at[at], sems.at[4 + 4 * i + side]))
+            copies[-1].start()
     for copy in copies:
         copy.wait()
 
 
-def call(kernel, args, specs, outs, out_specs=None, scratch=(), flops=0, name=None):
+def call(kernel, args, specs, outs, out_specs=None, scratch=(), flops=0, limit=16, name=None):
     moved = sum(math.prod(a.shape) * a.dtype.itemsize for a in (*args, *outs))
+    args = [pltpu.with_memory_space_constraint(a, pltpu.HBM) if spec is HBM else a for a, spec in zip(args, specs)]
     return pl.pallas_call(
         kernel,
         in_specs=specs,
         out_specs=out_specs or [VMEM] * len(outs),
         out_shape=outs,
         scratch_shapes=list(scratch),
-        compiler_params=pltpu.CompilerParams(vmem_limit_bytes=16 << 20),
+        compiler_params=pltpu.CompilerParams(vmem_limit_bytes=limit << 20),
         cost_estimate=pl.CostEstimate(flops=flops, bytes_accessed=moved, transcendentals=0),
         name=name,
     )(*args)
@@ -250,25 +269,39 @@
     message = SDS((n + 8, n), f32)
     hop_parts = SDS((hops * n, 2 * n), bf16)
     diag_parts = SDS((diags * n, 2 * n), bf16)
-    channel = 8 * 2 * n**3
-
-    (own,) = call(first_message, (sector_sizes, x0), [SMEM, VMEM], [message], name="first_message")
+    out = SDS((diags + hops, n, n), f32)
+    channel = 20 * 8 * 2 * n**3
+
+    own, cl, cr = call(
+        load,
+        (sector_sizes, x0, dl, hl, dr, hr),
+        [SMEM] + [HBM] * 5,
+        [message, out, out],
+        scratch=[
+            pltpu.VMEM((n, n), f32),
+            pltpu.SemaphoreType.DMA((3 + 2 * PARTS,)),
+        ],
+        limit=32,
+        name="load",
+    )
     below0 = lax.ppermute(own, "blk", up)
-    lt, rc, dlt, drc, b = call(
+    lt, rc, dlt, drc, clt, b = call(
         first_adjoint,
-        (own, hl, hr, dl, dr),
-        [VMEM] * 5,
-        [hop_parts, hop_parts, diag_parts, diag_parts, block],
+        (own, cl, cr),
+        [VMEM] * 3,
+        [hop_parts, hop_parts, diag_parts, diag_parts, out, block],
         flops=channel * hops,
         name="first_adjoint",
     )
     got_b = lax.ppermute(b, "blk", down)
-    dl_in, hl_in = lax.ppermute(dl, "seg", seg_up), lax.ppermute(hl, "seg", seg_up)
-    dr_in, hr_in = lax.ppermute(dr, "seg", seg_down), lax.ppermute(hr, "seg", seg_down)
     ops = (lt, rc, dlt, drc)
     (a,) = call(first_apply, (own, below0, *ops), [VMEM] * 6, [block], flops=channel * (hops + diags), name="apply0")
     for k in range(1, ITERS):
         got_a = lax.ppermute(a, "blk", up)
+        if k == 1:
+            xl = lax.ppermute(lax.optimization_barrier((clt, a))[0], "seg", seg_up)
+        if k == 2:
+            xr = lax.ppermute(lax.optimization_barrier((cr, a))[0], "seg", seg_down)
         last_b = b
         v, b = call(
             adjoint, (own, a, got_b, lt, rc), [VMEM] * 5, [block, block], flops=channel * hops, name=f"adjoint{k}"
@@ -285,30 +318,27 @@
     v4, kept = call(finish, (ranks, own, v, a, got_b), [SMEM] + [VMEM] * 4, [block, message], name="finish")
     from_left = lax.ppermute(kept, "seg", seg_up)
     from_right = lax.ppermute(kept, "seg", seg_down)
-    (sums,) = call(sums_message, (kept, from_left, from_right), [VMEM] * 3, [SDS((blocks, n), f32)], name="sums_message")
+    sums_block = SDS((blocks, n), f32)
+    (sums,) = call(sums_message, (kept, from_left, from_right), [VMEM] * 3, [sums_block], name="sums_message")
     sums = lax.all_to_all(sums, "blk", 0, 0, tiled=True)
-    out = SDS((hops + diags, n, n), f32)
-    el, er = call(
+    state, left, right, energy = call(
         extend,
-        (from_left, from_right, dl_in, hl_in, dr_in, hr_in),
-        [VMEM] * 6,
-        [out, out],
-        flops=2 * channel * (hops + diags),
-        name="extend",
-    )
-    state, left, right, energy = call(
-        scaled,
-        (sums, from_left, from_right, v4, el, er),
-        [VMEM] * 6,
+        (sums, from_left, from_right, v4, xl, xr),
+        [ANY, VMEM, VMEM, VMEM, ANY, ANY],
         [block, out, out, SDS((1,), f32)],
         out_specs=[HBM, HBM, HBM, SMEM],
         scratch=[
+            pltpu.VMEM(sums_block.shape, f32),
+            pltpu.VMEM(out.shape, f32),
+            pltpu.VMEM(out.shape, f32),
             pltpu.VMEM((n, n), f32),
             pltpu.VMEM(out.shape, f32),
             pltpu.VMEM(out.shape, f32),
-            pltpu.SemaphoreType.DMA((7,)),
+            pltpu.SemaphoreType.DMA((2 + 4 * CHUNKS,)),
         ],
-        name="scaled",
+        flops=2 * channel * (hops + diags),
+        limit=32,
+        name="extend",
     )
     return state[None, None], left[None, None], right[None, None], energy
 

time: 101 us -> 94.8 us (0.939)
  blocking collectives: 0 us -> 34.5 us
  starting transfers between devices: 65 us -> 35.5 us
  local copies, waits for them, and re-layouts: 9.48 us -> 0 us
  waiting for transfers between devices: 7.7 us -> 4.89 us
    all_to_all x0 -> x1, blocking collectives: none -> 34.5 us  [shards(): sums = lax.all_to_all(sums, 'blk', 0, 0, tiled=True)]
    all_to_all x1 -> x0, starting transfers between devices: 24.3 us -> none  [shards(): sums = lax.all_to_all(sums, 'blk', 0, 0, tiled=True)]
    unnamed x22 -> x0, local copies, waits for them, and re-layouts: 9.48 us -> none
    ppermute x4 -> x2, starting transfers between devices: 14.5 us -> 8.25 us  [the longest x1 4.52 us: shards(): xl = lax.ppermute(lax.optimization_barrier((clt, a))[0], 'seg', seg_up)]
    ppermute x1, waiting for transfers between devices: 3.7 us -> 0.05 us  [shards(): from_right = lax.ppermute(kept, 'seg', seg_down)]
    ppermute x1, starting transfers between devices: 5.91 us -> 3.13 us  [shards(): from_left = lax.ppermute(kept, 'seg', seg_up)]
    ppermute x1, starting transfers between devices: 1.29 us -> 4.03 us  [shards(): below0 = lax.ppermute(own, 'blk', up)]
    all_to_all x1 -> x0, waiting for transfers between devices: 1.84 us -> none  [shards(): sums = lax.all_to_all(sums, 'blk', 0, 0, tiled=True)]
  transfers between devices with their start and end apart: 15 -> 12, of which waited for: 3 -> 2; matrix products, arithmetic and copies ran while one was open for 0% -> 0% of each run, Pallas kernels for 13% -> 9%
where the time goes in v2:
time: 94.8 us; the launch traced here: 93.1 us
  starting transfers between devices  35.5 us (37%)
  blocking collectives  34.5 us (36%)
  Pallas kernels  16 us (17%)
  waiting for transfers between devices  4.89 us (5%)
  between operations  2.15 us (2%)
    all_to_all x1, blocking collectives, shards(): sums = lax.all_to_all(sums, 'blk', 0, 0, tiled=True)  34.5 us
    pallas_call x12, Pallas kernels, call(): pl.pallas_call(kernel, in_specs=specs, out_specs=out_specs or [VMEM] * le...  16 us
    ppermute x3, starting transfers between devices, shards(): got_a = lax.ppermute(a, 'blk', up)  12.5 us
    ppermute x4, starting transfers between devices, shards(): got_b = lax.ppermute(b, 'blk', down)  5.17 us
    ppermute x1, starting transfers between devices, shards(): xl = lax.ppermute(lax.optimization_barrier((clt, a))[0], 'seg', seg_up)  4.52 us
    ppermute x1, starting transfers between devices, shards(): below0 = lax.ppermute(own, 'blk', up)  4.03 us
    ppermute x1, starting transfers between devices, shards(): xr = lax.ppermute(lax.optimization_barrier((cr, a))[0], 'seg', seg_down)  3.73 us
    ppermute x4, waiting for transfers between devices, shards(): got_b = lax.ppermute(b, 'blk', down)  3.53 us
  transfers between devices with their start and end apart: 12, of which 2 were waited for; matrix products, arithmetic and copies ran while one was open for 0% of the time, Pallas kernels for 9%

profile of v2, /device:TPU:1, one launch (start us, length us, event | category | flops | bytes accessed | tf_op | source)
XLA Modules:
  0.0 93.1 jit_solution(5022312297420238979)
XLA Ops:
  1.3 1.8 %load.1 = (f32[136,128]{1,0:T(8,128)S(1)}, f32[18,128,128]{2,1,0:T(8,128)S(1)}, f32[18,128,128]{2,1,0:T(8,128)S(1)}) custom-call(s32[1,1]{1,0:T(1,128)S(6)} %copy.12.size_ref, f32[128,128]{1,0:T(8,128)} %bitcast.18, f32[2,128,128]{2,1,0:T(8,128)} %bitcast.16, f32[16,128,128]{2,1,0:T(8,128)} %bitcast.14, f32[2,128,128]{2,1,0:T(8,128)} %bitcast.17, ...), custom_call_target="tpu_custom_call" | custom-call | bytes 4853764 | tf_op jit(solution)/shard_map/load/pallas_call | solution.py:246
  3.0 4.0 %collective-permute-start = (f32[136,128]{1,0:T(8,128)S(1)}, f32[136,128]{1,0:T(8,128)S(1)}, u32[]{:S(2)}, u32[]{:S(2)}) collective-permute-start(f32[136,128]{1,0:T(8,128)S(1)} %get-tuple-element.27.own_ref), channel_id=1, source_target_pairs={{0,1},{1,2},{2,3},{3,4},{4,5},{5,6},{6,7},{7,8},{8,9},{9,10},{10,1... | collective-permute-start | bytes 208904 | tf_op jit(solution)/shard_map/ppermute | solution.py:287
  7.1 1.0 %first_adjoint.1 = (bf16[2048,256]{1,0:T(8,128)(2,1)S(1)}, bf16[2048,256]{1,0:T(8,128)(2,1)S(1)}, bf16[256,256]{1,0:T(8,128)(2,1)S(1)}, bf16[256,256]{1,0:T(8,12...) custom-call(f32[136,128]{1,0:T(8,128)S(1)} %get-tuple-element.27.own_ref, ...), custom_call_target="tpu_custom_call" | custom-call | flops 10737418240 | bytes 6033408 | tf_op jit(solution)/shard_map/first_adjoint/pallas_call | solution.py:246
  8.1 1.3 %collective-permute-start.1 = (f32[128,128]{1,0:T(8,128)S(1)}, f32[128,128]{1,0:T(8,128)S(1)}, u32[]{:S(2)}, u32[]{:S(2)}) collective-permute-start(f32[128,128]{1,0:T(8,128)S(1)} %get-tuple-element.34.b_ref), channel_id=1, source_target_pairs={{1,0},{2,1},{3,2},{4,3},{5,4},{6,5},{7,6},{8,7},{9,8},{10,9},{11,1... | collective-permute-start | bytes 196616 | tf_op jit(solution)/shard_map/ppermute | solution.py:296
  10.1 0.0 collective-permute-done.below_ref
  10.1 1.0 %apply0.1.a_ref = f32[128,128]{1,0:T(8,128)S(1)} custom-call(f32[136,128]{1,0:T(8,128)S(1)} %get-tuple-element.27.own_ref, f32[136,128]{1,0:T(8,128)S(1)} %collective-permute-done.below_ref, bf16[2048,256]{1,0:T(8,128)(2,1)S(1)} %get-tuple-element.30.lt_ref, bf16[2048,256]{1,0:T(8,128)(2,1)S(1)} %get-tuple-element.31.rc_ref, ...), custom_call_target="tpu_custom_call" | custom-call | flops 12079595520 | bytes 2564096 | tf_op jit(solution)/shard_map/apply0/pallas_call | solution.py:246
  11.1 4.0 %collective-permute-start.2 = (f32[128,128]{1,0:T(8,128)S(1)}, f32[128,128]{1,0:T(8,128)S(1)}, u32[]{:S(2)}, u32[]{:S(2)}) collective-permute-start(f32[128,128]{1,0:T(8,128)S(1)} %apply0.1.a_ref), channel_id=1, source_target_pairs={{0,1},{1,2},{2,3},{3,4},{4,5},{5,6},{6,7},{7,8},{8,9},{9,10},{10,1... | collective-permute-start | bytes 196616 | tf_op jit(solution)/shard_map/ppermute | solution.py:300
  15.1 0.0 collective-permute-done.1.got_b_ref
  15.2 0.9 %adjoint1.1 = (f32[128,128]{1,0:T(8,128)S(1)}, f32[128,128]{1,0:T(8,128)S(1)}) custom-call(f32[136,128]{1,0:T(8,128)S(1)} %get-tuple-element.27.own_ref, f32[128,128]{1,0:T(8,128)S(1)} %apply0.1.a_ref, f32[128,128]{1,0:T(8,128)S(1)} %collective-permute-done.1.got_b_ref, bf16[2048,256]{1,0:T(8,128)(2,1)S(1)} %get-tuple-element.30.lt_ref, ...), custom_call_target="tpu_custom_call" | custom-call | flops 10737418240 | bytes 2428928 | tf_op jit(solution)/shard_map/adjoint1/pallas_call | solution.py:246
  16.1 1.3 %collective-permute-start.3 = (f32[128,128]{1,0:T(8,128)S(1)}, f32[128,128]{1,0:T(8,128)S(1)}, u32[]{:S(2)}, u32[]{:S(2)}) collective-permute-start(f32[128,128]{1,0:T(8,128)S(1)} %get-tuple-element.36.b_ref), channel_id=1, source_target_pairs={{1,0},{2,1},{3,2},{4,3},{5,4},{6,5},{7,6},{8,7},{9,8},{10,9},{11,1... | collective-permute-start | bytes 196616 | tf_op jit(solution)/shard_map/ppermute | solution.py:309
  17.4 4.5 %collective-permute-start.10 = (f32[18,128,128]{2,1,0:T(8,128)S(1)}, f32[18,128,128]{2,1,0:T(8,128)S(1)}, u32[]{:S(2)}, u32[]{:S(2)}) collective-permute-start(f32[18,128,128]{2,1,0:T(8,128)S(1)} %get-tuple-element.44), channel_id=1, source_target_pairs={{0,64},{64,128},{128,192},{192,256},{256,320},{320,384},{384,448},... | collective-permute-start | bytes 3538952 | tf_op jit(solution)/shard_map/ppermute | solution.py:302
  21.9 0.0 collective-permute-done.2.got_a_ref
  21.9 1.0 %apply1.1.a_ref = f32[128,128]{1,0:T(8,128)S(1)} custom-call(f32[136,128]{1,0:T(8,128)S(1)} %get-tuple-element.27.own_ref, f32[136,128]{1,0:T(8,128)S(1)} %collective-permute-done.below_ref, f32[128,128]{1,0:T(8,128)S(1)} %get-tuple-element.35.v_ref, f32[128,128]{1,0:T(8,128)S(1)} %collective-permute-done.2.got_a_ref, ...), custom_call_target="tpu_custom_call" | custom-call | flops 12079595520 | bytes 2760704 | tf_op jit(solution)/shard_map/apply1/pallas_call | solution.py:246
  23.0 4.3 %collective-permute-start.4 = (f32[128,128]{1,0:T(8,128)S(1)}, f32[128,128]{1,0:T(8,128)S(1)}, u32[]{:S(2)}, u32[]{:S(2)}) collective-permute-start(f32[128,128]{1,0:T(8,128)S(1)} %apply1.1.a_ref), channel_id=1, source_target_pairs={{0,1},{1,2},{2,3},{3,4},{4,5},{5,6},{6,7},{7,8},{8,9},{9,10},{10,1... | collective-permute-start | bytes 196616 | tf_op jit(solution)/shard_map/ppermute | solution.py:300
  27.3 0.0 collective-permute-done.3.got_b_ref
  27.3 0.9 %adjoint2.1 = (f32[128,128]{1,0:T(8,128)S(1)}, f32[128,128]{1,0:T(8,128)S(1)}) custom-call(f32[136,128]{1,0:T(8,128)S(1)} %get-tuple-element.27.own_ref, f32[128,128]{1,0:T(8,128)S(1)} %apply1.1.a_ref, f32[128,128]{1,0:T(8,128)S(1)} %collective-permute-done.3.got_b_ref, bf16[2048,256]{1,0:T(8,128)(2,1)S(1)} %get-tuple-element.30.lt_ref, ...), custom_call_target="tpu_custom_call" | custom-call | flops 10737418240 | bytes 2428928 | tf_op jit(solution)/shard_map/adjoint2/pallas_call | solution.py:246
  28.2 1.3 %collective-permute-start.5 = (f32[128,128]{1,0:T(8,128)S(1)}, f32[128,128]{1,0:T(8,128)S(1)}, u32[]{:S(2)}, u32[]{:S(2)}) collective-permute-start(f32[128,128]{1,0:T(8,128)S(1)} %get-tuple-element.38.b_ref), channel_id=1, source_target_pairs={{1,0},{2,1},{3,2},{4,3},{5,4},{6,5},{7,6},{8,7},{9,8},{10,9},{11,1... | collective-permute-start | bytes 196616 | tf_op jit(solution)/shard_map/ppermute | solution.py:309
  29.5 3.7 %collective-permute-start.11 = (f32[18,128,128]{2,1,0:T(8,128)S(1)}, f32[18,128,128]{2,1,0:T(8,128)S(1)}, u32[]{:S(2)}, u32[]{:S(2)}) collective-permute-start(f32[18,128,128]{2,1,0:T(8,128)S(1)} %get-tuple-element.45.cr_ref), channel_id=1, source_target_pairs={{64,0},{128,64},{192,128},{256,192},{320,256},{384,320},{448,384},... | collective-permute-start | bytes 3538952 | tf_op jit(solution)/shard_map/ppermute | solution.py:304
  33.3 0.0 collective-permute-done.4.got_a_ref
  33.3 1.0 %apply2.1.a_ref = f32[128,128]{1,0:T(8,128)S(1)} custom-call(f32[136,128]{1,0:T(8,128)S(1)} %get-tuple-element.27.own_ref, f32[136,128]{1,0:T(8,128)S(1)} %collective-permute-done.below_ref, f32[128,128]{1,0:T(8,128)S(1)} %get-tuple-element.37.v_ref, f32[128,128]{1,0:T(8,128)S(1)} %collective-permute-done.4.got_a_ref, ...), custom_call_target="tpu_custom_call" | custom-call | flops 12079595520 | bytes 2760704 | tf_op jit(solution)/shard_map/apply2/pallas_call | solution.py:246
  34.3 4.3 %collective-permute-start.6 = (f32[128,128]{1,0:T(8,128)S(1)}, f32[128,128]{1,0:T(8,128)S(1)}, u32[]{:S(2)}, u32[]{:S(2)}) collective-permute-start(f32[128,128]{1,0:T(8,128)S(1)} %apply2.1.a_ref), channel_id=1, source_target_pairs={{0,1},{1,2},{2,3},{3,4},{4,5},{5,6},{6,7},{7,8},{8,9},{9,10},{10,1... | collective-permute-start | bytes 196616 | tf_op jit(solution)/shard_map/ppermute | solution.py:300
  38.6 0.0 collective-permute-done.5.got_b_ref
  38.6 0.9 %adjoint3.1 = (f32[128,128]{1,0:T(8,128)S(1)}, f32[128,128]{1,0:T(8,128)S(1)}) custom-call(f32[136,128]{1,0:T(8,128)S(1)} %get-tuple-element.27.own_ref, f32[128,128]{1,0:T(8,128)S(1)} %apply2.1.a_ref, f32[128,128]{1,0:T(8,128)S(1)} %collective-permute-done.5.got_b_ref, bf16[2048,256]{1,0:T(8,128)(2,1)S(1)} %get-tuple-element.30.lt_ref, ...), custom_call_target="tpu_custom_call" | custom-call | flops 10737418240 | bytes 2428928 | tf_op jit(solution)/shard_map/adjoint3/pallas_call | solution.py:246
  39.5 1.3 %collective-permute-start.7 = (f32[128,128]{1,0:T(8,128)S(1)}, f32[128,128]{1,0:T(8,128)S(1)}, u32[]{:S(2)}, u32[]{:S(2)}) collective-permute-start(f32[128,128]{1,0:T(8,128)S(1)} %get-tuple-element.40), channel_id=1, source_target_pairs={{1,0},{2,1},{3,2},{4,3},{5,4},{6,5},{7,6},{8,7},{9,8},{10,9},{11,1... | collective-permute-start | bytes 196616 | tf_op jit(solution)/shard_map/ppermute | solution.py:309
  40.8 0.0 collective-permute-done.6.got_a_ref
  40.9 1.0 %apply3.1.part_ref = f32[128,128]{1,0:T(8,128)S(1)} custom-call(f32[136,128]{1,0:T(8,128)S(1)} %get-tuple-element.27.own_ref, f32[136,128]{1,0:T(8,128)S(1)} %collective-permute-done.below_ref, f32[128,128]{1,0:T(8,128)S(1)} %get-tuple-element.39.v_ref, f32[128,128]{1,0:T(8,128)S(1)} %collective-permute-done.6.got_a_ref, ...), custom_call_target="tpu_custom_call" | custom-call | flops 12079595520 | bytes 2760704 | tf_op jit(solution)/shard_map/apply3/pallas_call | solution.py:246
  41.9 3.5 %collective-permute-done.7.got_b_ref = f32[128,128]{1,0:T(8,128)S(1)} collective-permute-done((f32[128,128]{1,0:T(8,128)S(1)}, f32[128,128]{1,0:T(8,128)S(1)}, u32[]{:S(2)}, u32[]{:S(2)}) %collective-permute-start.7) | collective-permute-done | bytes 65568 | tf_op jit(solution)/shard_map/ppermute | solution.py:309
  45.4 0.1 finish.1
  45.6 2.4 %collective-permute-start.9 = (f32[136,128]{1,0:T(8,128)S(1)}, f32[136,128]{1,0:T(8,128)S(1)}, u32[]{:S(2)}, u32[]{:S(2)}) collective-permute-start(f32[136,128]{1,0:T(8,128)S(1)} %get-tuple-element.41.own_ref), channel_id=1, source_target_pairs={{64,0},{128,64},{192,128},{256,192},{320,256},{384,320},{448,384},... | collective-permute-start | bytes 208904 | tf_op jit(solution)/shard_map/ppermute | solution.py:320
  48.0 3.1 %collective-permute-start.8 = (f32[136,128]{1,0:T(8,128)S(1)}, f32[136,128]{1,0:T(8,128)S(1)}, u32[]{:S(2)}, u32[]{:S(2)}) collective-permute-start(f32[136,128]{1,0:T(8,128)S(1)} %get-tuple-element.41.own_ref), channel_id=1, source_target_pairs={{0,64},{64,128},{128,192},{192,256},{256,320},{320,384},{384,448},... | collective-permute-start | bytes 208904 | tf_op jit(solution)/shard_map/ppermute | solution.py:319
  51.1 0.1 collective-permute-done.9.right_ref
  51.2 1.3 %collective-permute-done.8.left_ref = f32[136,128]{1,0:T(8,128)S(1)} collective-permute-done((f32[136,128]{1,0:T(8,128)S(1)}, f32[136,128]{1,0:T(8,128)S(1)}, u32[]{:S(2)}, u32[]{:S(2)}) %collective-permute-start.8) | collective-permute-done | bytes 69664 | tf_op jit(solution)/shard_map/ppermute | solution.py:319
  52.5 0.1 sums_message.1
  52.6 34.5 %all_to_all.11 = f32[64,1,128]{2,1,0:T(1,128)S(1)} all-to-all(f32[64,1,128]{2,1,0:T(1,128)S(1)} %bitcast.12), channel_id=1, replica_groups=mesh['seg'=8,'blk'=64] {'blk'}, dimensions={0} | all-to-all | bytes 65536 | tf_op jit(solution)/shard_map/all_to_all | solution.py:323
  87.1 0.0 collective-permute-done.10.xl_ref
  87.1 0.0 collective-permute-done.11.xr_ref
  87.1 6.1 %extend.1 = (f32[128,128]{1,0:T(8,128)}, f32[18,128,128]{2,1,0:T(8,128)}, f32[18,128,128]{2,1,0:T(8,128)}, f32[1]{0:T(128)}) custom-call(f32[64,128]{1,0:T(8,128)S(1)} %bitcast.13, f32[136,128]{1,0:T(8,128)S(1)} %collective-permute-done.8.left_ref, f32[136,128]{1,0:T(8,128)S(1)} %collective-permute-done.9.right_ref, ...), custom_call_target="tpu_custom_call" | custom-call | flops 24159191040 | bytes 5021700 | tf_op jit(solution)/shard_map/extend/pallas_call | solution.py:246
Async XLA Ops:
  3.0 7.0 %collective-permute-start = (f32[136,128]{1,0:T(8,128)S(1)}, f32[136,128]{1,0:T(8,128)S(1)}, u32[]{:S(2)}, u32[]{:S(2)}) collective-permute-start(f32[136,128]{1,0:T(8,128)S(1)} %get-tuple-element.27.own_ref), channel_id=1, source_target_pairs={{0,1},{1,2},{2,3},{3,4},{4,5},{5,6},{6,7},{7,8},{8,9},{9,10},{10,1... | collective-permute-start | bytes 208904 | tf_op jit(solution)/shard_map/ppermute | solution.py:287
  8.1 7.0 %collective-permute-start.1 = (f32[128,128]{1,0:T(8,128)S(1)}, f32[128,128]{1,0:T(8,128)S(1)}, u32[]{:S(2)}, u32[]{:S(2)}) collective-permute-start(f32[128,128]{1,0:T(8,128)S(1)} %get-tuple-element.34.b_ref), channel_id=1, source_target_pairs={{1,0},{2,1},{3,2},{4,3},{5,4},{6,5},{7,6},{8,7},{9,8},{10,9},{11,1... | collective-permute-start | bytes 196616 | tf_op jit(solution)/shard_map/ppermute | solution.py:296
  11.1 10.8 %collective-permute-start.2 = (f32[128,128]{1,0:T(8,128)S(1)}, f32[128,128]{1,0:T(8,128)S(1)}, u32[]{:S(2)}, u32[]{:S(2)}) collective-permute-start(f32[128,128]{1,0:T(8,128)S(1)} %apply0.1.a_ref), channel_id=1, source_target_pairs={{0,1},{1,2},{2,3},{3,4},{4,5},{5,6},{6,7},{7,8},{8,9},{9,10},{10,1... | collective-permute-start | bytes 196616 | tf_op jit(solution)/shard_map/ppermute | solution.py:300
  16.1 11.2 %collective-permute-start.3 = (f32[128,128]{1,0:T(8,128)S(1)}, f32[128,128]{1,0:T(8,128)S(1)}, u32[]{:S(2)}, u32[]{:S(2)}) collective-permute-start(f32[128,128]{1,0:T(8,128)S(1)} %get-tuple-element.36.b_ref), channel_id=1, source_target_pairs={{1,0},{2,1},{3,2},{4,3},{5,4},{6,5},{7,6},{8,7},{9,8},{10,9},{11,1... | collective-permute-start | bytes 196616 | tf_op jit(solution)/shard_map/ppermute | solution.py:309
  17.4 69.7 %collective-permute-start.10 = (f32[18,128,128]{2,1,0:T(8,128)S(1)}, f32[18,128,128]{2,1,0:T(8,128)S(1)}, u32[]{:S(2)}, u32[]{:S(2)}) collective-permute-start(f32[18,128,128]{2,1,0:T(8,128)S(1)} %get-tuple-element.44), channel_id=1, source_target_pairs={{0,64},{64,128},{128,192},{192,256},{256,320},{320,384},{384,448},... | collective-permute-start | bytes 3538952 | tf_op jit(solution)/shard_map/ppermute | solution.py:302
  23.0 10.3 %collective-permute-start.4 = (f32[128,128]{1,0:T(8,128)S(1)}, f32[128,128]{1,0:T(8,128)S(1)}, u32[]{:S(2)}, u32[]{:S(2)}) collective-permute-start(f32[128,128]{1,0:T(8,128)S(1)} %apply1.1.a_ref), channel_id=1, source_target_pairs={{0,1},{1,2},{2,3},{3,4},{4,5},{5,6},{6,7},{7,8},{8,9},{9,10},{10,1... | collective-permute-start | bytes 196616 | tf_op jit(solution)/shard_map/ppermute | solution.py:300
  28.2 10.4 %collective-permute-start.5 = (f32[128,128]{1,0:T(8,128)S(1)}, f32[128,128]{1,0:T(8,128)S(1)}, u32[]{:S(2)}, u32[]{:S(2)}) collective-permute-start(f32[128,128]{1,0:T(8,128)S(1)} %get-tuple-element.38.b_ref), channel_id=1, source_target_pairs={{1,0},{2,1},{3,2},{4,3},{5,4},{6,5},{7,6},{8,7},{9,8},{10,9},{11,1... | collective-permute-start | bytes 196616 | tf_op jit(solution)/shard_map/ppermute | solution.py:309
  29.5 57.6 %collective-permute-start.11 = (f32[18,128,128]{2,1,0:T(8,128)S(1)}, f32[18,128,128]{2,1,0:T(8,128)S(1)}, u32[]{:S(2)}, u32[]{:S(2)}) collective-permute-start(f32[18,128,128]{2,1,0:T(8,128)S(1)} %get-tuple-element.45.cr_ref), channel_id=1, source_target_pairs={{64,0},{128,64},{192,128},{256,192},{320,256},{384,320},{448,384},... | collective-permute-start | bytes 3538952 | tf_op jit(solution)/shard_map/ppermute | solution.py:304
  34.3 6.5 %collective-permute-start.6 = (f32[128,128]{1,0:T(8,128)S(1)}, f32[128,128]{1,0:T(8,128)S(1)}, u32[]{:S(2)}, u32[]{:S(2)}) collective-permute-start(f32[128,128]{1,0:T(8,128)S(1)} %apply2.1.a_ref), channel_id=1, source_target_pairs={{0,1},{1,2},{2,3},{3,4},{4,5},{5,6},{6,7},{7,8},{8,9},{9,10},{10,1... | collective-permute-start | bytes 196616 | tf_op jit(solution)/shard_map/ppermute | solution.py:300
  39.5 5.9 %collective-permute-start.7 = (f32[128,128]{1,0:T(8,128)S(1)}, f32[128,128]{1,0:T(8,128)S(1)}, u32[]{:S(2)}, u32[]{:S(2)}) collective-permute-start(f32[128,128]{1,0:T(8,128)S(1)} %get-tuple-element.40), channel_id=1, source_target_pairs={{1,0},{2,1},{3,2},{4,3},{5,4},{6,5},{7,6},{8,7},{9,8},{10,9},{11,1... | collective-permute-start | bytes 196616 | tf_op jit(solution)/shard_map/ppermute | solution.py:309
  45.6 5.6 %collective-permute-start.9 = (f32[136,128]{1,0:T(8,128)S(1)}, f32[136,128]{1,0:T(8,128)S(1)}, u32[]{:S(2)}, u32[]{:S(2)}) collective-permute-start(f32[136,128]{1,0:T(8,128)S(1)} %get-tuple-element.41.own_ref), channel_id=1, source_target_pairs={{64,0},{128,64},{192,128},{256,192},{320,256},{384,320},{448,384},... | collective-permute-start | bytes 208904 | tf_op jit(solution)/shard_map/ppermute | solution.py:320
  48.0 4.5 %collective-permute-start.8 = (f32[136,128]{1,0:T(8,128)S(1)}, f32[136,128]{1,0:T(8,128)S(1)}, u32[]{:S(2)}, u32[]{:S(2)}) collective-permute-start(f32[136,128]{1,0:T(8,128)S(1)} %get-tuple-element.41.own_ref), channel_id=1, source_target_pairs={{0,64},{64,128},{128,192},{192,256},{256,320},{320,384},{384,448},... | collective-permute-start | bytes 208904 | tf_op jit(solution)/shard_map/ppermute | solution.py:319

commit v3 on v2

--- a/solution.py
+++ b/solution.py
@@ -148,93 +148,61 @@
     return jnp.sum(jnp.sum(x, axis=0, keepdims=True), axis=1, keepdims=True)
 
 
-def finish(rank_ref, own_ref, v_ref, part_ref, got_b_ref, v4_ref, kept_ref):
-    n = own_ref.shape[1]
-    size = own_ref[n : n + 1, :]
+def finish(rank_ref, own_ref, v_ref, part_ref, got_b_ref, v4_ref, sums_ref):
+    n = own_ref.shape[1]
     v = v_ref[...]
-    applied = part_ref[...] + where(square_mask(size), got_b_ref[...])
+    applied = part_ref[...] + where(square_mask(own_ref[n : n + 1, :]), got_b_ref[...])
     v4 = SHIFT * v - applied
-    v4_ref[...] = v4
-    square = total_of(v4 * v4)
-    top = total_of(v * applied)
-    low = total_of(v * v)
-    safe = jnp.maximum(square, 1e-37)
-    kept_cols = jnp.minimum(jnp.full((1, n), rank_ref[0, 0].astype(f32), f32), size)
+    v4_ref[:n, :] = v4
+    kept_cols = jnp.minimum(jnp.full((1, n), rank_ref[0, 0].astype(f32), f32), own_ref[n : n + 1, :])
+    v4_ref[n:, :] = jnp.broadcast_to(kept_cols, (8, n))
+    lane = lax.broadcasted_iota(jnp.int32, (1, n), 1)
+    row = jnp.where(lane == 0, total_of(v4 * v4), 0.0)
+    row = jnp.where(lane == 1, total_of(v * applied), row)
+    row = jnp.where(lane == 2, total_of(v * v), row)
+    sums_ref[...] = jnp.broadcast_to(row, sums_ref.shape)
+
+
+def normalise(v4_ref, sums_ref, state_ref, kept_ref, energy_ref):
+    n = v4_ref.shape[1]
+    total = jnp.sum(sums_ref[...], axis=0, keepdims=True)
+    lane = lax.broadcasted_iota(jnp.int32, (1, n), 1)
+
+    def pick(j):
+        return jnp.sum(jnp.where(lane == j, total, 0.0), axis=1, keepdims=True)
+
+    state = v4_ref[:n, :] * jnp.sqrt(BOND * n / pick(0))
+    state_ref[...] = state
     cols = lax.broadcasted_iota(jnp.int32, (n, n), 1).astype(f32)
-    kept = where(cols < jnp.broadcast_to(kept_cols, (n, n)), v4)
-    kept_ref[:n, :] = kept * lax.rsqrt(safe)
-    lane = lax.broadcasted_iota(jnp.int32, (8, n), 1)
-    row = jnp.where(lane == 0, square, 0.0)
-    row = jnp.where(lane == 1, top, row)
-    row = jnp.where(lane == 2, low, row)
-    row = jnp.where(lane == 3, safe, row)
-    row = jnp.where(lane == 4, 1.0, row)
-    kept_ref[n:, :] = row
-
-
-def sums_message(own_ref, left_ref, right_ref, out_ref):
-    n = own_ref.shape[1]
-    lane = lax.broadcasted_iota(jnp.int32, (1, n), 1)
-
-    def pick(ref, j):
-        return jnp.sum(jnp.where(lane == j, ref[n : n + 1, :], 0.0), axis=1, keepdims=True)
-
-    row = jnp.where(lane < 3, own_ref[n : n + 1, :], 0.0)
-    row = jnp.where(lane == 3, pick(left_ref, 0), row)
-    row = jnp.where(lane == 4, pick(right_ref, 0), row)
-    out_ref[...] = jnp.broadcast_to(row, out_ref.shape)
-
-
-def twice(x, w):
-    n = x.shape[1]
-    half = folded(dot(jnp.concatenate(split(x), 1), w))
-    flip = jnp.concatenate([half[:n].T, half[n:].T], 0)
-    return folded(dot(jnp.concatenate(split(flip), 1), w))
-
-
-def extend(
-    sums_ref, left_ref, right_ref, v4_ref, xl_ref, xr_ref, state_ref, lo_ref, ro_ref, energy_ref, sums, xl, xr, state, lo, ro, sems
-):
-    n = v4_ref.shape[1]
-    channels = xl.shape[0]
+    kept_ref[...] = where(cols < jnp.broadcast_to(v4_ref[n : n + 1, :], (n, n)), state)
+    energy_ref[0] = jnp.sum(pick(1) / pick(2))
+
+
+def parts(xl_ref, xr_ref, pl_ref, pr_ref):
+    n = xl_ref.shape[1]
+    for c in range(xl_ref.shape[0]):
+        put_parts(pl_ref, c, n, xl_ref[c])
+        put_parts(pr_ref, c, n, xr_ref[c])
+
+
+def extend(left_ref, right_ref, state_ref, pl_ref, pr_ref, new_ref, lo_ref, ro_ref, lo, ro, sems):
+    n = left_ref.shape[0]
+    channels = lo.shape[0]
+    scale = 1.0 / math.sqrt(n)
+    copies = [pltpu.make_async_copy(state_ref, new_ref, sems.at[0])]
+    copies[0].start()
+    sides = ((pl_ref, weight(left_ref[...]), lo, lo_ref), (pr_ref, weight(right_ref[...].T), ro, ro_ref))
     step = channels // CHUNKS
-    get_sums = pltpu.make_async_copy(sums_ref, sums, sems.at[0])
-    get_sums.start()
-    loads, copies = [], []
     for i in range(CHUNKS):
         at = pl.ds(i * step, step)
-        loads.append(pltpu.make_async_copy(xl_ref.at[at], xl.at[at], sems.at[2 + 4 * i]))
-        loads.append(pltpu.make_async_copy(xr_ref.at[at], xr.at[at], sems.at[3 + 4 * i]))
-    for copy in loads:
-        copy.start()
-    wl = weight(left_ref[:n, :])
-    wr = weight(right_ref[:n, :].T)
-    get_sums.wait()
-    total = jnp.sum(sums[...], axis=0, keepdims=True)
-    lane = lax.broadcasted_iota(jnp.int32, (1, n), 1)
-
-    def pick(row, j):
-        return jnp.sum(jnp.where(lane == j, row, 0.0), axis=1, keepdims=True)
-
-    state[...] = v4_ref[...] * jnp.sqrt(BOND * n / pick(total, 0))
-    copies.append(pltpu.make_async_copy(state, state_ref, sems.at[1]))
-    copies[0].start()
-    energy_ref[0] = jnp.sum(pick(total, 1) / pick(total, 2))
-    left_row, right_row = left_ref[n : n + 1, :], right_ref[n : n + 1, :]
-    root = BOND * n / math.sqrt(n)
-    left_scale = jnp.where(pick(left_row, 4) > 0.0, root * (pick(left_row, 3) / pick(total, 3)), 0.0)
-    right_scale = jnp.where(pick(right_row, 4) > 0.0, root * (pick(right_row, 3) / pick(total, 4)), 0.0)
-    for i in range(CHUNKS):
-        at = pl.ds(i * step, step)
-        for side, (x, w, scale, out, out_ref) in enumerate(
-            ((xl, wl, left_scale, lo, lo_ref), (xr, wr, right_scale, ro, ro_ref))
-        ):
-            loads[2 * i + side].wait()
+        for side, (x, w, out, out_ref) in enumerate(sides):
             for c in range(i * step, (i + 1) * step, 2):
-                y = twice(x[pl.ds(c, 2)].reshape(2 * n, n), w) * scale
+                half = folded(dot(x[pl.ds(c * n, 2 * n), :], w))
+                flip = jnp.concatenate([half[:n].T, half[n:].T], 0)
+                y = folded(dot(jnp.concatenate(split(flip), 1), w)) * scale
                 out[c] = y[:n]
                 out[c + 1] = y[n:]
-            copies.append(pltpu.make_async_copy(out.at[at], out_ref.at[at], sems.at[4 + 4 * i + side]))
+            copies.append(pltpu.make_async_copy(out.at[at], out_ref.at[at], sems.at[1 + 2 * i + side]))
             copies[-1].start()
     for copy in copies:
         copy.wait()
@@ -298,15 +266,14 @@
     (a,) = call(first_apply, (own, below0, *ops), [VMEM] * 6, [block], flops=channel * (hops + diags), name="apply0")
     for k in range(1, ITERS):
         got_a = lax.ppermute(a, "blk", up)
-        if k == 1:
-            xl = lax.ppermute(lax.optimization_barrier((clt, a))[0], "seg", seg_up)
-        if k == 2:
-            xr = lax.ppermute(lax.optimization_barrier((cr, a))[0], "seg", seg_down)
         last_b = b
         v, b = call(
             adjoint, (own, a, got_b, lt, rc), [VMEM] * 5, [block, block], flops=channel * hops, name=f"adjoint{k}"
         )
         got_b = lax.ppermute(b, "blk", down)
+        if k == ITERS - 1:
+            xl = lax.ppermute(lax.optimization_barrier((clt, b))[0], "seg", seg_up)
+            xr = lax.ppermute(lax.optimization_barrier((cr, b))[0], "seg", seg_down)
         (a,) = call(
             functools.partial(later_apply, k == ITERS - 1),
             (own, below0, v, got_a, last_b, *ops),
@@ -315,29 +282,33 @@
             flops=channel * (hops + diags),
             name=f"apply{k}",
         )
-    v4, kept = call(finish, (ranks, own, v, a, got_b), [SMEM] + [VMEM] * 4, [block, message], name="finish")
+    sums_block = SDS((blocks, n), f32)
+    v4, sums = call(finish, (ranks, own, v, a, got_b), [SMEM] + [VMEM] * 4, [message, sums_block], name="finish")
+    sums = lax.all_to_all(sums, "blk", 0, 0, tiled=True)
+    state, kept, energy = call(
+        normalise,
+        (v4, sums),
+        [VMEM] * 2,
+        [block, block, SDS((1,), f32)],
+        out_specs=[VMEM, VMEM, SMEM],
+        name="normalise",
+    )
     from_left = lax.ppermute(kept, "seg", seg_up)
     from_right = lax.ppermute(kept, "seg", seg_down)
-    sums_block = SDS((blocks, n), f32)
-    (sums,) = call(sums_message, (kept, from_left, from_right), [VMEM] * 3, [sums_block], name="sums_message")
-    sums = lax.all_to_all(sums, "blk", 0, 0, tiled=True)
-    state, left, right, energy = call(
+    all_parts = SDS(((diags + hops) * n, 2 * n), bf16)
+    xl, xr = call(parts, (xl, xr), [VMEM] * 2, [all_parts, all_parts], flops=channel * hops, name="parts")
+    state, left, right = call(
         extend,
-        (sums, from_left, from_right, v4, xl, xr),
-        [ANY, VMEM, VMEM, VMEM, ANY, ANY],
-        [block, out, out, SDS((1,), f32)],
-        out_specs=[HBM, HBM, HBM, SMEM],
+        (from_left, from_right, state, xl, xr),
+        [VMEM] * 5,
+        [block, out, out],
+        out_specs=[ANY] * 3,
         scratch=[
-            pltpu.VMEM(sums_block.shape, f32),
             pltpu.VMEM(out.shape, f32),
             pltpu.VMEM(out.shape, f32),
-            pltpu.VMEM((n, n), f32),
-            pltpu.VMEM(out.shape, f32),
-            pltpu.VMEM(out.shape, f32),
-            pltpu.SemaphoreType.DMA((2 + 4 * CHUNKS,)),
+            pltpu.SemaphoreType.DMA((1 + 2 * CHUNKS,)),
         ],
         flops=2 * channel * (hops + diags),
-        limit=32,
         name="extend",
     )
     return state[None, None], left[None, None], right[None, None], energy

time: 94.8 us -> 88.7 us (0.936); the launches traced: 93.1 us -> 88.2 us
  waiting for transfers between devices: 4.89 us -> 0.92 us
  Pallas kernels: 16 us -> 13.4 us
  starting transfers between devices: 35.5 us -> 37.3 us
    ppermute x4, waiting for transfers between devices: 3.53 us -> 0.01 us  [shards(): got_b = lax.ppermute(b, 'blk', down)]
    pallas_call x12 -> x13, Pallas kernels: 16 us -> 13.4 us  [call(): pl.pallas_call(kernel, in_specs=specs, out_specs=out_specs or [VMEM] * le...]
    ppermute x1, starting transfers between devices: 3.13 us -> 4.78 us  [shards(): from_left = lax.ppermute(kept, 'seg', seg_up)]
  transfers between devices with their start and end apart: 12 -> 12, of which waited for: 2 -> 1; matrix products, arithmetic and copies ran while one was open for 0% -> 0% of each run, Pallas kernels for 9% -> 10%
where the time goes in v3:
time: 88.7 us; the launch traced here: 88.2 us
  starting transfers between devices  37.3 us (42%)
  blocking collectives  34.5 us (39%)
  Pallas kernels  13.4 us (15%)
  between operations  2.19 us (2%)
  waiting for transfers between devices  0.92 us (1%)
    all_to_all x1, blocking collectives, shards(): sums = lax.all_to_all(sums, 'blk', 0, 0, tiled=True)  34.5 us
    pallas_call x13, Pallas kernels, call(): pl.pallas_call(kernel, in_specs=specs, out_specs=out_specs or [VMEM] * le...  13.4 us
    ppermute x3, starting transfers between devices, shards(): got_a = lax.ppermute(a, 'blk', up)  12.7 us
    ppermute x4, starting transfers between devices, shards(): got_b = lax.ppermute(b, 'blk', down)  5.17 us
    ppermute x1, starting transfers between devices, shards(): xl = lax.ppermute(lax.optimization_barrier((clt, b))[0], 'seg', seg_up)  4.9 us
    ppermute x1, starting transfers between devices, shards(): from_left = lax.ppermute(kept, 'seg', seg_up)  4.78 us
    ppermute x1, starting transfers between devices, shards(): below0 = lax.ppermute(own, 'blk', up)  4.03 us
    ppermute x1, starting transfers between devices, shards(): xr = lax.ppermute(lax.optimization_barrier((cr, b))[0], 'seg', seg_down)  3.45 us
  transfers between devices with their start and end apart: 12, of which 1 were waited for; matrix products, arithmetic and copies ran while one was open for 0% of the time, Pallas kernels for 10%

profile of v3, /device:TPU:1, one launch (start us, length us, event | category | flops | bytes accessed | tf_op | source)
XLA Modules:
  0.0 88.2 jit_solution(4650876052209707901)
XLA Ops:
  1.3 1.8 %load.1 = (f32[136,128]{1,0:T(8,128)S(1)}, f32[18,128,128]{2,1,0:T(8,128)S(1)}, f32[18,128,128]{2,1,0:T(8,128)S(1)}) custom-call(s32[1,1]{1,0:T(1,128)S(6)} %copy.12.size_ref, f32[128,128]{1,0:T(8,128)} %bitcast.18, f32[2,128,128]{2,1,0:T(8,128)} %bitcast.16, f32[16,128,128]{2,1,0:T(8,128)} %bitcast.14, f32[2,128,128]{2,1,0:T(8,128)} %bitcast.17, ...), custom_call_target="tpu_custom_call" | custom-call | bytes 4853764 | tf_op jit(solution)/shard_map/load/pallas_call | solution.py:214
  3.0 4.0 %collective-permute-start = (f32[136,128]{1,0:T(8,128)S(1)}, f32[136,128]{1,0:T(8,128)S(1)}, u32[]{:S(2)}, u32[]{:S(2)}) collective-permute-start(f32[136,128]{1,0:T(8,128)S(1)} %get-tuple-element.31.own_ref), channel_id=1, source_target_pairs={{0,1},{1,2},{2,3},{3,4},{4,5},{5,6},{6,7},{7,8},{8,9},{9,10},{10,1... | collective-permute-start | bytes 208904 | tf_op jit(solution)/shard_map/ppermute | solution.py:255
  7.1 1.1 %first_adjoint.1 = (bf16[2048,256]{1,0:T(8,128)(2,1)S(1)}, bf16[2048,256]{1,0:T(8,128)(2,1)S(1)}, bf16[256,256]{1,0:T(8,128)(2,1)S(1)}, bf16[256,256]{1,0:T(8,12...) custom-call(f32[136,128]{1,0:T(8,128)S(1)} %get-tuple-element.31.own_ref, ...), custom_call_target="tpu_custom_call" | custom-call | flops 10737418240 | bytes 6033408 | tf_op jit(solution)/shard_map/first_adjoint/pallas_call | solution.py:214
  8.2 1.3 %collective-permute-start.1 = (f32[128,128]{1,0:T(8,128)S(1)}, f32[128,128]{1,0:T(8,128)S(1)}, u32[]{:S(2)}, u32[]{:S(2)}) collective-permute-start(f32[128,128]{1,0:T(8,128)S(1)} %get-tuple-element.38.b_ref), channel_id=1, source_target_pairs={{1,0},{2,1},{3,2},{4,3},{5,4},{6,5},{7,6},{8,7},{9,8},{10,9},{11,1... | collective-permute-start | bytes 196616 | tf_op jit(solution)/shard_map/ppermute | solution.py:264
  10.1 0.0 collective-permute-done.below_ref
  10.1 1.0 %apply0.1.a_ref = f32[128,128]{1,0:T(8,128)S(1)} custom-call(f32[136,128]{1,0:T(8,128)S(1)} %get-tuple-element.31.own_ref, f32[136,128]{1,0:T(8,128)S(1)} %collective-permute-done.below_ref, bf16[2048,256]{1,0:T(8,128)(2,1)S(1)} %get-tuple-element.34.lt_ref, bf16[2048,256]{1,0:T(8,128)(2,1)S(1)} %get-tuple-element.35.rc_ref, ...), custom_call_target="tpu_custom_call" | custom-call | flops 12079595520 | bytes 2564096 | tf_op jit(solution)/shard_map/apply0/pallas_call | solution.py:214
  11.2 4.0 %collective-permute-start.2 = (f32[128,128]{1,0:T(8,128)S(1)}, f32[128,128]{1,0:T(8,128)S(1)}, u32[]{:S(2)}, u32[]{:S(2)}) collective-permute-start(f32[128,128]{1,0:T(8,128)S(1)} %apply0.1.a_ref), channel_id=1, source_target_pairs={{0,1},{1,2},{2,3},{3,4},{4,5},{5,6},{6,7},{7,8},{8,9},{9,10},{10,1... | collective-permute-start | bytes 196616 | tf_op jit(solution)/shard_map/ppermute | solution.py:268
  15.2 0.0 collective-permute-done.1.got_b_ref
  15.2 0.9 %adjoint1.1 = (f32[128,128]{1,0:T(8,128)S(1)}, f32[128,128]{1,0:T(8,128)S(1)}) custom-call(f32[136,128]{1,0:T(8,128)S(1)} %get-tuple-element.31.own_ref, f32[128,128]{1,0:T(8,128)S(1)} %apply0.1.a_ref, f32[128,128]{1,0:T(8,128)S(1)} %collective-permute-done.1.got_b_ref, bf16[2048,256]{1,0:T(8,128)(2,1)S(1)} %get-tuple-element.34.lt_ref, ...), custom_call_target="tpu_custom_call" | custom-call | flops 10737418240 | bytes 2428928 | tf_op jit(solution)/shard_map/adjoint1/pallas_call | solution.py:214
  16.1 1.3 %collective-permute-start.3 = (f32[128,128]{1,0:T(8,128)S(1)}, f32[128,128]{1,0:T(8,128)S(1)}, u32[]{:S(2)}, u32[]{:S(2)}) collective-permute-start(f32[128,128]{1,0:T(8,128)S(1)} %get-tuple-element.40.b_ref), channel_id=1, source_target_pairs={{1,0},{2,1},{3,2},{4,3},{5,4},{6,5},{7,6},{8,7},{9,8},{10,9},{11,1... | collective-permute-start | bytes 196616 | tf_op jit(solution)/shard_map/ppermute | solution.py:273
  17.4 0.0 collective-permute-done.2.got_a_ref
  17.4 1.0 %apply1.1.a_ref = f32[128,128]{1,0:T(8,128)S(1)} custom-call(f32[136,128]{1,0:T(8,128)S(1)} %get-tuple-element.31.own_ref, f32[136,128]{1,0:T(8,128)S(1)} %collective-permute-done.below_ref, f32[128,128]{1,0:T(8,128)S(1)} %get-tuple-element.39.v_ref, f32[128,128]{1,0:T(8,128)S(1)} %collective-permute-done.2.got_a_ref, ...), custom_call_target="tpu_custom_call" | custom-call | flops 12079595520 | bytes 2760704 | tf_op jit(solution)/shard_map/apply1/pallas_call | solution.py:214
  18.5 4.0 %collective-permute-start.4 = (f32[128,128]{1,0:T(8,128)S(1)}, f32[128,128]{1,0:T(8,128)S(1)}, u32[]{:S(2)}, u32[]{:S(2)}) collective-permute-start(f32[128,128]{1,0:T(8,128)S(1)} %apply1.1.a_ref), channel_id=1, source_target_pairs={{0,1},{1,2},{2,3},{3,4},{4,5},{5,6},{6,7},{7,8},{8,9},{9,10},{10,1... | collective-permute-start | bytes 196616 | tf_op jit(solution)/shard_map/ppermute | solution.py:268
  22.5 0.0 collective-permute-done.3.got_b_ref
  22.5 0.9 %adjoint2.1 = (f32[128,128]{1,0:T(8,128)S(1)}, f32[128,128]{1,0:T(8,128)S(1)}) custom-call(f32[136,128]{1,0:T(8,128)S(1)} %get-tuple-element.31.own_ref, f32[128,128]{1,0:T(8,128)S(1)} %apply1.1.a_ref, f32[128,128]{1,0:T(8,128)S(1)} %collective-permute-done.3.got_b_ref, bf16[2048,256]{1,0:T(8,128)(2,1)S(1)} %get-tuple-element.34.lt_ref, ...), custom_call_target="tpu_custom_call" | custom-call | flops 10737418240 | bytes 2428928 | tf_op jit(solution)/shard_map/adjoint2/pallas_call | solution.py:214
  23.4 1.3 %collective-permute-start.5 = (f32[128,128]{1,0:T(8,128)S(1)}, f32[128,128]{1,0:T(8,128)S(1)}, u32[]{:S(2)}, u32[]{:S(2)}) collective-permute-start(f32[128,128]{1,0:T(8,128)S(1)} %get-tuple-element.42.b_ref), channel_id=1, source_target_pairs={{1,0},{2,1},{3,2},{4,3},{5,4},{6,5},{7,6},{8,7},{9,8},{10,9},{11,1... | collective-permute-start | bytes 196616 | tf_op jit(solution)/shard_map/ppermute | solution.py:273
  24.7 0.0 collective-permute-done.4.got_a_ref
  24.7 1.0 %apply2.1.a_ref = f32[128,128]{1,0:T(8,128)S(1)} custom-call(f32[136,128]{1,0:T(8,128)S(1)} %get-tuple-element.31.own_ref, f32[136,128]{1,0:T(8,128)S(1)} %collective-permute-done.below_ref, f32[128,128]{1,0:T(8,128)S(1)} %get-tuple-element.41.v_ref, f32[128,128]{1,0:T(8,128)S(1)} %collective-permute-done.4.got_a_ref, ...), custom_call_target="tpu_custom_call" | custom-call | flops 12079595520 | bytes 2760704 | tf_op jit(solution)/shard_map/apply2/pallas_call | solution.py:214
  25.8 4.7 %collective-permute-start.6 = (f32[128,128]{1,0:T(8,128)S(1)}, f32[128,128]{1,0:T(8,128)S(1)}, u32[]{:S(2)}, u32[]{:S(2)}) collective-permute-start(f32[128,128]{1,0:T(8,128)S(1)} %apply2.1.a_ref), channel_id=1, source_target_pairs={{0,1},{1,2},{2,3},{3,4},{4,5},{5,6},{6,7},{7,8},{8,9},{9,10},{10,1... | collective-permute-start | bytes 196616 | tf_op jit(solution)/shard_map/ppermute | solution.py:268
  30.5 0.0 collective-permute-done.5.got_b_ref
  30.5 0.9 %adjoint3.1 = (f32[128,128]{1,0:T(8,128)S(1)}, f32[128,128]{1,0:T(8,128)S(1)}) custom-call(f32[136,128]{1,0:T(8,128)S(1)} %get-tuple-element.31.own_ref, f32[128,128]{1,0:T(8,128)S(1)} %apply2.1.a_ref, f32[128,128]{1,0:T(8,128)S(1)} %collective-permute-done.5.got_b_ref, bf16[2048,256]{1,0:T(8,128)(2,1)S(1)} %get-tuple-element.34.lt_ref, ...), custom_call_target="tpu_custom_call" | custom-call | flops 10737418240 | bytes 2428928 | tf_op jit(solution)/shard_map/adjoint3/pallas_call | solution.py:214
  31.5 1.3 %collective-permute-start.7 = (f32[128,128]{1,0:T(8,128)S(1)}, f32[128,128]{1,0:T(8,128)S(1)}, u32[]{:S(2)}, u32[]{:S(2)}) collective-permute-start(f32[128,128]{1,0:T(8,128)S(1)} %get-tuple-element.44), channel_id=1, source_target_pairs={{1,0},{2,1},{3,2},{4,3},{5,4},{6,5},{7,6},{8,7},{9,8},{10,9},{11,1... | collective-permute-start | bytes 196616 | tf_op jit(solution)/shard_map/ppermute | solution.py:273
  32.8 4.9 %collective-permute-start.10 = (f32[18,128,128]{2,1,0:T(8,128)S(1)}, f32[18,128,128]{2,1,0:T(8,128)S(1)}, u32[]{:S(2)}, u32[]{:S(2)}) collective-permute-start(f32[18,128,128]{2,1,0:T(8,128)S(1)} %get-tuple-element.50), channel_id=1, source_target_pairs={{0,64},{64,128},{128,192},{192,256},{256,320},{320,384},{384,448},... | collective-permute-start | bytes 3538952 | tf_op jit(solution)/shard_map/ppermute | solution.py:275
  37.7 3.5 %collective-permute-start.11 = (f32[18,128,128]{2,1,0:T(8,128)S(1)}, f32[18,128,128]{2,1,0:T(8,128)S(1)}, u32[]{:S(2)}, u32[]{:S(2)}) collective-permute-start(f32[18,128,128]{2,1,0:T(8,128)S(1)} %get-tuple-element.51.cr_ref), channel_id=1, source_target_pairs={{64,0},{128,64},{192,128},{256,192},{320,256},{384,320},{448,384},... | collective-permute-start | bytes 3538952 | tf_op jit(solution)/shard_map/ppermute | solution.py:276
  41.2 0.0 collective-permute-done.6.got_a_ref
  41.2 1.0 %apply3.1.part_ref = f32[128,128]{1,0:T(8,128)S(1)} custom-call(f32[136,128]{1,0:T(8,128)S(1)} %get-tuple-element.31.own_ref, f32[136,128]{1,0:T(8,128)S(1)} %collective-permute-done.below_ref, f32[128,128]{1,0:T(8,128)S(1)} %get-tuple-element.43.v_ref, f32[128,128]{1,0:T(8,128)S(1)} %collective-permute-done.6.got_a_ref, ...), custom_call_target="tpu_custom_call" | custom-call | flops 12079595520 | bytes 2760704 | tf_op jit(solution)/shard_map/apply3/pallas_call | solution.py:214
  42.2 0.0 collective-permute-done.7.got_b_ref
  42.2 0.1 finish.1
  42.4 34.5 %all_to_all.11 = f32[64,1,128]{2,1,0:T(1,128)S(1)} all-to-all(f32[64,1,128]{2,1,0:T(1,128)S(1)} %bitcast.13), channel_id=1, replica_groups=mesh['seg'=8,'blk'=64] {'blk'}, dimensions={0} | all-to-all | bytes 65536 | tf_op jit(solution)/shard_map/all_to_all | solution.py:287
  76.8 0.6 normalise.1
  77.5 2.2 %collective-permute-start.9 = (f32[128,128]{1,0:T(8,128)S(1)}, f32[128,128]{1,0:T(8,128)S(1)}, u32[]{:S(2)}, u32[]{:S(2)}) collective-permute-start(f32[128,128]{1,0:T(8,128)S(1)} %get-tuple-element.47), channel_id=1, source_target_pairs={{64,0},{128,64},{192,128},{256,192},{320,256},{384,320},{448,384},... | collective-permute-start | bytes 196616 | tf_op jit(solution)/shard_map/ppermute | solution.py:297
  79.7 4.8 %collective-permute-start.8 = (f32[128,128]{1,0:T(8,128)S(1)}, f32[128,128]{1,0:T(8,128)S(1)}, u32[]{:S(2)}, u32[]{:S(2)}) collective-permute-start(f32[128,128]{1,0:T(8,128)S(1)} %get-tuple-element.47), channel_id=1, source_target_pairs={{0,64},{64,128},{128,192},{192,256},{256,320},{320,384},{384,448},... | collective-permute-start | bytes 196616 | tf_op jit(solution)/shard_map/ppermute | solution.py:296
  84.5 0.0 collective-permute-done.10.xl_ref
  84.5 0.0 collective-permute-done.11.xr_ref
  84.5 0.4 parts.1
  84.9 0.0 collective-permute-done.9.right_ref
  84.9 0.9 %collective-permute-done.8.left_ref = f32[128,128]{1,0:T(8,128)S(1)} collective-permute-done((f32[128,128]{1,0:T(8,128)S(1)}, f32[128,128]{1,0:T(8,128)S(1)}, u32[]{:S(2)}, u32[]{:S(2)}) %collective-permute-start.8) | collective-permute-done | bytes 65568 | tf_op jit(solution)/shard_map/ppermute | solution.py:296
  85.8 2.4 %extend.1 = (f32[128,128]{1,0:T(8,128)}, f32[18,128,128]{2,1,0:T(8,128)}, f32[18,128,128]{2,1,0:T(8,128)}) custom-call(f32[128,128]{1,0:T(8,128)S(1)} %collective-permute-done.8.left_ref, f32[128,128]{1,0:T(8,128)S(1)} %collective-permute-done.9.right_ref, f32[128,128]{1,0:T(8,128)S(1)} %get-tuple-element.48.state_ref, ...), custom_call_target="tpu_custom_call" | custom-call | flops 24159191040 | bytes 4980736 | tf_op jit(solution)/shard_map/extend/pallas_call | solution.py:214
Async XLA Ops:
  3.0 7.1 %collective-permute-start = (f32[136,128]{1,0:T(8,128)S(1)}, f32[136,128]{1,0:T(8,128)S(1)}, u32[]{:S(2)}, u32[]{:S(2)}) collective-permute-start(f32[136,128]{1,0:T(8,128)S(1)} %get-tuple-element.31.own_ref), channel_id=1, source_target_pairs={{0,1},{1,2},{2,3},{3,4},{4,5},{5,6},{6,7},{7,8},{8,9},{9,10},{10,1... | collective-permute-start | bytes 208904 | tf_op jit(solution)/shard_map/ppermute | solution.py:255
  8.2 7.0 %collective-permute-start.1 = (f32[128,128]{1,0:T(8,128)S(1)}, f32[128,128]{1,0:T(8,128)S(1)}, u32[]{:S(2)}, u32[]{:S(2)}) collective-permute-start(f32[128,128]{1,0:T(8,128)S(1)} %get-tuple-element.38.b_ref), channel_id=1, source_target_pairs={{1,0},{2,1},{3,2},{4,3},{5,4},{6,5},{7,6},{8,7},{9,8},{10,9},{11,1... | collective-permute-start | bytes 196616 | tf_op jit(solution)/shard_map/ppermute | solution.py:264
  11.2 6.3 %collective-permute-start.2 = (f32[128,128]{1,0:T(8,128)S(1)}, f32[128,128]{1,0:T(8,128)S(1)}, u32[]{:S(2)}, u32[]{:S(2)}) collective-permute-start(f32[128,128]{1,0:T(8,128)S(1)} %apply0.1.a_ref), channel_id=1, source_target_pairs={{0,1},{1,2},{2,3},{3,4},{4,5},{5,6},{6,7},{7,8},{8,9},{9,10},{10,1... | collective-permute-start | bytes 196616 | tf_op jit(solution)/shard_map/ppermute | solution.py:268
  16.1 6.4 %collective-permute-start.3 = (f32[128,128]{1,0:T(8,128)S(1)}, f32[128,128]{1,0:T(8,128)S(1)}, u32[]{:S(2)}, u32[]{:S(2)}) collective-permute-start(f32[128,128]{1,0:T(8,128)S(1)} %get-tuple-element.40.b_ref), channel_id=1, source_target_pairs={{1,0},{2,1},{3,2},{4,3},{5,4},{6,5},{7,6},{8,7},{9,8},{10,9},{11,1... | collective-permute-start | bytes 196616 | tf_op jit(solution)/shard_map/ppermute | solution.py:273
  18.5 6.3 %collective-permute-start.4 = (f32[128,128]{1,0:T(8,128)S(1)}, f32[128,128]{1,0:T(8,128)S(1)}, u32[]{:S(2)}, u32[]{:S(2)}) collective-permute-start(f32[128,128]{1,0:T(8,128)S(1)} %apply1.1.a_ref), channel_id=1, source_target_pairs={{0,1},{1,2},{2,3},{3,4},{4,5},{5,6},{6,7},{7,8},{8,9},{9,10},{10,1... | collective-permute-start | bytes 196616 | tf_op jit(solution)/shard_map/ppermute | solution.py:268
  23.4 7.1 %collective-permute-start.5 = (f32[128,128]{1,0:T(8,128)S(1)}, f32[128,128]{1,0:T(8,128)S(1)}, u32[]{:S(2)}, u32[]{:S(2)}) collective-permute-start(f32[128,128]{1,0:T(8,128)S(1)} %get-tuple-element.42.b_ref), channel_id=1, source_target_pairs={{1,0},{2,1},{3,2},{4,3},{5,4},{6,5},{7,6},{8,7},{9,8},{10,9},{11,1... | collective-permute-start | bytes 196616 | tf_op jit(solution)/shard_map/ppermute | solution.py:273
  25.8 15.4 %collective-permute-start.6 = (f32[128,128]{1,0:T(8,128)S(1)}, f32[128,128]{1,0:T(8,128)S(1)}, u32[]{:S(2)}, u32[]{:S(2)}) collective-permute-start(f32[128,128]{1,0:T(8,128)S(1)} %apply2.1.a_ref), channel_id=1, source_target_pairs={{0,1},{1,2},{2,3},{3,4},{4,5},{5,6},{6,7},{7,8},{8,9},{9,10},{10,1... | collective-permute-start | bytes 196616 | tf_op jit(solution)/shard_map/ppermute | solution.py:268
  31.5 10.7 %collective-permute-start.7 = (f32[128,128]{1,0:T(8,128)S(1)}, f32[128,128]{1,0:T(8,128)S(1)}, u32[]{:S(2)}, u32[]{:S(2)}) collective-permute-start(f32[128,128]{1,0:T(8,128)S(1)} %get-tuple-element.44), channel_id=1, source_target_pairs={{1,0},{2,1},{3,2},{4,3},{5,4},{6,5},{7,6},{8,7},{9,8},{10,9},{11,1... | collective-permute-start | bytes 196616 | tf_op jit(solution)/shard_map/ppermute | solution.py:273
  32.8 51.7 %collective-permute-start.10 = (f32[18,128,128]{2,1,0:T(8,128)S(1)}, f32[18,128,128]{2,1,0:T(8,128)S(1)}, u32[]{:S(2)}, u32[]{:S(2)}) collective-permute-start(f32[18,128,128]{2,1,0:T(8,128)S(1)} %get-tuple-element.50), channel_id=1, source_target_pairs={{0,64},{64,128},{128,192},{192,256},{256,320},{320,384},{384,448},... | collective-permute-start | bytes 3538952 | tf_op jit(solution)/shard_map/ppermute | solution.py:275
  37.7 46.8 %collective-permute-start.11 = (f32[18,128,128]{2,1,0:T(8,128)S(1)}, f32[18,128,128]{2,1,0:T(8,128)S(1)}, u32[]{:S(2)}, u32[]{:S(2)}) collective-permute-start(f32[18,128,128]{2,1,0:T(8,128)S(1)} %get-tuple-element.51.cr_ref), channel_id=1, source_target_pairs={{64,0},{128,64},{192,128},{256,192},{320,256},{384,320},{448,384},... | collective-permute-start | bytes 3538952 | tf_op jit(solution)/shard_map/ppermute | solution.py:276
  77.5 7.4 %collective-permute-start.9 = (f32[128,128]{1,0:T(8,128)S(1)}, f32[128,128]{1,0:T(8,128)S(1)}, u32[]{:S(2)}, u32[]{:S(2)}) collective-permute-start(f32[128,128]{1,0:T(8,128)S(1)} %get-tuple-element.47), channel_id=1, source_target_pairs={{64,0},{128,64},{192,128},{256,192},{320,256},{384,320},{448,384},... | collective-permute-start | bytes 196616 | tf_op jit(solution)/shard_map/ppermute | solution.py:297
  79.7 6.1 %collective-permute-start.8 = (f32[128,128]{1,0:T(8,128)S(1)}, f32[128,128]{1,0:T(8,128)S(1)}, u32[]{:S(2)}, u32[]{:S(2)}) collective-permute-start(f32[128,128]{1,0:T(8,128)S(1)} %get-tuple-element.47), channel_id=1, source_target_pairs={{0,64},{64,128},{128,192},{192,256},{256,320},{320,384},{384,448},... | collective-permute-start | bytes 196616 | tf_op jit(solution)/shard_map/ppermute | solution.py:296

commit v4 on v3

--- a/solution.py
+++ b/solution.py
@@ -12,7 +12,7 @@
 SHIFT = 20.0
 BOND = 6144.0
 PARTS = 4
-CHUNKS = 3
+CHUNKS = 9
 f32 = jnp.float32
 bf16 = jnp.bfloat16
 VMEM = pl.BlockSpec(memory_space=pltpu.VMEM)
@@ -81,38 +81,60 @@
     out_ref[pl.ds(h * n, n), n:] = low
 
 
-def load(size_ref, x_ref, dl_ref, hl_ref, dr_ref, hr_ref, own_ref, cl_ref, cr_ref, x, sems):
+def odd_segment():
+    return lax.rem(lax.axis_index("seg"), 2) == 1
+
+
+def load(size_ref, x_ref, dl_ref, hl_ref, dr_ref, hr_ref, own_ref, m0_ref, m1_ref, x, sems):
     n = x.shape[0]
     diags, hops = dl_ref.shape[0], hl_ref.shape[0]
     first = pltpu.make_async_copy(x_ref, x, sems.at[0])
     first.start()
-    rest = [
-        pltpu.make_async_copy(dl_ref, cl_ref.at[pl.ds(0, diags)], sems.at[1]),
-        pltpu.make_async_copy(dr_ref, cr_ref.at[pl.ds(0, diags)], sems.at[2]),
-    ]
     part = hops // PARTS
-    for i in range(PARTS):
-        source, target = pl.ds(i * part, part), pl.ds(diags + i * part, part)
-        rest.append(pltpu.make_async_copy(hl_ref.at[source], cl_ref.at[target], sems.at[3 + 2 * i]))
-        rest.append(pltpu.make_async_copy(hr_ref.at[source], cr_ref.at[target], sems.at[4 + 2 * i]))
-    for copy in rest:
-        copy.start()
+    left, right = (dl_ref, hl_ref), (dr_ref, hr_ref)
+
+    def loads(sides):
+        copies = []
+        for side, ((diag, hop), out) in enumerate(zip(sides, (m0_ref, m1_ref))):
+            sem = 1 + side * (1 + PARTS)
+            copies.append(pltpu.make_async_copy(diag, out.at[pl.ds(0, diags)], sems.at[sem]))
+            for i in range(PARTS):
+                source, target = pl.ds(i * part, part), pl.ds(diags + i * part, part)
+                copies.append(pltpu.make_async_copy(hop.at[source], out.at[target], sems.at[sem + 1 + i]))
+        return copies
+
+    odd = odd_segment()
+
+    @pl.when(odd)
+    def _():
+        for copy in loads((right, left)):
+            copy.start()
+
+    @pl.when(jnp.logical_not(odd))
+    def _():
+        for copy in loads((left, right)):
+            copy.start()
+
     first.wait()
     live = jnp.full((1, n), size_ref[0, 0].astype(f32), f32)
     own_ref[:n, :] = where(square_mask(live), x[...])
     own_ref[n:, :] = jnp.broadcast_to(live, (8, n))
-    for copy in rest:
+    for copy in loads((left, right)):
         copy.wait()
 
 
-def first_adjoint(own_ref, cl_ref, cr_ref, lt_ref, rc_ref, dlt_ref, drc_ref, clt_ref, b_ref):
+def first_adjoint(own_ref, m0_ref, m1_ref, lt_ref, rc_ref, dlt_ref, drc_ref, b_ref):
     n = own_ref.shape[1]
     diags = dlt_ref.shape[0] // n
-    for c in range(cl_ref.shape[0]):
-        flip = cl_ref[c].T
-        clt_ref[c] = flip
-        put_parts(dlt_ref if c < diags else lt_ref, c if c < diags else c - diags, n, flip)
-        put_parts(drc_ref if c < diags else rc_ref, c if c < diags else c - diags, n, cr_ref[c])
+
+    def fill(left, right):
+        for c in range(left.shape[0]):
+            put_parts(dlt_ref if c < diags else lt_ref, c if c < diags else c - diags, n, left[c].T)
+            put_parts(drc_ref if c < diags else rc_ref, c if c < diags else c - diags, n, right[c])
+
+    odd = odd_segment()
+    pl.when(odd)(lambda: fill(m1_ref, m0_ref))
+    pl.when(jnp.logical_not(odd))(lambda: fill(m0_ref, m1_ref))
     b_ref[...] = sandwich(lt_ref, rc_ref, own_ref[:n, :])
 
 
@@ -163,52 +185,72 @@
     sums_ref[...] = jnp.broadcast_to(row, sums_ref.shape)
 
 
-def normalise(v4_ref, sums_ref, state_ref, kept_ref, energy_ref):
+def lane_of(row, j):
+    lane = lax.broadcasted_iota(jnp.int32, row.shape, 1)
+    return jnp.sum(jnp.where(lane == j, row, 0.0), axis=1, keepdims=True)
+
+
+def normalise(v4_ref, sums_ref, state_ref, kept_ref):
     n = v4_ref.shape[1]
     total = jnp.sum(sums_ref[...], axis=0, keepdims=True)
-    lane = lax.broadcasted_iota(jnp.int32, (1, n), 1)
-
-    def pick(j):
-        return jnp.sum(jnp.where(lane == j, total, 0.0), axis=1, keepdims=True)
-
-    state = v4_ref[:n, :] * jnp.sqrt(BOND * n / pick(0))
+    state = v4_ref[:n, :] * jnp.sqrt(BOND * n / lane_of(total, 0))
     state_ref[...] = state
     cols = lax.broadcasted_iota(jnp.int32, (n, n), 1).astype(f32)
     kept_ref[...] = where(cols < jnp.broadcast_to(v4_ref[n : n + 1, :], (n, n)), state)
-    energy_ref[0] = jnp.sum(pick(1) / pick(2))
-
-
-def parts(xl_ref, xr_ref, pl_ref, pr_ref):
-    n = xl_ref.shape[1]
-    for c in range(xl_ref.shape[0]):
-        put_parts(pl_ref, c, n, xl_ref[c])
-        put_parts(pr_ref, c, n, xr_ref[c])
-
-
-def extend(left_ref, right_ref, state_ref, pl_ref, pr_ref, new_ref, lo_ref, ro_ref, lo, ro, sems):
-    n = left_ref.shape[0]
-    channels = lo.shape[0]
-    scale = 1.0 / math.sqrt(n)
-    copies = [pltpu.make_async_copy(state_ref, new_ref, sems.at[0])]
-    copies[0].start()
-    sides = ((pl_ref, weight(left_ref[...]), lo, lo_ref), (pr_ref, weight(right_ref[...].T), ro, ro_ref))
+
+
+def parts(x0_ref, x1_ref, p0_ref, p1_ref):
+    n = x0_ref.shape[1]
+
+    def fill(left, left_out, right, right_out):
+        for c in range(left.shape[0]):
+            put_parts(left_out, c, n, left[c].T)
+            put_parts(right_out, c, n, right[c])
+
+    odd = odd_segment()
+    pl.when(odd)(lambda: fill(x0_ref, p0_ref, x1_ref, p1_ref))
+    pl.when(jnp.logical_not(odd))(lambda: fill(x1_ref, p1_ref, x0_ref, p0_ref))
+
+
+def extend(is_left, kept, p_ref, left_ref, right_ref, out, sems):
+    n = kept.shape[0]
+    channels = out.shape[0]
     step = channels // CHUNKS
+    w = weight(jnp.where(is_left, kept, kept.T))
+
+    def copy(target, i):
+        at = pl.ds(i * step, step)
+        return pltpu.make_async_copy(out.at[at], target.at[at], sems.at[i])
+
     for i in range(CHUNKS):
-        at = pl.ds(i * step, step)
-        for side, (x, w, out, out_ref) in enumerate(sides):
-            for c in range(i * step, (i + 1) * step, 2):
-                half = folded(dot(x[pl.ds(c * n, 2 * n), :], w))
-                flip = jnp.concatenate([half[:n].T, half[n:].T], 0)
-                y = folded(dot(jnp.concatenate(split(flip), 1), w)) * scale
-                out[c] = y[:n]
-                out[c + 1] = y[n:]
-            copies.append(pltpu.make_async_copy(out.at[at], out_ref.at[at], sems.at[1 + 2 * i + side]))
-            copies[-1].start()
-    for copy in copies:
-        copy.wait()
-
-
-def call(kernel, args, specs, outs, out_specs=None, scratch=(), flops=0, limit=16, name=None):
+        for c in range(i * step, (i + 1) * step, 2):
+            half = folded(dot(p_ref[pl.ds(c * n, 2 * n), :], w))
+            flip = jnp.concatenate([half[:n].T, half[n:].T], 0)
+            y = folded(dot(jnp.concatenate(split(flip), 1), w)) * (1.0 / math.sqrt(n))
+            out[c] = y[:n]
+            out[c + 1] = y[n:]
+        pl.when(is_left)(copy(left_ref, i).start)
+        pl.when(jnp.logical_not(is_left))(copy(right_ref, i).start)
+    for i in range(CHUNKS):
+        copy(left_ref, i).wait()
+
+
+def extend_first(kept_ref, p_ref, left_ref, right_ref, out, sems):
+    extend(odd_segment(), kept_ref[...], p_ref, left_ref, right_ref, out, sems)
+
+
+def extend_second(
+    kept_ref, p_ref, state_ref, sums_ref, left_in, right_in, new_ref, left_ref, right_ref, energy_ref, out, sems, state_sem
+):
+    copy = pltpu.make_async_copy(state_ref, new_ref, state_sem)
+    copy.start()
+    total = jnp.sum(sums_ref[...], axis=0, keepdims=True)
+    energy_ref[0] = jnp.sum(lane_of(total, 1) / lane_of(total, 2))
+    extend(jnp.logical_not(odd_segment()), kept_ref[...], p_ref, left_ref, right_ref, out, sems)
+    copy.wait()
+
+
+def call(kernel, args, specs, outs, out_specs=None, scratch=(), flops=0, limit=16, aliases=None, name=None):
     moved = sum(math.prod(a.shape) * a.dtype.itemsize for a in (*args, *outs))
     args = [pltpu.with_memory_space_constraint(a, pltpu.HBM) if spec is HBM else a for a, spec in zip(args, specs)]
     return pl.pallas_call(
@@ -217,6 +259,7 @@
         out_specs=out_specs or [VMEM] * len(outs),
         out_shape=outs,
         scratch_shapes=list(scratch),
+        input_output_aliases=aliases or {},
         compiler_params=pltpu.CompilerParams(vmem_limit_bytes=limit << 20),
         cost_estimate=pl.CostEstimate(flops=flops, bytes_accessed=moved, transcendentals=0),
         name=name,
@@ -231,8 +274,9 @@
     blocks, segs = lax.axis_size("blk"), lax.axis_size("seg")
     up = [(i, i + 1) for i in range(blocks - 1)]
     down = [(i + 1, i) for i in range(blocks - 1)]
-    seg_up = [(i, i + 1) for i in range(segs - 1)]
-    seg_down = [(i + 1, i) for i in range(segs - 1)]
+    chip = [(i, i ^ 1) for i in range(segs)]
+    across = [(i, i + 1) for i in range(1, segs - 1, 2)]
+    across += [(target, source) for source, target in across]
     block = SDS((n, n), f32)
     message = SDS((n + 8, n), f32)
     hop_parts = SDS((hops * n, 2 * n), bf16)
@@ -240,7 +284,7 @@
     out = SDS((diags + hops, n, n), f32)
     channel = 20 * 8 * 2 * n**3
 
-    own, cl, cr = call(
+    own, m0, m1 = call(
         load,
         (sector_sizes, x0, dl, hl, dr, hr),
         [SMEM] + [HBM] * 5,
@@ -253,11 +297,11 @@
         name="load",
     )
     below0 = lax.ppermute(own, "blk", up)
-    lt, rc, dlt, drc, clt, b = call(
+    lt, rc, dlt, drc, b = call(
         first_adjoint,
-        (own, cl, cr),
+        (own, m0, m1),
         [VMEM] * 3,
-        [hop_parts, hop_parts, diag_parts, diag_parts, out, block],
+        [hop_parts, hop_parts, diag_parts, diag_parts, block],
         flops=channel * hops,
         name="first_adjoint",
     )
@@ -272,8 +316,8 @@
         )
         got_b = lax.ppermute(b, "blk", down)
         if k == ITERS - 1:
-            xl = lax.ppermute(lax.optimization_barrier((clt, b))[0], "seg", seg_up)
-            xr = lax.ppermute(lax.optimization_barrier((cr, b))[0], "seg", seg_down)
+            x1 = lax.ppermute(lax.optimization_barrier((m1, b))[0], "seg", across)
+            x0 = lax.ppermute(lax.optimization_barrier((m0, b))[0], "seg", chip)
         (a,) = call(
             functools.partial(later_apply, k == ITERS - 1),
             (own, below0, v, got_a, last_b, *ops),
@@ -285,31 +329,32 @@
     sums_block = SDS((blocks, n), f32)
     v4, sums = call(finish, (ranks, own, v, a, got_b), [SMEM] + [VMEM] * 4, [message, sums_block], name="finish")
     sums = lax.all_to_all(sums, "blk", 0, 0, tiled=True)
-    state, kept, energy = call(
-        normalise,
-        (v4, sums),
+    state, kept = call(normalise, (v4, sums), [VMEM] * 2, [block, block], name="normalise")
+    kept1 = lax.ppermute(kept, "seg", across)
+    kept0 = lax.ppermute(kept, "seg", chip)
+    all_parts = SDS(((diags + hops) * n, 2 * n), bf16)
+    p0, p1 = call(parts, (x0, x1), [VMEM] * 2, [all_parts, all_parts], flops=channel * hops, name="parts")
+    rooms = [pltpu.VMEM(out.shape, f32), pltpu.SemaphoreType.DMA((CHUNKS,))]
+    left, right = call(
+        extend_first,
+        (kept0, p0),
         [VMEM] * 2,
-        [block, block, SDS((1,), f32)],
-        out_specs=[VMEM, VMEM, SMEM],
-        name="normalise",
-    )
-    from_left = lax.ppermute(kept, "seg", seg_up)
-    from_right = lax.ppermute(kept, "seg", seg_down)
-    all_parts = SDS(((diags + hops) * n, 2 * n), bf16)
-    xl, xr = call(parts, (xl, xr), [VMEM] * 2, [all_parts, all_parts], flops=channel * hops, name="parts")
-    state, left, right = call(
-        extend,
-        (from_left, from_right, state, xl, xr),
-        [VMEM] * 5,
-        [block, out, out],
-        out_specs=[ANY] * 3,
-        scratch=[
-            pltpu.VMEM(out.shape, f32),
-            pltpu.VMEM(out.shape, f32),
-            pltpu.SemaphoreType.DMA((1 + 2 * CHUNKS,)),
-        ],
-        flops=2 * channel * (hops + diags),
-        name="extend",
+        [out, out],
+        out_specs=[ANY] * 2,
+        scratch=rooms,
+        flops=channel * (hops + diags),
+        name="extend_first",
+    )
+    state, left, right, energy = call(
+        extend_second,
+        (kept1, p1, state, sums, left, right),
+        [VMEM] * 4 + [ANY] * 2,
+        [block, out, out, SDS((1,), f32)],
+        out_specs=[ANY] * 3 + [SMEM],
+        scratch=[*rooms, pltpu.SemaphoreType.DMA],
+        flops=channel * (hops + diags),
+        aliases={4: 1, 5: 2},
+        name="extend_second",
     )
     return state[None, None], left[None, None], right[None, None], energy
 

time: 88.7 us -> 88.5 us (level)
  Pallas kernels: 13.4 us -> 15.1 us
  waiting for transfers between devices: 0.92 us -> 0.03 us
    pallas_call x13 -> x14, Pallas kernels: 13.4 us -> 15.1 us  [call(): pl.pallas_call(kernel, in_specs=specs, out_specs=out_specs or [VMEM] * le...]
  transfers between devices with their start and end apart: 12 -> 12, of which waited for: 1 -> 0; matrix products, arithmetic and copies ran while one was open for 0% -> 0% of each run, Pallas kernels for 10% -> 13%
where the time goes in v4:
time: 88.5 us; the launch traced here: 88 us
  starting transfers between devices  36.8 us (42%)
  blocking collectives  33.9 us (38%)
  Pallas kernels  15.1 us (17%)
  between operations  2.21 us (2%)
    all_to_all x1, blocking collectives, shards(): sums = lax.all_to_all(sums, 'blk', 0, 0, tiled=True)  33.9 us
    pallas_call x14, Pallas kernels, call(): pl.pallas_call(kernel, in_specs=specs, out_specs=out_specs or [VMEM] * le...  15.1 us
    ppermute x3, starting transfers between devices, shards(): got_a = lax.ppermute(a, 'blk', up)  12.7 us
    ppermute x1, starting transfers between devices, shards(): x0 = lax.ppermute(lax.optimization_barrier((m0, b))[0], 'seg', chip)  6.99 us
    ppermute x4, starting transfers between devices, shards(): got_b = lax.ppermute(b, 'blk', down)  5.17 us
    ppermute x1, starting transfers between devices, shards(): below0 = lax.ppermute(own, 'blk', up)  4.03 us
    ppermute x1, starting transfers between devices, shards(): kept1 = lax.ppermute(kept, 'seg', across)  3.74 us
    ppermute x1, starting transfers between devices, shards(): kept0 = lax.ppermute(kept, 'seg', chip)  2.21 us
  transfers between devices with their start and end apart: 12, of which 0 were waited for; matrix products, arithmetic and copies ran while one was open for 0% of the time, Pallas kernels for 13%

profile of v4, /device:TPU:1, one launch (start us, length us, event | category | flops | bytes accessed | tf_op | source)
XLA Modules:
  0.0 88.0 jit_solution(4995595358362379040)
XLA Ops:
  1.3 1.7 %load.1 = (f32[136,128]{1,0:T(8,128)S(1)}, f32[18,128,128]{2,1,0:T(8,128)S(1)}, f32[18,128,128]{2,1,0:T(8,128)S(1)}) custom-call(s32[1,1]{1,0:T(1,128)S(6)} %copy.16.size_ref, f32[128,128]{1,0:T(8,128)} %bitcast.19, f32[2,128,128]{2,1,0:T(8,128)} %bitcast.17, f32[16,128,128]{2,1,0:T(8,128)} %bitcast.15, f32[2,128,128]{2,1,0:T(8,128)} %bitcast.18, ...), custom_call_target="tpu_custom_call" | custom-call | bytes 4853764 | tf_op jit(solution)/shard_map/load/pallas_call | solution.py:256
  3.0 4.0 %collective-permute-start = (f32[136,128]{1,0:T(8,128)S(1)}, f32[136,128]{1,0:T(8,128)S(1)}, u32[]{:S(2)}, u32[]{:S(2)}) collective-permute-start(f32[136,128]{1,0:T(8,128)S(1)} %get-tuple-element.32.own_ref), channel_id=1, source_target_pairs={{0,1},{1,2},{2,3},{3,4},{4,5},{5,6},{6,7},{7,8},{8,9},{9,10},{10,1... | collective-permute-start | bytes 208904 | tf_op jit(solution)/shard_map/ppermute | solution.py:299
  7.1 1.5 %first_adjoint.1 = (bf16[2048,256]{1,0:T(8,128)(2,1)S(1)}, bf16[2048,256]{1,0:T(8,128)(2,1)S(1)}, bf16[256,256]{1,0:T(8,128)(2,1)S(1)}, bf16[256,256]{1,0:T(8,128)(2,1)S(1)}, f32[128,128]{1,0:T(8,128)S(1)}) custom-call(f32[136,128]{1,0:T(8,128)S(1)} %get-tuple-element.32.own_ref, f32[18,128,128]{2,1,0:T(8,128)S(1)} %get-tuple-element.49.m0_ref, ...), custom_call_target="tpu_custom_call" | custom-call | flops 10737418240 | bytes 4853760 | tf_op jit(solution)/shard_map/first_adjoint/pallas_call | solution.py:256
  8.6 1.3 %collective-permute-start.1 = (f32[128,128]{1,0:T(8,128)S(1)}, f32[128,128]{1,0:T(8,128)S(1)}, u32[]{:S(2)}, u32[]{:S(2)}) collective-permute-start(f32[128,128]{1,0:T(8,128)S(1)} %get-tuple-element.39.b_ref), channel_id=1, source_target_pairs={{1,0},{2,1},{3,2},{4,3},{5,4},{6,5},{7,6},{8,7},{9,8},{10,9},{11,1... | collective-permute-start | bytes 196616 | tf_op jit(solution)/shard_map/ppermute | solution.py:308
  10.5 0.0 collective-permute-done.below_ref
  10.5 1.0 %apply0.1.a_ref = f32[128,128]{1,0:T(8,128)S(1)} custom-call(f32[136,128]{1,0:T(8,128)S(1)} %get-tuple-element.32.own_ref, f32[136,128]{1,0:T(8,128)S(1)} %collective-permute-done.below_ref, bf16[2048,256]{1,0:T(8,128)(2,1)S(1)} %get-tuple-element.35.lt_ref, bf16[2048,256]{1,0:T(8,128)(2,1)S(1)} %get-tuple-element.36.rc_ref, ...), custom_call_target="tpu_custom_call" | custom-call | flops 12079595520 | bytes 2564096 | tf_op jit(solution)/shard_map/apply0/pallas_call | solution.py:256
  11.6 4.0 %collective-permute-start.2 = (f32[128,128]{1,0:T(8,128)S(1)}, f32[128,128]{1,0:T(8,128)S(1)}, u32[]{:S(2)}, u32[]{:S(2)}) collective-permute-start(f32[128,128]{1,0:T(8,128)S(1)} %apply0.1.a_ref), channel_id=1, source_target_pairs={{0,1},{1,2},{2,3},{3,4},{4,5},{5,6},{6,7},{7,8},{8,9},{9,10},{10,1... | collective-permute-start | bytes 196616 | tf_op jit(solution)/shard_map/ppermute | solution.py:312
  15.6 0.0 collective-permute-done.1.got_b_ref
  15.6 0.9 %adjoint1.1 = (f32[128,128]{1,0:T(8,128)S(1)}, f32[128,128]{1,0:T(8,128)S(1)}) custom-call(f32[136,128]{1,0:T(8,128)S(1)} %get-tuple-element.32.own_ref, f32[128,128]{1,0:T(8,128)S(1)} %apply0.1.a_ref, f32[128,128]{1,0:T(8,128)S(1)} %collective-permute-done.1.got_b_ref, bf16[2048,256]{1,0:T(8,128)(2,1)S(1)} %get-tuple-element.35.lt_ref, ...), custom_call_target="tpu_custom_call" | custom-call | flops 10737418240 | bytes 2428928 | tf_op jit(solution)/shard_map/adjoint1/pallas_call | solution.py:256
  16.5 1.3 %collective-permute-start.3 = (f32[128,128]{1,0:T(8,128)S(1)}, f32[128,128]{1,0:T(8,128)S(1)}, u32[]{:S(2)}, u32[]{:S(2)}) collective-permute-start(f32[128,128]{1,0:T(8,128)S(1)} %get-tuple-element.41.b_ref), channel_id=1, source_target_pairs={{1,0},{2,1},{3,2},{4,3},{5,4},{6,5},{7,6},{8,7},{9,8},{10,9},{11,1... | collective-permute-start | bytes 196616 | tf_op jit(solution)/shard_map/ppermute | solution.py:317
  17.8 0.0 collective-permute-done.2.got_a_ref
  17.8 1.0 %apply1.1.a_ref = f32[128,128]{1,0:T(8,128)S(1)} custom-call(f32[136,128]{1,0:T(8,128)S(1)} %get-tuple-element.32.own_ref, f32[136,128]{1,0:T(8,128)S(1)} %collective-permute-done.below_ref, f32[128,128]{1,0:T(8,128)S(1)} %get-tuple-element.40.v_ref, f32[128,128]{1,0:T(8,128)S(1)} %collective-permute-done.2.got_a_ref, ...), custom_call_target="tpu_custom_call" | custom-call | flops 12079595520 | bytes 2760704 | tf_op jit(solution)/shard_map/apply1/pallas_call | solution.py:256
  18.9 4.0 %collective-permute-start.4 = (f32[128,128]{1,0:T(8,128)S(1)}, f32[128,128]{1,0:T(8,128)S(1)}, u32[]{:S(2)}, u32[]{:S(2)}) collective-permute-start(f32[128,128]{1,0:T(8,128)S(1)} %apply1.1.a_ref), channel_id=1, source_target_pairs={{0,1},{1,2},{2,3},{3,4},{4,5},{5,6},{6,7},{7,8},{8,9},{9,10},{10,1... | collective-permute-start | bytes 196616 | tf_op jit(solution)/shard_map/ppermute | solution.py:312
  22.9 0.0 collective-permute-done.3.got_b_ref
  22.9 0.9 %adjoint2.1 = (f32[128,128]{1,0:T(8,128)S(1)}, f32[128,128]{1,0:T(8,128)S(1)}) custom-call(f32[136,128]{1,0:T(8,128)S(1)} %get-tuple-element.32.own_ref, f32[128,128]{1,0:T(8,128)S(1)} %apply1.1.a_ref, f32[128,128]{1,0:T(8,128)S(1)} %collective-permute-done.3.got_b_ref, bf16[2048,256]{1,0:T(8,128)(2,1)S(1)} %get-tuple-element.35.lt_ref, ...), custom_call_target="tpu_custom_call" | custom-call | flops 10737418240 | bytes 2428928 | tf_op jit(solution)/shard_map/adjoint2/pallas_call | solution.py:256
  23.8 1.3 %collective-permute-start.5 = (f32[128,128]{1,0:T(8,128)S(1)}, f32[128,128]{1,0:T(8,128)S(1)}, u32[]{:S(2)}, u32[]{:S(2)}) collective-permute-start(f32[128,128]{1,0:T(8,128)S(1)} %get-tuple-element.43.b_ref), channel_id=1, source_target_pairs={{1,0},{2,1},{3,2},{4,3},{5,4},{6,5},{7,6},{8,7},{9,8},{10,9},{11,1... | collective-permute-start | bytes 196616 | tf_op jit(solution)/shard_map/ppermute | solution.py:317
  25.1 0.0 collective-permute-done.4.got_a_ref
  25.1 1.0 %apply2.1.a_ref = f32[128,128]{1,0:T(8,128)S(1)} custom-call(f32[136,128]{1,0:T(8,128)S(1)} %get-tuple-element.32.own_ref, f32[136,128]{1,0:T(8,128)S(1)} %collective-permute-done.below_ref, f32[128,128]{1,0:T(8,128)S(1)} %get-tuple-element.42.v_ref, f32[128,128]{1,0:T(8,128)S(1)} %collective-permute-done.4.got_a_ref, ...), custom_call_target="tpu_custom_call" | custom-call | flops 12079595520 | bytes 2760704 | tf_op jit(solution)/shard_map/apply2/pallas_call | solution.py:256
  26.2 4.7 %collective-permute-start.6 = (f32[128,128]{1,0:T(8,128)S(1)}, f32[128,128]{1,0:T(8,128)S(1)}, u32[]{:S(2)}, u32[]{:S(2)}) collective-permute-start(f32[128,128]{1,0:T(8,128)S(1)} %apply2.1.a_ref), channel_id=1, source_target_pairs={{0,1},{1,2},{2,3},{3,4},{4,5},{5,6},{6,7},{7,8},{8,9},{9,10},{10,1... | collective-permute-start | bytes 196616 | tf_op jit(solution)/shard_map/ppermute | solution.py:312
  30.9 0.0 collective-permute-done.5.got_b_ref
  30.9 0.9 %adjoint3.1 = (f32[128,128]{1,0:T(8,128)S(1)}, f32[128,128]{1,0:T(8,128)S(1)}) custom-call(f32[136,128]{1,0:T(8,128)S(1)} %get-tuple-element.32.own_ref, f32[128,128]{1,0:T(8,128)S(1)} %apply2.1.a_ref, f32[128,128]{1,0:T(8,128)S(1)} %collective-permute-done.5.got_b_ref, bf16[2048,256]{1,0:T(8,128)(2,1)S(1)} %get-tuple-element.35.lt_ref, ...), custom_call_target="tpu_custom_call" | custom-call | flops 10737418240 | bytes 2428928 | tf_op jit(solution)/shard_map/adjoint3/pallas_call | solution.py:256
  31.9 1.3 %collective-permute-start.7 = (f32[128,128]{1,0:T(8,128)S(1)}, f32[128,128]{1,0:T(8,128)S(1)}, u32[]{:S(2)}, u32[]{:S(2)}) collective-permute-start(f32[128,128]{1,0:T(8,128)S(1)} %get-tuple-element.45), channel_id=1, source_target_pairs={{1,0},{2,1},{3,2},{4,3},{5,4},{6,5},{7,6},{8,7},{9,8},{10,9},{11,1... | collective-permute-start | bytes 196616 | tf_op jit(solution)/shard_map/ppermute | solution.py:317
  33.2 7.0 %collective-permute-start.9 = (f32[18,128,128]{2,1,0:T(8,128)S(1)}, f32[18,128,128]{2,1,0:T(8,128)S(1)}, u32[]{:S(2)}, u32[]{:S(2)}) collective-permute-start(f32[18,128,128]{2,1,0:T(8,128)S(1)} %get-tuple-element.49.m0_ref), channel_id=1, source_target_pairs={{0,64},{64,0},{128,192},{192,128},{256,320},{320,256},{384,448},{4... | collective-permute-start | bytes 3538952 | tf_op jit(solution)/shard_map/ppermute | solution.py:320
  40.2 1.9 %collective-permute-start.10 = (f32[18,128,128]{2,1,0:T(8,128)S(1)}, f32[18,128,128]{2,1,0:T(8,128)S(1)}, u32[]{:S(2)}, u32[]{:S(2)}) collective-permute-start(f32[18,128,128]{2,1,0:T(8,128)S(1)} %get-tuple-element.50.m1_ref), channel_id=1, source_target_pairs={{64,128},{192,256},{320,384},{128,64},{256,192},{384,320},{65,129}... | collective-permute-start | bytes 3538952 | tf_op jit(solution)/shard_map/ppermute | solution.py:319
  42.1 0.0 collective-permute-done.6.got_a_ref
  42.1 1.0 %apply3.1.part_ref = f32[128,128]{1,0:T(8,128)S(1)} custom-call(f32[136,128]{1,0:T(8,128)S(1)} %get-tuple-element.32.own_ref, f32[136,128]{1,0:T(8,128)S(1)} %collective-permute-done.below_ref, f32[128,128]{1,0:T(8,128)S(1)} %get-tuple-element.44.v_ref, f32[128,128]{1,0:T(8,128)S(1)} %collective-permute-done.6.got_a_ref, ...), custom_call_target="tpu_custom_call" | custom-call | flops 12079595520 | bytes 2760704 | tf_op jit(solution)/shard_map/apply3/pallas_call | solution.py:256
  43.2 0.0 collective-permute-done.7.got_b_ref
  43.2 0.1 finish.1
  43.3 33.9 %all_to_all.11 = f32[64,1,128]{2,1,0:T(1,128)S(1)} all-to-all(f32[64,1,128]{2,1,0:T(1,128)S(1)} %bitcast.14), channel_id=1, replica_groups=mesh['seg'=8,'blk'=64] {'blk'}, dimensions={0} | all-to-all | bytes 65536 | tf_op jit(solution)/shard_map/all_to_all | solution.py:331
  77.2 0.1 normalise.1
  77.3 2.2 %collective-permute-start.11 = (f32[128,128]{1,0:T(8,128)S(1)}, f32[128,128]{1,0:T(8,128)S(1)}, u32[]{:S(2)}, u32[]{:S(2)}) collective-permute-start(f32[128,128]{1,0:T(8,128)S(1)} %get-tuple-element.48), channel_id=1, source_target_pairs={{0,64},{64,0},{128,192},{192,128},{256,320},{320,256},{384,448},{4... | collective-permute-start | bytes 196616 | tf_op jit(solution)/shard_map/ppermute | solution.py:334
  79.6 3.7 %collective-permute-start.8 = (f32[128,128]{1,0:T(8,128)S(1)}, f32[128,128]{1,0:T(8,128)S(1)}, u32[]{:S(2)}, u32[]{:S(2)}) collective-permute-start(f32[128,128]{1,0:T(8,128)S(1)} %get-tuple-element.48), channel_id=1, source_target_pairs={{64,128},{192,256},{320,384},{128,64},{256,192},{384,320},{65,129}... | collective-permute-start | bytes 196616 | tf_op jit(solution)/shard_map/ppermute | solution.py:333
  83.3 0.0 collective-permute-done.9.x0_ref
  83.3 0.0 collective-permute-done.10.x1_ref
  83.3 0.6 parts.1
  83.9 0.0 collective-permute-done.11.kept_ref
  83.9 1.8 %extend_first.1 = (f32[18,128,128]{2,1,0:T(8,128)}, f32[18,128,128]{2,1,0:T(8,128)}) custom-call(f32[128,128]{1,0:T(8,128)S(1)} %collective-permute-done.11.kept_ref, bf16[2304,256]{1,0:T(8,128)(2,1)S(1)} %get-tuple-element.53.p_ref), custom_call_target="tpu_custom_call" | custom-call | flops 12079595520 | bytes 3604480 | tf_op jit(solution)/shard_map/extend_first/pallas_call | solution.py:256
  85.7 0.0 collective-permute-done.8.kept_ref
  85.7 2.3 %extend_second.1 = (f32[128,128]{1,0:T(8,128)}, f32[18,128,128]{2,1,0:T(8,128)}, f32[18,128,128]{2,1,0:T(8,128)}, f32[1]{0:T(128)}) custom-call(f32[128,128]{1,0:T(8,128)S(1)} %collective-permute-done.8.kept_ref, bf16[2304,256]{1,0:T(8,128)(2,1)S(1)} %get-tuple-element.51.p_ref, ...), custom_call_target="tpu_custom_call", output_to_operand_aliasing={{1}: (4, {}), {2}: (5, {})} | custom-call | flops 12079595520 | bytes 6127620 | tf_op jit(solution)/shard_map/extend_second/pallas_call | solution.py:256
Async XLA Ops:
  3.0 7.5 %collective-permute-start = (f32[136,128]{1,0:T(8,128)S(1)}, f32[136,128]{1,0:T(8,128)S(1)}, u32[]{:S(2)}, u32[]{:S(2)}) collective-permute-start(f32[136,128]{1,0:T(8,128)S(1)} %get-tuple-element.32.own_ref), channel_id=1, source_target_pairs={{0,1},{1,2},{2,3},{3,4},{4,5},{5,6},{6,7},{7,8},{8,9},{9,10},{10,1... | collective-permute-start | bytes 208904 | tf_op jit(solution)/shard_map/ppermute | solution.py:299
  8.6 7.0 %collective-permute-start.1 = (f32[128,128]{1,0:T(8,128)S(1)}, f32[128,128]{1,0:T(8,128)S(1)}, u32[]{:S(2)}, u32[]{:S(2)}) collective-permute-start(f32[128,128]{1,0:T(8,128)S(1)} %get-tuple-element.39.b_ref), channel_id=1, source_target_pairs={{1,0},{2,1},{3,2},{4,3},{5,4},{6,5},{7,6},{8,7},{9,8},{10,9},{11,1... | collective-permute-start | bytes 196616 | tf_op jit(solution)/shard_map/ppermute | solution.py:308
  11.6 6.3 %collective-permute-start.2 = (f32[128,128]{1,0:T(8,128)S(1)}, f32[128,128]{1,0:T(8,128)S(1)}, u32[]{:S(2)}, u32[]{:S(2)}) collective-permute-start(f32[128,128]{1,0:T(8,128)S(1)} %apply0.1.a_ref), channel_id=1, source_target_pairs={{0,1},{1,2},{2,3},{3,4},{4,5},{5,6},{6,7},{7,8},{8,9},{9,10},{10,1... | collective-permute-start | bytes 196616 | tf_op jit(solution)/shard_map/ppermute | solution.py:312
  16.5 6.4 %collective-permute-start.3 = (f32[128,128]{1,0:T(8,128)S(1)}, f32[128,128]{1,0:T(8,128)S(1)}, u32[]{:S(2)}, u32[]{:S(2)}) collective-permute-start(f32[128,128]{1,0:T(8,128)S(1)} %get-tuple-element.41.b_ref), channel_id=1, source_target_pairs={{1,0},{2,1},{3,2},{4,3},{5,4},{6,5},{7,6},{8,7},{9,8},{10,9},{11,1... | collective-permute-start | bytes 196616 | tf_op jit(solution)/shard_map/ppermute | solution.py:317
  18.9 6.3 %collective-permute-start.4 = (f32[128,128]{1,0:T(8,128)S(1)}, f32[128,128]{1,0:T(8,128)S(1)}, u32[]{:S(2)}, u32[]{:S(2)}) collective-permute-start(f32[128,128]{1,0:T(8,128)S(1)} %apply1.1.a_ref), channel_id=1, source_target_pairs={{0,1},{1,2},{2,3},{3,4},{4,5},{5,6},{6,7},{7,8},{8,9},{9,10},{10,1... | collective-permute-start | bytes 196616 | tf_op jit(solution)/shard_map/ppermute | solution.py:312
  23.8 7.1 %collective-permute-start.5 = (f32[128,128]{1,0:T(8,128)S(1)}, f32[128,128]{1,0:T(8,128)S(1)}, u32[]{:S(2)}, u32[]{:S(2)}) collective-permute-start(f32[128,128]{1,0:T(8,128)S(1)} %get-tuple-element.43.b_ref), channel_id=1, source_target_pairs={{1,0},{2,1},{3,2},{4,3},{5,4},{6,5},{7,6},{8,7},{9,8},{10,9},{11,1... | collective-permute-start | bytes 196616 | tf_op jit(solution)/shard_map/ppermute | solution.py:317
  26.2 15.9 %collective-permute-start.6 = (f32[128,128]{1,0:T(8,128)S(1)}, f32[128,128]{1,0:T(8,128)S(1)}, u32[]{:S(2)}, u32[]{:S(2)}) collective-permute-start(f32[128,128]{1,0:T(8,128)S(1)} %apply2.1.a_ref), channel_id=1, source_target_pairs={{0,1},{1,2},{2,3},{3,4},{4,5},{5,6},{6,7},{7,8},{8,9},{9,10},{10,1... | collective-permute-start | bytes 196616 | tf_op jit(solution)/shard_map/ppermute | solution.py:312
  31.9 11.3 %collective-permute-start.7 = (f32[128,128]{1,0:T(8,128)S(1)}, f32[128,128]{1,0:T(8,128)S(1)}, u32[]{:S(2)}, u32[]{:S(2)}) collective-permute-start(f32[128,128]{1,0:T(8,128)S(1)} %get-tuple-element.45), channel_id=1, source_target_pairs={{1,0},{2,1},{3,2},{4,3},{5,4},{6,5},{7,6},{8,7},{9,8},{10,9},{11,1... | collective-permute-start | bytes 196616 | tf_op jit(solution)/shard_map/ppermute | solution.py:317
  33.2 50.1 %collective-permute-start.9 = (f32[18,128,128]{2,1,0:T(8,128)S(1)}, f32[18,128,128]{2,1,0:T(8,128)S(1)}, u32[]{:S(2)}, u32[]{:S(2)}) collective-permute-start(f32[18,128,128]{2,1,0:T(8,128)S(1)} %get-tuple-element.49.m0_ref), channel_id=1, source_target_pairs={{0,64},{64,0},{128,192},{192,128},{256,320},{320,256},{384,448},{4... | collective-permute-start | bytes 3538952 | tf_op jit(solution)/shard_map/ppermute | solution.py:320
  40.2 43.1 %collective-permute-start.10 = (f32[18,128,128]{2,1,0:T(8,128)S(1)}, f32[18,128,128]{2,1,0:T(8,128)S(1)}, u32[]{:S(2)}, u32[]{:S(2)}) collective-permute-start(f32[18,128,128]{2,1,0:T(8,128)S(1)} %get-tuple-element.50.m1_ref), channel_id=1, source_target_pairs={{64,128},{192,256},{320,384},{128,64},{256,192},{384,320},{65,129}... | collective-permute-start | bytes 3538952 | tf_op jit(solution)/shard_map/ppermute | solution.py:319
  77.3 6.6 %collective-permute-start.11 = (f32[128,128]{1,0:T(8,128)S(1)}, f32[128,128]{1,0:T(8,128)S(1)}, u32[]{:S(2)}, u32[]{:S(2)}) collective-permute-start(f32[128,128]{1,0:T(8,128)S(1)} %get-tuple-element.48), channel_id=1, source_target_pairs={{0,64},{64,0},{128,192},{192,128},{256,320},{320,256},{384,448},{4... | collective-permute-start | bytes 196616 | tf_op jit(solution)/shard_map/ppermute | solution.py:334
  79.6 6.1 %collective-permute-start.8 = (f32[128,128]{1,0:T(8,128)S(1)}, f32[128,128]{1,0:T(8,128)S(1)}, u32[]{:S(2)}, u32[]{:S(2)}) collective-permute-start(f32[128,128]{1,0:T(8,128)S(1)} %get-tuple-element.48), channel_id=1, source_target_pairs={{64,128},{192,256},{320,384},{128,64},{256,192},{384,320},{65,129}... | collective-permute-start | bytes 196616 | tf_op jit(solution)/shard_map/ppermute | solution.py:333

commit v5 on v4

v5 whole, which is shorter than its diff:
```python
import functools
import math

import jax
import jax.numpy as jnp
from jax import lax
from jax.experimental import pallas as pl
from jax.experimental.pallas import tpu as pltpu
from jax.sharding import PartitionSpec as P

ITERS = 4
SHIFT = 20.0
BOND = 6144.0
PARTS = 4
CHUNKS = 3
f32 = jnp.float32
bf16 = jnp.bfloat16
VMEM = pl.BlockSpec(memory_space=pltpu.VMEM)
SMEM = pl.BlockSpec(memory_space=pltpu.SMEM)
HBM = pl.BlockSpec(memory_space=pltpu.HBM)
ANY = pl.BlockSpec(memory_space=pl.ANY)
SDS = jax.ShapeDtypeStruct


def dot(a, b):
    return jnp.dot(a, b, preferred_element_type=f32)


def split(x):
    high = x.astype(bf16)
    return high, (x - high.astype(f32)).astype(bf16)


def weight(x):
    high, low = split(x)
    row = jnp.concatenate([high, low], 1)
    return jnp.concatenate([row, row], 0)


def folded(t):
    n = t.shape[1] // 2
    return t[:, :n] + t[:, n:]


def sandwich(p_ref, q_ref, x):
    n = x.shape[0]
    w = weight(x)
    total = None
    for pair in range(p_ref.shape[0] // (2 * n)):
        rows = pl.ds(pair * 2 * n, 2 * n)
        t = folded(dot(p_ref[rows, :], w))
        high, low = split(t)
        lhs = jnp.concatenate(
            [
                jnp.concatenate([high[:n], high[n:]], 1),
                jnp.concatenate([low[:n], low[n:]], 1),
            ],
            0,
        )
        term = dot(lhs, q_ref[rows, :])
        total = term if total is None else total + term
    total = folded(total)
    return total[:n] + total[n:]


def square_mask(size):
    n = size.shape[1]
    size = jnp.broadcast_to(size, (n, n))
    rows = lax.broadcasted_iota(jnp.int32, (n, n), 0).astype(f32)
    cols = lax.broadcasted_iota(jnp.int32, (n, n), 1).astype(f32)
    return (rows < size) & (cols < size)


def where(mask, x):
    return jnp.where(mask, x, 0.0)


def put_parts(out_ref, h, n, x):
    high, low = split(x)
    out_ref[pl.ds(h * n, n), :n] = high
    out_ref[pl.ds(h * n, n), n:] = low


def odd(axis):
    return lax.rem(lax.axis_index(axis), 2) == 1


def load(size_ref, x_ref, dl_ref, hl_ref, dr_ref, hr_ref, own_ref, m0_ref, m1_ref, x, sems):
    n = x.shape[0]
    diags, hops = dl_ref.shape[0], hl_ref.shape[0]
    first = pltpu.make_async_copy(x_ref, x, sems.at[0])
    first.start()
    part = hops // PARTS
    left, right = (dl_ref, hl_ref), (dr_ref, hr_ref)

    def loads(sides):
        copies = []
        for side, ((diag, hop), out) in enumerate(zip(sides, (m0_ref, m1_ref))):
            sem = 1 + side * (1 + PARTS)
            copies.append(pltpu.make_async_copy(diag, out.at[pl.ds(0, diags)], sems.at[sem]))
            for i in range(PARTS):
                source, target = pl.ds(i * part, part), pl.ds(diags + i * part, part)
                copies.append(pltpu.make_async_copy(hop.at[source], out.at[target], sems.at[sem + 1 + i]))
        return copies

    segment = odd("seg")

    @pl.when(segment)
    def _():
        for copy in loads((right, left)):
            copy.start()

    @pl.when(jnp.logical_not(segment))
    def _():
        for copy in loads((left, right)):
            copy.start()

    first.wait()
    live = jnp.full((1, n), size_ref[0, 0].astype(f32), f32)
    own_ref[:n, :] = where(square_mask(live), x[...])
    own_ref[n:, :] = jnp.broadcast_to(live, (8, n))
    for copy in loads((left, right)):
        copy.wait()


def messages(low_ref, high_ref, up, down):
    n = up.shape[0]
    sector = odd("blk")
    low_ref[:n, :] = jnp.where(sector, down, up)
    high_ref[:n, :] = jnp.where(sector, up, down)


def received(low_ref, high_ref):
    n = low_ref.shape[1]
    low, high = low_ref[:n, :], high_ref[:n, :]
    sector = odd("blk")
    return jnp.where(sector, low, high), jnp.where(sector, high, low)


def sent_down(low_ref, high_ref):
    n = low_ref.shape[1]
    return jnp.where(odd("blk"), low_ref[:n, :], high_ref[:n, :])


def first_adjoint(own_ref, m0_ref, m1_ref, lt_ref, rc_ref, dlt_ref, drc_ref, low_ref, high_ref):
    n = own_ref.shape[1]
    diags = dlt_ref.shape[0] // n
    segment = odd("seg")
    for c in range(m0_ref.shape[0]):
        x, y = m0_ref[c], m1_ref[c]
        k = c if c < diags else c - diags
        put_parts(dlt_ref if c < diags else lt_ref, k, n, jnp.where(segment, y, x).T)
        put_parts(drc_ref if c < diags else rc_ref, k, n, jnp.where(segment, x, y))
    v = own_ref[:n, :]
    messages(low_ref, high_ref, v, sandwich(lt_ref, rc_ref, v))
    low_ref[n:, :] = own_ref[n:, :]
    high_ref[n:, :] = own_ref[n:, :]


def applied_here(size, v, below, lt_ref, rc_ref, dlt_ref, drc_ref):
    hop = sandwich(rc_ref, lt_ref, below.T)
    diag = sandwich(drc_ref, dlt_ref, v.T)
    return where(square_mask(size), (hop + diag).T)


def first_round(own_ref, high_in, low_in, lt_ref, rc_ref, dlt_ref, drc_ref, size_ref, v_ref, low_ref, high_ref):
    n = own_ref.shape[1]
    size = own_ref[n : n + 1, :]
    below, above = received(low_in, high_in)
    size_ref[...] = jnp.where(odd("blk"), low_in[n:, :], high_in[n:, :])
    v = own_ref[:n, :]
    a = SHIFT * v - applied_here(size, v, below, lt_ref, rc_ref, dlt_ref, drc_ref)
    v = a - where(square_mask(size), above)
    v_ref[...] = v
    messages(low_ref, high_ref, a, sandwich(lt_ref, rc_ref, v))


def later_round(
    own_ref, v_ref, high_in, low_in, low_sent, high_sent, size_ref, lt_ref, rc_ref, dlt_ref, drc_ref, new_ref, low_ref, high_ref
):
    n = own_ref.shape[1]
    size = own_ref[n : n + 1, :]
    below, above = received(low_in, high_in)
    below = where(square_mask(size_ref[0:1, :]), below - sent_down(low_sent, high_sent))
    v = v_ref[...]
    a = SHIFT * v - applied_here(size, v, below, lt_ref, rc_ref, dlt_ref, drc_ref)
    v = a - where(square_mask(size), above)
    new_ref[...] = v
    messages(low_ref, high_ref, a, sandwich(lt_ref, rc_ref, v))


def total_of(x):
    return jnp.sum(jnp.sum(x, axis=0, keepdims=True), axis=1, keepdims=True)


def last_round(
    rank_ref, own_ref, v_ref, high_in, low_in, low_sent, high_sent, size_ref, lt_ref, rc_ref, dlt_ref, drc_ref, v4_ref, sums_ref
):
    n = own_ref.shape[1]
    size = own_ref[n : n + 1, :]
    below, above = received(low_in, high_in)
    below = where(square_mask(size_ref[0:1, :]), below - sent_down(low_sent, high_sent))
    v = v_ref[...]
    applied = applied_here(size, v, below, lt_ref, rc_ref, dlt_ref, drc_ref) + where(square_mask(size), above)
    v4 = SHIFT * v - applied
    v4_ref[:n, :] = v4
    kept_cols = jnp.minimum(jnp.full((1, n), rank_ref[0, 0].astype(f32), f32), size)
    v4_ref[n:, :] = jnp.broadcast_to(kept_cols, (8, n))
    lane = lax.broadcasted_iota(jnp.int32, (1, n), 1)
    row = jnp.where(lane == 0, total_of(v4 * v4), 0.0)
    row = jnp.where(lane == 1, total_of(v * applied), row)
    row = jnp.where(lane == 2, total_of(v * v), row)
    sums_ref[...] = jnp.broadcast_to(row, sums_ref.shape)


def lane_of(row, j):
    lane = lax.broadcasted_iota(jnp.int32, row.shape, 1)
    return jnp.sum(jnp.where(lane == j, row, 0.0), axis=1, keepdims=True)


def normalise(v4_ref, sums_ref, state_ref, kept_ref):
    n = v4_ref.shape[1]
    total = jnp.sum(sums_ref[...], axis=0, keepdims=True)
    state = v4_ref[:n, :] * jnp.sqrt(BOND * n / lane_of(total, 0))
    state_ref[...] = state
    cols = lax.broadcasted_iota(jnp.int32, (n, n), 1).astype(f32)
    kept_ref[...] = where(cols < jnp.broadcast_to(v4_ref[n : n + 1, :], (n, n)), state)


def parts(x0_ref, x1_ref, sums_ref, p0_ref, p1_ref, energy_ref):
    n = x0_ref.shape[1]
    segment = odd("seg")
    for c in range(x0_ref.shape[0]):
        x, y = x0_ref[c], x1_ref[c]
        put_parts(p0_ref, c, n, jnp.where(segment, x.T, x))
        put_parts(p1_ref, c, n, jnp.where(segment, y, y.T))
    total = jnp.sum(sums_ref[...], axis=0, keepdims=True)
    energy_ref[0] = jnp.sum(lane_of(total, 1) / lane_of(total, 2))


def extend(
    kept1_ref, kept0_ref, p0_ref, p1_ref, state_ref, new_ref, left_ref, right_ref, out0, out1, sems, state_sem
):
    n = kept0_ref.shape[0]
    channels = out0.shape[0]
    step = channels // CHUNKS
    segment = odd("seg")
    even = jnp.logical_not(segment)
    state_copy = pltpu.make_async_copy(state_ref, new_ref, state_sem)
    state_copy.start()
    sides = []
    for side, (kept_ref, p_ref, out, is_left) in enumerate(
        ((kept0_ref, p0_ref, out0, segment), (kept1_ref, p1_ref, out1, even))
    ):
        kept = kept_ref[...]
        sides.append((side, p_ref, out, weight(jnp.where(is_left, kept, kept.T))))

    def copy(side, target, i):
        at = pl.ds(i * step, step)
        return pltpu.make_async_copy((out0, out1)[side].at[at], target.at[at], sems.at[side, i])

    for i in range(CHUNKS):
        for side, p_ref, out, w in sides:
            for c in range(i * step, (i + 1) * step, 2):
                half = folded(dot(p_ref[pl.ds(c * n, 2 * n), :], w))
                flip = jnp.concatenate([half[:n].T, half[n:].T], 0)
                y = folded(dot(jnp.concatenate(split(flip), 1), w)) * (1.0 / math.sqrt(n))
                out[c] = y[:n]
                out[c + 1] = y[n:]

        @pl.when(segment)
        def _():
            copy(0, left_ref, i).start()
            copy(1, right_ref, i).start()

        @pl.when(even)
        def _():
            copy(0, right_ref, i).start()
            copy(1, left_ref, i).start()

    for i in range(CHUNKS):
        copy(0, left_ref, i).wait()
        copy(1, right_ref, i).wait()
    state_copy.wait()


def call(kernel, args, specs, outs, out_specs=None, scratch=(), flops=0, limit=16, name=None):
    moved = sum(math.prod(a.shape) * a.dtype.itemsize for a in (*args, *outs))
    args = [pltpu.with_memory_space_constraint(a, pltpu.HBM) if spec is HBM else a for a, spec in zip(args, specs)]
    return pl.pallas_call(
        kernel,
        in_specs=specs,
        out_specs=out_specs or [VMEM] * len(outs),
        out_shape=outs,
        scratch_shapes=list(scratch),
        compiler_params=pltpu.CompilerParams(vmem_limit_bytes=limit << 20),
        cost_estimate=pl.CostEstimate(flops=flops, bytes_accessed=moved, transcendentals=0),
        name=name,
    )(*args)


def shards(two_site, diag_left, diag_right, hop_left, hop_right, sector_sizes, ranks):
    n = two_site.shape[2]
    x0 = two_site[0, 0]
    dl, dr, hl, hr = diag_left[0, 0], diag_right[0, 0], hop_left[0, 0], hop_right[0, 0]
    hops, diags = hl.shape[0], dl.shape[0]
    blocks, segs = lax.axis_size("blk"), lax.axis_size("seg")
    low_pairs = [(i, i ^ 1) for i in range(blocks)]
    high_pairs = [(i, i + 1) for i in range(1, blocks - 1, 2)]
    high_pairs += [(target, source) for source, target in high_pairs]
    chip = [(i, i ^ 1) for i in range(segs)]
    across = [(i, i + 1) for i in range(1, segs - 1, 2)]
    across += [(target, source) for source, target in across]
    block = SDS((n, n), f32)
    message = SDS((n + 8, n), f32)
    hop_parts = SDS((hops * n, 2 * n), bf16)
    diag_parts = SDS((diags * n, 2 * n), bf16)
    out = SDS((diags + hops, n, n), f32)
    channel = 20 * 8 * 2 * n**3

    own, m0, m1 = call(
        load,
        (sector_sizes, x0, dl, hl, dr, hr),
        [SMEM] + [HBM] * 5,
        [message, out, out],
        scratch=[
            pltpu.VMEM((n, n), f32),
            pltpu.SemaphoreType.DMA((3 + 2 * PARTS,)),
        ],
        limit=32,
        name="load",
    )
    lt, rc, dlt, drc, low, high = call(
        first_adjoint,
        (own, m0, m1),
        [VMEM] * 3,
        [hop_parts, hop_parts, diag_parts, diag_parts, message, message],
        flops=channel * hops,
        name="first_adjoint",
    )
    ops = (lt, rc, dlt, drc)
    for k in range(ITERS):
        high_in = lax.ppermute(high, "blk", high_pairs)
        low_in = lax.ppermute(low, "blk", low_pairs)
        sent = low, high
        if k == 0:
            size, v, low, high = call(
                first_round,
                (own, high_in, low_in, *ops),
                [VMEM] * 7,
                [SDS((8, n), f32), block, block, block],
                flops=channel * (2 * hops + diags),
                name="round0",
            )
        elif k < ITERS - 1:
            v, low, high = call(
                later_round,
                (own, v, high_in, low_in, *before, size, *ops),
                [VMEM] * 11,
                [block, block, block],
                flops=channel * (2 * hops + diags),
                name=f"round{k}",
            )
        if k < ITERS - 1:
            before = sent
    x1 = lax.ppermute(lax.optimization_barrier((m1, sent[0]))[0], "seg", across)
    x0 = lax.ppermute(lax.optimization_barrier((m0, sent[0]))[0], "seg", chip)
    sums_block = SDS((blocks, n), f32)
    v4, sums = call(
        last_round,
        (lax.optimization_barrier((ranks, sent[0]))[0], own, v, high_in, low_in, *before, size, *ops),
        [SMEM] + [VMEM] * 11,
        [message, sums_block],
        flops=channel * (hops + diags),
        name="last_round",
    )
    sums = lax.all_to_all(sums, "blk", 0, 0, tiled=True)
    state, kept = call(normalise, (v4, sums), [VMEM] * 2, [block, block], name="normalise")
    kept1 = lax.ppermute(kept, "seg", across)
    kept0 = lax.ppermute(kept, "seg", chip)
    all_parts = SDS(((diags + hops) * n, 2 * n), bf16)
    p0, p1, energy = call(
        parts,
        (x0, x1, sums),
        [VMEM] * 3,
        [all_parts, all_parts, SDS((1,), f32)],
        out_specs=[VMEM, VMEM, SMEM],
        flops=channel * hops,
        name="parts",
    )
    state, left, right = call(
        extend,
        (kept1, kept0, p0, p1, state),
        [VMEM] * 5,
        [block, out, out],
        out_specs=[ANY] * 3,
        scratch=[
            pltpu.VMEM(out.shape, f32),
            pltpu.VMEM(out.shape, f32),
            pltpu.SemaphoreType.DMA((2, CHUNKS)),
            pltpu.SemaphoreType.DMA,
        ],
        flops=2 * channel * (hops + diags),
        name="extend",
    )
    return state[None, None], left[None, None], right[None, None], energy


def solution(mesh):
    wide = P("seg", "blk", None, None, None)
    return jax.shard_map(
        shards,
        mesh=mesh,
        in_specs=(P("seg", "blk", None, None), wide, wide, wide, wide, P("seg", "blk"), P("seg", "blk")),
        out_specs=(P("seg", "blk", None, None), wide, wide, P("seg")),
        check_vma=False,
    )
```

time: 88.5 us -> 91.6 us (1.035)
  blocking collectives: 33.9 us -> 25.6 us
  starting transfers between devices: 36.8 us -> 44.2 us
  waiting for transfers between devices: 0.03 us -> 6.12 us
  Pallas kernels: 15.1 us -> 13.1 us
    all_to_all x1, blocking collectives: 33.9 us -> 25.6 us  [shards(): sums = lax.all_to_all(sums, 'blk', 0, 0, tiled=True)]
    ppermute x10, starting transfers between devices: 30.8 us -> 38.2 us  [the longest x4 25.4 us: shards(): low_in = lax.ppermute(low, 'blk', low_pairs)]
    ppermute x10, waiting for transfers between devices: 0.03 us -> 4.95 us  [the longest x4 4.93 us: shards(): low_in = lax.ppermute(low, 'blk', low_pairs)]
    pallas_call x14 -> x9, Pallas kernels: 15.1 us -> 13.1 us  [call(): pl.pallas_call(kernel, in_specs=specs, out_specs=out_specs or [VMEM] * le...]
    ppermute x1, waiting for transfers between devices: 0.01 us -> 1.17 us  [shards(): kept1 = lax.ppermute(kept, 'seg', across)]
  transfers between devices with their start and end apart: 12 -> 12, of which waited for: 0 -> 4; matrix products, arithmetic and copies ran while one was open for 0% -> 0% of each run, Pallas kernels for 13% -> 2%
where the time goes in v5:
time: 91.6 us; the launch traced here: 91.1 us
  starting transfers between devices  44.2 us (48%)
  blocking collectives  25.6 us (28%)
  Pallas kernels  13.1 us (14%)
  waiting for transfers between devices  6.12 us (7%)
  between operations  2.14 us (2%)
    all_to_all x1, blocking collectives, shards(): sums = lax.all_to_all(sums, 'blk', 0, 0, tiled=True)  25.6 us
    ppermute x4, starting transfers between devices, shards(): low_in = lax.ppermute(low, 'blk', low_pairs)  25.4 us
    pallas_call x9, Pallas kernels, call(): pl.pallas_call(kernel, in_specs=specs, out_specs=out_specs or [VMEM] * le...  13.1 us
    ppermute x1, starting transfers between devices, shards(): x0 = lax.ppermute(lax.optimization_barrier((m0, sent[0]))[0], 'seg', chip)  7.15 us
    ppermute x4, waiting for transfers between devices, shards(): low_in = lax.ppermute(low, 'blk', low_pairs)  4.93 us
    ppermute x1, starting transfers between devices, shards(): kept1 = lax.ppermute(kept, 'seg', across)  4.03 us
    ppermute x1, starting transfers between devices, shards(): x1 = lax.ppermute(lax.optimization_barrier((m1, sent[0]))[0], 'seg', across)  3.02 us
    ppermute x4, starting transfers between devices, shards(): high_in = lax.ppermute(high, 'blk', high_pairs)  2.66 us
  transfers between devices with their start and end apart: 12, of which 4 were waited for; matrix products, arithmetic and copies ran while one was open for 0% of the time, Pallas kernels for 2%

profile of v5, /device:TPU:1, one launch (start us, length us, event | category | flops | bytes accessed | tf_op | source)
XLA Modules:
  0.0 91.1 jit_solution(6906413645694831293)
XLA Ops:
  1.3 1.7 %load.1 = (f32[136,128]{1,0:T(8,128)S(1)}, f32[18,128,128]{2,1,0:T(8,128)S(1)}, f32[18,128,128]{2,1,0:T(8,128)S(1)}) custom-call(s32[1,1]{1,0:T(1,128)S(6)} %copy.12.size_ref, f32[128,128]{1,0:T(8,128)} %bitcast.19, f32[2,128,128]{2,1,0:T(8,128)} %bitcast.17, f32[16,128,128]{2,1,0:T(8,128)} %bitcast.15, f32[2,128,128]{2,1,0:T(8,128)} %bitcast.18, ...), custom_call_target="tpu_custom_call" | custom-call | bytes 4853764 | tf_op jit(solution)/shard_map/load/pallas_call | solution.py:290
  3.0 1.0 %first_adjoint.1 = (bf16[2048,256]{1,0:T(8,128)(2,1)S(1)}, bf16[2048,256]{1,0:T(8,128)(2,1)S(1)}, bf16[256,256]{1,0:T(8,128)(2,1)S(1)}, bf16[256,256]{1,0:T(8,12...) custom-call(f32[136,128]{1,0:T(8,128)S(1)} %get-tuple-element.36.own_ref, ...), custom_call_target="tpu_custom_call" | custom-call | flops 10737418240 | bytes 4927488 | tf_op jit(solution)/shard_map/first_adjoint/pallas_call | solution.py:290
  4.1 0.7 collective-permute-start
  4.7 6.6 %collective-permute-start.1 = (f32[136,128]{1,0:T(8,128)S(1)}, f32[136,128]{1,0:T(8,128)S(1)}, u32[]{:S(2)}, u32[]{:S(2)}) collective-permute-start(f32[136,128]{1,0:T(8,128)S(1)} %get-tuple-element.40.low_sent), channel_id=1, source_target_pairs={{0,1},{1,0},{2,3},{3,2},{4,5},{5,4},{6,7},{7,6},{8,9},{9,8},{10,11... | collective-permute-start | bytes 208904 | tf_op jit(solution)/shard_map/ppermute | solution.py:344
  11.3 0.0 collective-permute-done.high_in
  11.3 1.7 %collective-permute-done.1.low_in = f32[136,128]{1,0:T(8,128)S(1)} collective-permute-done((f32[136,128]{1,0:T(8,128)S(1)}, f32[136,128]{1,0:T(8,128)S(1)}, u32[]{:S(2)}, u32[]{:S(2)}) %collective-permute-start.1) | collective-permute-done | bytes 69664 | tf_op jit(solution)/shard_map/ppermute | solution.py:344
  13.0 2.0 %round0.1 = (f32[8,128]{1,0:T(8,128)S(1)}, f32[128,128]{1,0:T(8,128)S(1)}, f32[128,128]{1,0:T(8,128)S(1)}, f32[128,128]{1,0:T(8,128)S(1)}) custom-call(f32[136,128]{1,0:T(8,128)S(1)} %get-tuple-element.36.own_ref, f32[136,128]{1,0:T(8,128)S(1)} %collective-permute-done.high_in, f32[136,128]{1,0:T(8,128)S(1)} %collective-permute-done.1.low_in, ...), custom_call_target="tpu_custom_call" | custom-call | flops 22817013760 | bytes 2768896 | tf_op jit(solution)/shard_map/round0/pallas_call | solution.py:290
  15.0 0.7 collective-permute-start.2
  15.6 7.0 %collective-permute-start.3 = (f32[128,128]{1,0:T(8,128)S(1)}, f32[128,128]{1,0:T(8,128)S(1)}, u32[]{:S(2)}, u32[]{:S(2)}) collective-permute-start(f32[128,128]{1,0:T(8,128)S(1)} %get-tuple-element.47.low_sent), channel_id=1, source_target_pairs={{0,1},{1,0},{2,3},{3,2},{4,5},{5,4},{6,7},{7,6},{8,9},{9,8},{10,11... | collective-permute-start | bytes 196616 | tf_op jit(solution)/shard_map/ppermute | solution.py:344
  22.6 0.0 collective-permute-done.2.high_in
  22.6 1.6 %collective-permute-done.3.low_in = f32[128,128]{1,0:T(8,128)S(1)} collective-permute-done((f32[128,128]{1,0:T(8,128)S(1)}, f32[128,128]{1,0:T(8,128)S(1)}, u32[]{:S(2)}, u32[]{:S(2)}) %collective-permute-start.3) | collective-permute-done | bytes 65568 | tf_op jit(solution)/shard_map/ppermute | solution.py:344
  24.2 2.0 %round1.1 = (f32[128,128]{1,0:T(8,128)S(1)}, f32[128,128]{1,0:T(8,128)S(1)}, f32[128,128]{1,0:T(8,128)S(1)}) custom-call(f32[136,128]{1,0:T(8,128)S(1)} %get-tuple-element.36.own_ref, f32[128,128]{1,0:T(8,128)S(1)} %get-tuple-element.45.v_ref, f32[128,128]{1,0:T(8,128)S(1)} %collective-permute-done.2.high_in, f32[128,128]{1,0:T(8,128)S(1)} %collective-permute-done.3.low_in, ...), custom_call_target="tpu_custom_call" | custom-call | flops 22817013760 | bytes 2965504 | tf_op jit(solution)/shard_map/round1/pallas_call | solution.py:290
  26.2 0.7 collective-permute-start.4
  26.9 5.3 %collective-permute-start.5 = (f32[128,128]{1,0:T(8,128)S(1)}, f32[128,128]{1,0:T(8,128)S(1)}, u32[]{:S(2)}, u32[]{:S(2)}) collective-permute-start(f32[128,128]{1,0:T(8,128)S(1)} %get-tuple-element.51.low_sent), channel_id=1, source_target_pairs={{0,1},{1,0},{2,3},{3,2},{4,5},{5,4},{6,7},{7,6},{8,9},{9,8},{10,11... | collective-permute-start | bytes 196616 | tf_op jit(solution)/shard_map/ppermute | solution.py:344
  32.2 0.0 collective-permute-done.4.high_in
  32.2 1.6 %collective-permute-done.5.low_in = f32[128,128]{1,0:T(8,128)S(1)} collective-permute-done((f32[128,128]{1,0:T(8,128)S(1)}, f32[128,128]{1,0:T(8,128)S(1)}, u32[]{:S(2)}, u32[]{:S(2)}) %collective-permute-start.5) | collective-permute-done | bytes 65568 | tf_op jit(solution)/shard_map/ppermute | solution.py:344
  33.8 2.0 %round2.1 = (f32[128,128]{1,0:T(8,128)S(1)}, f32[128,128]{1,0:T(8,128)S(1)}, f32[128,128]{1,0:T(8,128)S(1)}) custom-call(f32[136,128]{1,0:T(8,128)S(1)} %get-tuple-element.36.own_ref, f32[128,128]{1,0:T(8,128)S(1)} %get-tuple-element.49.v_ref, f32[128,128]{1,0:T(8,128)S(1)} %collective-permute-done.4.high_in, f32[128,128]{1,0:T(8,128)S(1)} %collective-permute-done.5.low_in, ...), custom_call_target="tpu_custom_call" | custom-call | flops 22817013760 | bytes 2957312 | tf_op jit(solution)/shard_map/round2/pallas_call | solution.py:290
  35.8 0.7 collective-permute-start.6
  36.4 6.6 %collective-permute-start.7 = (f32[128,128]{1,0:T(8,128)S(1)}, f32[128,128]{1,0:T(8,128)S(1)}, u32[]{:S(2)}, u32[]{:S(2)}) collective-permute-start(f32[128,128]{1,0:T(8,128)S(1)} %get-tuple-element.52), channel_id=1, source_target_pairs={{0,1},{1,0},{2,3},{3,2},{4,5},{5,4},{6,7},{7,6},{8,9},{9,8},{10,11... | collective-permute-start | bytes 196616 | tf_op jit(solution)/shard_map/ppermute | solution.py:344
  43.7 7.2 %collective-permute-start.10 = (f32[18,128,128]{2,1,0:T(8,128)S(1)}, f32[18,128,128]{2,1,0:T(8,128)S(1)}, u32[]{:S(2)}, u32[]{:S(2)}) collective-permute-start(f32[18,128,128]{2,1,0:T(8,128)S(1)} %get-tuple-element.59.m0_ref), channel_id=1, source_target_pairs={{0,64},{64,0},{128,192},{192,128},{256,320},{320,256},{384,448},{4... | collective-permute-start | bytes 3538952 | tf_op jit(solution)/shard_map/ppermute | solution.py:367
  50.9 3.0 %collective-permute-start.11 = (f32[18,128,128]{2,1,0:T(8,128)S(1)}, f32[18,128,128]{2,1,0:T(8,128)S(1)}, u32[]{:S(2)}, u32[]{:S(2)}) collective-permute-start(f32[18,128,128]{2,1,0:T(8,128)S(1)} %get-tuple-element.60.m1_ref), channel_id=1, source_target_pairs={{64,128},{192,256},{320,384},{128,64},{256,192},{384,320},{65,129}... | collective-permute-start | bytes 3538952 | tf_op jit(solution)/shard_map/ppermute | solution.py:366
  53.9 0.0 collective-permute-done.6.high_in
  53.9 0.0 collective-permute-done.7.low_in
  53.9 1.1 %last_round.1 = (f32[136,128]{1,0:T(8,128)S(1)}, f32[64,128]{1,0:T(8,128)S(1)}) custom-call(s32[1,1]{1,0:T(1,128)S(6)} %copy.13.rank_ref, f32[136,128]{1,0:T(8,128)S(1)} %get-tuple-element.36.own_ref, f32[128,128]{1,0:T(8,128)S(1)} %get-tuple-element.54.v_ref, f32[128,128]{1,0:T(8,128)S(1)} %collective-permute-done.6.high_in, ...), custom_call_target="tpu_custom_call" | custom-call | flops 12079595520 | bytes 2863108 | tf_op jit(solution)/shard_map/last_round/pallas_call | solution.py:290
  55.1 25.6 %all_to_all.11 = f32[64,1,128]{2,1,0:T(1,128)S(1)} all-to-all(f32[64,1,128]{2,1,0:T(1,128)S(1)} %bitcast.14), channel_id=1, replica_groups=mesh['seg'=8,'blk'=64] {'blk'}, dimensions={0} | all-to-all | bytes 65536 | tf_op jit(solution)/shard_map/all_to_all | solution.py:377
  80.6 0.1 normalise.1
  80.8 1.9 %collective-permute-start.9 = (f32[128,128]{1,0:T(8,128)S(1)}, f32[128,128]{1,0:T(8,128)S(1)}, u32[]{:S(2)}, u32[]{:S(2)}) collective-permute-start(f32[128,128]{1,0:T(8,128)S(1)} %get-tuple-element.58), channel_id=1, source_target_pairs={{0,64},{64,0},{128,192},{192,128},{256,320},{320,256},{384,448},{4... | collective-permute-start | bytes 196616 | tf_op jit(solution)/shard_map/ppermute | solution.py:380
  82.7 4.0 %collective-permute-start.8 = (f32[128,128]{1,0:T(8,128)S(1)}, f32[128,128]{1,0:T(8,128)S(1)}, u32[]{:S(2)}, u32[]{:S(2)}) collective-permute-start(f32[128,128]{1,0:T(8,128)S(1)} %get-tuple-element.58), channel_id=1, source_target_pairs={{64,128},{192,256},{320,384},{128,64},{256,192},{384,320},{65,129}... | collective-permute-start | bytes 196616 | tf_op jit(solution)/shard_map/ppermute | solution.py:379
  86.7 0.0 collective-permute-done.10.x0_ref
  86.7 0.0 collective-permute-done.11.x1_ref
  86.7 0.7 parts.1
  87.5 0.0 collective-permute-done.9.kept0_ref
  87.5 1.2 %collective-permute-done.8.kept1_ref = f32[128,128]{1,0:T(8,128)S(1)} collective-permute-done((f32[128,128]{1,0:T(8,128)S(1)}, f32[128,128]{1,0:T(8,128)S(1)}, u32[]{:S(2)}, u32[]{:S(2)}) %collective-permute-start.8) | collective-permute-done | bytes 65568 | tf_op jit(solution)/shard_map/ppermute | solution.py:379
  88.7 2.5 %extend.1 = (f32[128,128]{1,0:T(8,128)}, f32[18,128,128]{2,1,0:T(8,128)}, f32[18,128,128]{2,1,0:T(8,128)}) custom-call(f32[128,128]{1,0:T(8,128)S(1)} %collective-permute-done.8.kept1_ref, f32[128,128]{1,0:T(8,128)S(1)} %collective-permute-done.9.kept0_ref, bf16[2304,256]{1,0:T(8,128)(2,1)S(1)} %get-tuple-element.61.p0_ref, ...), custom_call_target="tpu_custom_call" | custom-call | flops 24159191040 | bytes 4980736 | tf_op jit(solution)/shard_map/extend/pallas_call | solution.py:290
Async XLA Ops:
  4.1 7.3 %collective-permute-start = (f32[136,128]{1,0:T(8,128)S(1)}, f32[136,128]{1,0:T(8,128)S(1)}, u32[]{:S(2)}, u32[]{:S(2)}) collective-permute-start(f32[136,128]{1,0:T(8,128)S(1)} %get-tuple-element.39.high_sent), channel_id=1, source_target_pairs={{1,2},{3,4},{5,6},{7,8},{9,10},{11,12},{13,14},{15,16},{17,18},{19... | collective-permute-start | bytes 208904 | tf_op jit(solution)/shard_map/ppermute | solution.py:343
  4.7 8.3 %collective-permute-start.1 = (f32[136,128]{1,0:T(8,128)S(1)}, f32[136,128]{1,0:T(8,128)S(1)}, u32[]{:S(2)}, u32[]{:S(2)}) collective-permute-start(f32[136,128]{1,0:T(8,128)S(1)} %get-tuple-element.40.low_sent), channel_id=1, source_target_pairs={{0,1},{1,0},{2,3},{3,2},{4,5},{5,4},{6,7},{7,6},{8,9},{9,8},{10,11... | collective-permute-start | bytes 208904 | tf_op jit(solution)/shard_map/ppermute | solution.py:344
  15.0 7.6 %collective-permute-start.2 = (f32[128,128]{1,0:T(8,128)S(1)}, f32[128,128]{1,0:T(8,128)S(1)}, u32[]{:S(2)}, u32[]{:S(2)}) collective-permute-start(f32[128,128]{1,0:T(8,128)S(1)} %get-tuple-element.46.high_sent), channel_id=1, source_target_pairs={{1,2},{3,4},{5,6},{7,8},{9,10},{11,12},{13,14},{15,16},{17,18},{19... | collective-permute-start | bytes 196616 | tf_op jit(solution)/shard_map/ppermute | solution.py:343
  15.6 8.6 %collective-permute-start.3 = (f32[128,128]{1,0:T(8,128)S(1)}, f32[128,128]{1,0:T(8,128)S(1)}, u32[]{:S(2)}, u32[]{:S(2)}) collective-permute-start(f32[128,128]{1,0:T(8,128)S(1)} %get-tuple-element.47.low_sent), channel_id=1, source_target_pairs={{0,1},{1,0},{2,3},{3,2},{4,5},{5,4},{6,7},{7,6},{8,9},{9,8},{10,11... | collective-permute-start | bytes 196616 | tf_op jit(solution)/shard_map/ppermute | solution.py:344
  26.2 6.0 %collective-permute-start.4 = (f32[128,128]{1,0:T(8,128)S(1)}, f32[128,128]{1,0:T(8,128)S(1)}, u32[]{:S(2)}, u32[]{:S(2)}) collective-permute-start(f32[128,128]{1,0:T(8,128)S(1)} %get-tuple-element.50.high_sent), channel_id=1, source_target_pairs={{1,2},{3,4},{5,6},{7,8},{9,10},{11,12},{13,14},{15,16},{17,18},{19... | collective-permute-start | bytes 196616 | tf_op jit(solution)/shard_map/ppermute | solution.py:343
  26.9 6.9 %collective-permute-start.5 = (f32[128,128]{1,0:T(8,128)S(1)}, f32[128,128]{1,0:T(8,128)S(1)}, u32[]{:S(2)}, u32[]{:S(2)}) collective-permute-start(f32[128,128]{1,0:T(8,128)S(1)} %get-tuple-element.51.low_sent), channel_id=1, source_target_pairs={{0,1},{1,0},{2,3},{3,2},{4,5},{5,4},{6,7},{7,6},{8,9},{9,8},{10,11... | collective-permute-start | bytes 196616 | tf_op jit(solution)/shard_map/ppermute | solution.py:344
  35.8 18.1 %collective-permute-start.6 = (f32[128,128]{1,0:T(8,128)S(1)}, f32[128,128]{1,0:T(8,128)S(1)}, u32[]{:S(2)}, u32[]{:S(2)}) collective-permute-start(f32[128,128]{1,0:T(8,128)S(1)} %get-tuple-element.55), channel_id=1, source_target_pairs={{1,2},{3,4},{5,6},{7,8},{9,10},{11,12},{13,14},{15,16},{17,18},{19... | collective-permute-start | bytes 196616 | tf_op jit(solution)/shard_map/ppermute | solution.py:343
  36.4 17.5 %collective-permute-start.7 = (f32[128,128]{1,0:T(8,128)S(1)}, f32[128,128]{1,0:T(8,128)S(1)}, u32[]{:S(2)}, u32[]{:S(2)}) collective-permute-start(f32[128,128]{1,0:T(8,128)S(1)} %get-tuple-element.52), channel_id=1, source_target_pairs={{0,1},{1,0},{2,3},{3,2},{4,5},{5,4},{6,7},{7,6},{8,9},{9,8},{10,11... | collective-permute-start | bytes 196616 | tf_op jit(solution)/shard_map/ppermute | solution.py:344
  43.7 43.0 %collective-permute-start.10 = (f32[18,128,128]{2,1,0:T(8,128)S(1)}, f32[18,128,128]{2,1,0:T(8,128)S(1)}, u32[]{:S(2)}, u32[]{:S(2)}) collective-permute-start(f32[18,128,128]{2,1,0:T(8,128)S(1)} %get-tuple-element.59.m0_ref), channel_id=1, source_target_pairs={{0,64},{64,0},{128,192},{192,128},{256,320},{320,256},{384,448},{4... | collective-permute-start | bytes 3538952 | tf_op jit(solution)/shard_map/ppermute | solution.py:367
  50.9 35.9 %collective-permute-start.11 = (f32[18,128,128]{2,1,0:T(8,128)S(1)}, f32[18,128,128]{2,1,0:T(8,128)S(1)}, u32[]{:S(2)}, u32[]{:S(2)}) collective-permute-start(f32[18,128,128]{2,1,0:T(8,128)S(1)} %get-tuple-element.60.m1_ref), channel_id=1, source_target_pairs={{64,128},{192,256},{320,384},{128,64},{256,192},{384,320},{65,129}... | collective-permute-start | bytes 3538952 | tf_op jit(solution)/shard_map/ppermute | solution.py:366
  80.8 6.7 %collective-permute-start.9 = (f32[128,128]{1,0:T(8,128)S(1)}, f32[128,128]{1,0:T(8,128)S(1)}, u32[]{:S(2)}, u32[]{:S(2)}) collective-permute-start(f32[128,128]{1,0:T(8,128)S(1)} %get-tuple-element.58), channel_id=1, source_target_pairs={{0,64},{64,0},{128,192},{192,128},{256,320},{320,256},{384,448},{4... | collective-permute-start | bytes 196616 | tf_op jit(solution)/shard_map/ppermute | solution.py:380
  82.7 6.0 %collective-permute-start.8 = (f32[128,128]{1,0:T(8,128)S(1)}, f32[128,128]{1,0:T(8,128)S(1)}, u32[]{:S(2)}, u32[]{:S(2)}) collective-permute-start(f32[128,128]{1,0:T(8,128)S(1)} %get-tuple-element.58), channel_id=1, source_target_pairs={{64,128},{192,256},{320,384},{128,64},{256,192},{384,320},{65,129}... | collective-permute-start | bytes 196616 | tf_op jit(solution)/shard_map/ppermute | solution.py:379

commit v6 on v5

--- a/solution.py
+++ b/solution.py
@@ -123,26 +123,7 @@
         copy.wait()
 
 
-def messages(low_ref, high_ref, up, down):
-    n = up.shape[0]
-    sector = odd("blk")
-    low_ref[:n, :] = jnp.where(sector, down, up)
-    high_ref[:n, :] = jnp.where(sector, up, down)
-
-
-def received(low_ref, high_ref):
-    n = low_ref.shape[1]
-    low, high = low_ref[:n, :], high_ref[:n, :]
-    sector = odd("blk")
-    return jnp.where(sector, low, high), jnp.where(sector, high, low)
-
-
-def sent_down(low_ref, high_ref):
-    n = low_ref.shape[1]
-    return jnp.where(odd("blk"), low_ref[:n, :], high_ref[:n, :])
-
-
-def first_adjoint(own_ref, m0_ref, m1_ref, lt_ref, rc_ref, dlt_ref, drc_ref, low_ref, high_ref):
+def first_adjoint(own_ref, m0_ref, m1_ref, lt_ref, rc_ref, dlt_ref, drc_ref, b_ref):
     n = own_ref.shape[1]
     diags = dlt_ref.shape[0] // n
     segment = odd("seg")
@@ -151,60 +132,48 @@
         k = c if c < diags else c - diags
         put_parts(dlt_ref if c < diags else lt_ref, k, n, jnp.where(segment, y, x).T)
         put_parts(drc_ref if c < diags else rc_ref, k, n, jnp.where(segment, x, y))
-    v = own_ref[:n, :]
-    messages(low_ref, high_ref, v, sandwich(lt_ref, rc_ref, v))
-    low_ref[n:, :] = own_ref[n:, :]
-    high_ref[n:, :] = own_ref[n:, :]
-
-
-def applied_here(size, v, below, lt_ref, rc_ref, dlt_ref, drc_ref):
+    b_ref[...] = sandwich(lt_ref, rc_ref, own_ref[:n, :])
+
+
+def adjoint(own_ref, a_ref, got_b_ref, lt_ref, rc_ref, v_ref, b_ref):
+    n = own_ref.shape[1]
+    v = a_ref[...] - where(square_mask(own_ref[n : n + 1, :]), got_b_ref[...])
+    v_ref[...] = v
+    b_ref[...] = sandwich(lt_ref, rc_ref, v)
+
+
+def own_part(own_ref, v, below, lt_ref, rc_ref, dlt_ref, drc_ref):
+    n = own_ref.shape[1]
     hop = sandwich(rc_ref, lt_ref, below.T)
     diag = sandwich(drc_ref, dlt_ref, v.T)
-    return where(square_mask(size), (hop + diag).T)
-
-
-def first_round(own_ref, high_in, low_in, lt_ref, rc_ref, dlt_ref, drc_ref, size_ref, v_ref, low_ref, high_ref):
-    n = own_ref.shape[1]
-    size = own_ref[n : n + 1, :]
-    below, above = received(low_in, high_in)
-    size_ref[...] = jnp.where(odd("blk"), low_in[n:, :], high_in[n:, :])
+    return where(square_mask(own_ref[n : n + 1, :]), (hop + diag).T)
+
+
+def first_apply(own_ref, below_ref, lt_ref, rc_ref, dlt_ref, drc_ref, a_ref):
+    n = own_ref.shape[1]
     v = own_ref[:n, :]
-    a = SHIFT * v - applied_here(size, v, below, lt_ref, rc_ref, dlt_ref, drc_ref)
-    v = a - where(square_mask(size), above)
-    v_ref[...] = v
-    messages(low_ref, high_ref, a, sandwich(lt_ref, rc_ref, v))
-
-
-def later_round(
-    own_ref, v_ref, high_in, low_in, low_sent, high_sent, size_ref, lt_ref, rc_ref, dlt_ref, drc_ref, new_ref, low_ref, high_ref
-):
-    n = own_ref.shape[1]
-    size = own_ref[n : n + 1, :]
-    below, above = received(low_in, high_in)
-    below = where(square_mask(size_ref[0:1, :]), below - sent_down(low_sent, high_sent))
+    a_ref[...] = SHIFT * v - own_part(own_ref, v, below_ref[:n, :], lt_ref, rc_ref, dlt_ref, drc_ref)
+
+
+def later_apply(last, own_ref, below_ref, v_ref, got_a_ref, b_ref, lt_ref, rc_ref, dlt_ref, drc_ref, a_ref):
+    n = own_ref.shape[1]
+    below = where(square_mask(below_ref[n : n + 1, :]), got_a_ref[...] - b_ref[...])
     v = v_ref[...]
-    a = SHIFT * v - applied_here(size, v, below, lt_ref, rc_ref, dlt_ref, drc_ref)
-    v = a - where(square_mask(size), above)
-    new_ref[...] = v
-    messages(low_ref, high_ref, a, sandwich(lt_ref, rc_ref, v))
+    part = own_part(own_ref, v, below, lt_ref, rc_ref, dlt_ref, drc_ref)
+    a_ref[...] = part if last else SHIFT * v - part
 
 
 def total_of(x):
     return jnp.sum(jnp.sum(x, axis=0, keepdims=True), axis=1, keepdims=True)
 
 
-def last_round(
-    rank_ref, own_ref, v_ref, high_in, low_in, low_sent, high_sent, size_ref, lt_ref, rc_ref, dlt_ref, drc_ref, v4_ref, sums_ref
-):
-    n = own_ref.shape[1]
-    size = own_ref[n : n + 1, :]
-    below, above = received(low_in, high_in)
-    below = where(square_mask(size_ref[0:1, :]), below - sent_down(low_sent, high_sent))
+def finish(rank_ref, own_ref, v_ref, part_ref, got_b_ref, v4_ref, sums_ref):
+    n = own_ref.shape[1]
     v = v_ref[...]
-    applied = applied_here(size, v, below, lt_ref, rc_ref, dlt_ref, drc_ref) + where(square_mask(size), above)
+    applied = part_ref[...] + where(square_mask(own_ref[n : n + 1, :]), got_b_ref[...])
     v4 = SHIFT * v - applied
     v4_ref[:n, :] = v4
-    kept_cols = jnp.minimum(jnp.full((1, n), rank_ref[0, 0].astype(f32), f32), size)
+    kept_cols = jnp.minimum(jnp.full((1, n), rank_ref[0, 0].astype(f32), f32), own_ref[n : n + 1, :])
     v4_ref[n:, :] = jnp.broadcast_to(kept_cols, (8, n))
     lane = lax.broadcasted_iota(jnp.int32, (1, n), 1)
     row = jnp.where(lane == 0, total_of(v4 * v4), 0.0)
@@ -305,9 +274,8 @@
     dl, dr, hl, hr = diag_left[0, 0], diag_right[0, 0], hop_left[0, 0], hop_right[0, 0]
     hops, diags = hl.shape[0], dl.shape[0]
     blocks, segs = lax.axis_size("blk"), lax.axis_size("seg")
-    low_pairs = [(i, i ^ 1) for i in range(blocks)]
-    high_pairs = [(i, i + 1) for i in range(1, blocks - 1, 2)]
-    high_pairs += [(target, source) for source, target in high_pairs]
+    up = [(i, i + 1) for i in range(blocks - 1)]
+    down = [(i + 1, i) for i in range(blocks - 1)]
     chip = [(i, i ^ 1) for i in range(segs)]
     across = [(i, i + 1) for i in range(1, segs - 1, 2)]
     across += [(target, source) for source, target in across]
@@ -330,51 +298,40 @@
         limit=32,
         name="load",
     )
-    lt, rc, dlt, drc, low, high = call(
+    below0 = lax.ppermute(own, "blk", up)
+    lt, rc, dlt, drc, b = call(
         first_adjoint,
         (own, m0, m1),
         [VMEM] * 3,
-        [hop_parts, hop_parts, diag_parts, diag_parts, message, message],
+        [hop_parts, hop_parts, diag_parts, diag_parts, block],
         flops=channel * hops,
         name="first_adjoint",
     )
+    got_b = lax.ppermute(b, "blk", down)
     ops = (lt, rc, dlt, drc)
-    for k in range(ITERS):
-        high_in = lax.ppermute(high, "blk", high_pairs)
-        low_in = lax.ppermute(low, "blk", low_pairs)
-        sent = low, high
-        if k == 0:
-            size, v, low, high = call(
-                first_round,
-                (own, high_in, low_in, *ops),
-                [VMEM] * 7,
-                [SDS((8, n), f32), block, block, block],
-                flops=channel * (2 * hops + diags),
-                name="round0",
-            )
-        elif k < ITERS - 1:
-            v, low, high = call(
-                later_round,
-                (own, v, high_in, low_in, *before, size, *ops),
-                [VMEM] * 11,
-                [block, block, block],
-                flops=channel * (2 * hops + diags),
-                name=f"round{k}",
-            )
-        if k < ITERS - 1:
-            before = sent
-    x1 = lax.ppermute(lax.optimization_barrier((m1, sent[0]))[0], "seg", across)
-    x0 = lax.ppermute(lax.optimization_barrier((m0, sent[0]))[0], "seg", chip)
+    (a,) = call(first_apply, (own, below0, *ops), [VMEM] * 6, [block], flops=channel * (hops + diags), name="apply0")
+    for k in range(1, ITERS):
+        got_a = lax.ppermute(a, "blk", up)
+        last_b = b
+        v, b = call(
+            adjoint, (own, a, got_b, lt, rc), [VMEM] * 5, [block, block], flops=channel * hops, name=f"adjoint{k}"
+        )
+        got_b = lax.ppermute(b, "blk", down)
+        if k == ITERS - 1:
+            x1 = lax.ppermute(lax.optimization_barrier((m1, b))[0], "seg", across)
+            x0 = lax.ppermute(lax.optimization_barrier((m0, b))[0], "seg", chip)
+        (a,) = call(
+            functools.partial(later_apply, k == ITERS - 1),
+            (own, below0, v, got_a, last_b, *ops),
+            [VMEM] * 9,
+            [block],
+            flops=channel * (hops + diags),
+            name=f"apply{k}",
+        )
     sums_block = SDS((blocks, n), f32)
-    v4, sums = call(
-        last_round,
-        (lax.optimization_barrier((ranks, sent[0]))[0], own, v, high_in, low_in, *before, size, *ops),
-        [SMEM] + [VMEM] * 11,
-        [message, sums_block],
-        flops=channel * (hops + diags),
-        name="last_round",
-    )
-    sums = lax.all_to_all(sums, "blk", 0, 0, tiled=True)
+    v4, sums = call(finish, (ranks, own, v, a, got_b), [SMEM] + [VMEM] * 4, [message, sums_block], name="finish")
+    members = [(i + blocks // 2 + blocks // 16) % blocks for i in range(blocks)]
+    sums = lax.all_to_all(sums, "blk", 0, 0, tiled=True, axis_index_groups=[members])
     state, kept = call(normalise, (v4, sums), [VMEM] * 2, [block, block], name="normalise")
     kept1 = lax.ppermute(kept, "seg", across)
     kept0 = lax.ppermute(kept, "seg", chip)

time: 91.6 us -> 82.5 us (0.901)
  starting transfers between devices: 44.2 us -> 36.8 us
  waiting for transfers between devices: 6.12 us -> 0.48 us
  blocking collectives: 25.6 us -> 29.4 us
    ppermute x10, starting transfers between devices: 38.2 us -> 30.8 us  [the longest x3 12.7 us: shards(): got_a = lax.ppermute(a, 'blk', up)]
    ppermute x10, waiting for transfers between devices: 4.95 us -> 0.03 us  [the longest x4 0.01 us: shards(): got_b = lax.ppermute(b, 'blk', down)]
    all_to_all x1, blocking collectives: 25.6 us -> 29.4 us  [shards(): lax.all_to_all(sums, 'blk', 0, 0, tiled=True, axis_index_groups=[members])]
    ppermute x1, waiting for transfers between devices: 1.17 us -> 0.01 us  [shards(): kept1 = lax.ppermute(kept, 'seg', across)]
    pallas_call x9 -> x13, Pallas kernels: 13.1 us -> 13.2 us  [call(): pl.pallas_call(kernel, in_specs=specs, out_specs=out_specs or [VMEM] * le...]
  transfers between devices with their start and end apart: 12 -> 12, of which waited for: 4 -> 1; matrix products, arithmetic and copies ran while one was open for 0% -> 0% of each run, Pallas kernels for 2% -> 11%
where the time goes in v6:
time: 82.5 us; the launch traced here: 82 us
  starting transfers between devices  36.8 us (45%)
  blocking collectives  29.4 us (36%)
  Pallas kernels  13.2 us (16%)
  between operations  2.19 us (3%)
    all_to_all x1, blocking collectives, shards(): lax.all_to_all(sums, 'blk', 0, 0, tiled=True, axis_index_groups=[members])  29.4 us
    pallas_call x13, Pallas kernels, call(): pl.pallas_call(kernel, in_specs=specs, out_specs=out_specs or [VMEM] * le...  13.2 us
    ppermute x3, starting transfers between devices, shards(): got_a = lax.ppermute(a, 'blk', up)  12.7 us
    ppermute x1, starting transfers between devices, shards(): x0 = lax.ppermute(lax.optimization_barrier((m0, b))[0], 'seg', chip)  6.99 us
    ppermute x4, starting transfers between devices, shards(): got_b = lax.ppermute(b, 'blk', down)  5.17 us
    ppermute x1, starting transfers between devices, shards(): below0 = lax.ppermute(own, 'blk', up)  4.03 us
    ppermute x1, starting transfers between devices, shards(): kept1 = lax.ppermute(kept, 'seg', across)  4.03 us
    ppermute x1, starting transfers between devices, shards(): x1 = lax.ppermute(lax.optimization_barrier((m1, b))[0], 'seg', across)  1.92 us
  transfers between devices with their start and end apart: 12, of which 1 were waited for; matrix products, arithmetic and copies ran while one was open for 0% of the time, Pallas kernels for 11%

profile of v6, /device:TPU:1, one launch (start us, length us, event | category | flops | bytes accessed | tf_op | source)
XLA Modules:
  0.0 82.0 jit_solution(11849219658651625844)
XLA Ops:
  1.3 1.7 %load.1 = (f32[136,128]{1,0:T(8,128)S(1)}, f32[18,128,128]{2,1,0:T(8,128)S(1)}, f32[18,128,128]{2,1,0:T(8,128)S(1)}) custom-call(s32[1,1]{1,0:T(1,128)S(6)} %copy.12.size_ref, f32[128,128]{1,0:T(8,128)} %bitcast.19, f32[2,128,128]{2,1,0:T(8,128)} %bitcast.17, f32[16,128,128]{2,1,0:T(8,128)} %bitcast.15, f32[2,128,128]{2,1,0:T(8,128)} %bitcast.18, ...), custom_call_target="tpu_custom_call" | custom-call | bytes 4853764 | tf_op jit(solution)/shard_map/load/pallas_call | solution.py:259
  3.0 4.0 %collective-permute-start = (f32[136,128]{1,0:T(8,128)S(1)}, f32[136,128]{1,0:T(8,128)S(1)}, u32[]{:S(2)}, u32[]{:S(2)}) collective-permute-start(f32[136,128]{1,0:T(8,128)S(1)} %get-tuple-element.30.own_ref), channel_id=1, source_target_pairs={{0,1},{1,2},{2,3},{3,4},{4,5},{5,6},{6,7},{7,8},{8,9},{9,10},{10,1... | collective-permute-start | bytes 208904 | tf_op jit(solution)/shard_map/ppermute | solution.py:301
  7.1 1.0 %first_adjoint.1 = (bf16[2048,256]{1,0:T(8,128)(2,1)S(1)}, bf16[2048,256]{1,0:T(8,128)(2,1)S(1)}, bf16[256,256]{1,0:T(8,128)(2,1)S(1)}, bf16[256,256]{1,0:T(8,128)(2,1)S(1)}, f32[128,128]{1,0:T(8,128)S(1)}) custom-call(f32[136,128]{1,0:T(8,128)S(1)} %get-tuple-element.30.own_ref, f32[18,128,128]{2,1,0:T(8,128)S(1)} %get-tuple-element.47.m0_ref, ...), custom_call_target="tpu_custom_call" | custom-call | flops 10737418240 | bytes 4853760 | tf_op jit(solution)/shard_map/first_adjoint/pallas_call | solution.py:259
  8.1 1.3 %collective-permute-start.1 = (f32[128,128]{1,0:T(8,128)S(1)}, f32[128,128]{1,0:T(8,128)S(1)}, u32[]{:S(2)}, u32[]{:S(2)}) collective-permute-start(f32[128,128]{1,0:T(8,128)S(1)} %get-tuple-element.37.b_ref), channel_id=1, source_target_pairs={{1,0},{2,1},{3,2},{4,3},{5,4},{6,5},{7,6},{8,7},{9,8},{10,9},{11,1... | collective-permute-start | bytes 196616 | tf_op jit(solution)/shard_map/ppermute | solution.py:310
  10.0 0.0 collective-permute-done.below_ref
  10.1 1.0 %apply0.1.a_ref = f32[128,128]{1,0:T(8,128)S(1)} custom-call(f32[136,128]{1,0:T(8,128)S(1)} %get-tuple-element.30.own_ref, f32[136,128]{1,0:T(8,128)S(1)} %collective-permute-done.below_ref, bf16[2048,256]{1,0:T(8,128)(2,1)S(1)} %get-tuple-element.33.lt_ref, bf16[2048,256]{1,0:T(8,128)(2,1)S(1)} %get-tuple-element.34.rc_ref, ...), custom_call_target="tpu_custom_call" | custom-call | flops 12079595520 | bytes 2564096 | tf_op jit(solution)/shard_map/apply0/pallas_call | solution.py:259
  11.1 4.0 %collective-permute-start.2 = (f32[128,128]{1,0:T(8,128)S(1)}, f32[128,128]{1,0:T(8,128)S(1)}, u32[]{:S(2)}, u32[]{:S(2)}) collective-permute-start(f32[128,128]{1,0:T(8,128)S(1)} %apply0.1.a_ref), channel_id=1, source_target_pairs={{0,1},{1,2},{2,3},{3,4},{4,5},{5,6},{6,7},{7,8},{8,9},{9,10},{10,1... | collective-permute-start | bytes 196616 | tf_op jit(solution)/shard_map/ppermute | solution.py:314
  15.1 0.0 collective-permute-done.1.got_b_ref
  15.1 0.9 %adjoint1.1 = (f32[128,128]{1,0:T(8,128)S(1)}, f32[128,128]{1,0:T(8,128)S(1)}) custom-call(f32[136,128]{1,0:T(8,128)S(1)} %get-tuple-element.30.own_ref, f32[128,128]{1,0:T(8,128)S(1)} %apply0.1.a_ref, f32[128,128]{1,0:T(8,128)S(1)} %collective-permute-done.1.got_b_ref, bf16[2048,256]{1,0:T(8,128)(2,1)S(1)} %get-tuple-element.33.lt_ref, ...), custom_call_target="tpu_custom_call" | custom-call | flops 10737418240 | bytes 2428928 | tf_op jit(solution)/shard_map/adjoint1/pallas_call | solution.py:259
  16.1 1.3 %collective-permute-start.3 = (f32[128,128]{1,0:T(8,128)S(1)}, f32[128,128]{1,0:T(8,128)S(1)}, u32[]{:S(2)}, u32[]{:S(2)}) collective-permute-start(f32[128,128]{1,0:T(8,128)S(1)} %get-tuple-element.39.b_ref), channel_id=1, source_target_pairs={{1,0},{2,1},{3,2},{4,3},{5,4},{6,5},{7,6},{8,7},{9,8},{10,9},{11,1... | collective-permute-start | bytes 196616 | tf_op jit(solution)/shard_map/ppermute | solution.py:319
  17.4 0.0 collective-permute-done.2.got_a_ref
  17.4 1.0 %apply1.1.a_ref = f32[128,128]{1,0:T(8,128)S(1)} custom-call(f32[136,128]{1,0:T(8,128)S(1)} %get-tuple-element.30.own_ref, f32[136,128]{1,0:T(8,128)S(1)} %collective-permute-done.below_ref, f32[128,128]{1,0:T(8,128)S(1)} %get-tuple-element.38.v_ref, f32[128,128]{1,0:T(8,128)S(1)} %collective-permute-done.2.got_a_ref, ...), custom_call_target="tpu_custom_call" | custom-call | flops 12079595520 | bytes 2760704 | tf_op jit(solution)/shard_map/apply1/pallas_call | solution.py:259
  18.4 4.0 %collective-permute-start.4 = (f32[128,128]{1,0:T(8,128)S(1)}, f32[128,128]{1,0:T(8,128)S(1)}, u32[]{:S(2)}, u32[]{:S(2)}) collective-permute-start(f32[128,128]{1,0:T(8,128)S(1)} %apply1.1.a_ref), channel_id=1, source_target_pairs={{0,1},{1,2},{2,3},{3,4},{4,5},{5,6},{6,7},{7,8},{8,9},{9,10},{10,1... | collective-permute-start | bytes 196616 | tf_op jit(solution)/shard_map/ppermute | solution.py:314
  22.4 0.0 collective-permute-done.3.got_b_ref
  22.4 0.9 %adjoint2.1 = (f32[128,128]{1,0:T(8,128)S(1)}, f32[128,128]{1,0:T(8,128)S(1)}) custom-call(f32[136,128]{1,0:T(8,128)S(1)} %get-tuple-element.30.own_ref, f32[128,128]{1,0:T(8,128)S(1)} %apply1.1.a_ref, f32[128,128]{1,0:T(8,128)S(1)} %collective-permute-done.3.got_b_ref, bf16[2048,256]{1,0:T(8,128)(2,1)S(1)} %get-tuple-element.33.lt_ref, ...), custom_call_target="tpu_custom_call" | custom-call | flops 10737418240 | bytes 2428928 | tf_op jit(solution)/shard_map/adjoint2/pallas_call | solution.py:259
  23.4 1.3 %collective-permute-start.5 = (f32[128,128]{1,0:T(8,128)S(1)}, f32[128,128]{1,0:T(8,128)S(1)}, u32[]{:S(2)}, u32[]{:S(2)}) collective-permute-start(f32[128,128]{1,0:T(8,128)S(1)} %get-tuple-element.41.b_ref), channel_id=1, source_target_pairs={{1,0},{2,1},{3,2},{4,3},{5,4},{6,5},{7,6},{8,7},{9,8},{10,9},{11,1... | collective-permute-start | bytes 196616 | tf_op jit(solution)/shard_map/ppermute | solution.py:319
  24.7 0.0 collective-permute-done.4.got_a_ref
  24.7 1.0 %apply2.1.a_ref = f32[128,128]{1,0:T(8,128)S(1)} custom-call(f32[136,128]{1,0:T(8,128)S(1)} %get-tuple-element.30.own_ref, f32[136,128]{1,0:T(8,128)S(1)} %collective-permute-done.below_ref, f32[128,128]{1,0:T(8,128)S(1)} %get-tuple-element.40.v_ref, f32[128,128]{1,0:T(8,128)S(1)} %collective-permute-done.4.got_a_ref, ...), custom_call_target="tpu_custom_call" | custom-call | flops 12079595520 | bytes 2760704 | tf_op jit(solution)/shard_map/apply2/pallas_call | solution.py:259
  25.7 4.7 %collective-permute-start.6 = (f32[128,128]{1,0:T(8,128)S(1)}, f32[128,128]{1,0:T(8,128)S(1)}, u32[]{:S(2)}, u32[]{:S(2)}) collective-permute-start(f32[128,128]{1,0:T(8,128)S(1)} %apply2.1.a_ref), channel_id=1, source_target_pairs={{0,1},{1,2},{2,3},{3,4},{4,5},{5,6},{6,7},{7,8},{8,9},{9,10},{10,1... | collective-permute-start | bytes 196616 | tf_op jit(solution)/shard_map/ppermute | solution.py:314
  30.5 0.0 collective-permute-done.5.got_b_ref
  30.5 0.9 %adjoint3.1 = (f32[128,128]{1,0:T(8,128)S(1)}, f32[128,128]{1,0:T(8,128)S(1)}) custom-call(f32[136,128]{1,0:T(8,128)S(1)} %get-tuple-element.30.own_ref, f32[128,128]{1,0:T(8,128)S(1)} %apply2.1.a_ref, f32[128,128]{1,0:T(8,128)S(1)} %collective-permute-done.5.got_b_ref, bf16[2048,256]{1,0:T(8,128)(2,1)S(1)} %get-tuple-element.33.lt_ref, ...), custom_call_target="tpu_custom_call" | custom-call | flops 10737418240 | bytes 2428928 | tf_op jit(solution)/shard_map/adjoint3/pallas_call | solution.py:259
  31.4 1.3 %collective-permute-start.7 = (f32[128,128]{1,0:T(8,128)S(1)}, f32[128,128]{1,0:T(8,128)S(1)}, u32[]{:S(2)}, u32[]{:S(2)}) collective-permute-start(f32[128,128]{1,0:T(8,128)S(1)} %get-tuple-element.43), channel_id=1, source_target_pairs={{1,0},{2,1},{3,2},{4,3},{5,4},{6,5},{7,6},{8,7},{9,8},{10,9},{11,1... | collective-permute-start | bytes 196616 | tf_op jit(solution)/shard_map/ppermute | solution.py:319
  32.7 7.0 %collective-permute-start.10 = (f32[18,128,128]{2,1,0:T(8,128)S(1)}, f32[18,128,128]{2,1,0:T(8,128)S(1)}, u32[]{:S(2)}, u32[]{:S(2)}) collective-permute-start(f32[18,128,128]{2,1,0:T(8,128)S(1)} %get-tuple-element.47.m0_ref), channel_id=1, source_target_pairs={{0,64},{64,0},{128,192},{192,128},{256,320},{320,256},{384,448},{4... | collective-permute-start | bytes 3538952 | tf_op jit(solution)/shard_map/ppermute | solution.py:322
  39.7 1.9 %collective-permute-start.11 = (f32[18,128,128]{2,1,0:T(8,128)S(1)}, f32[18,128,128]{2,1,0:T(8,128)S(1)}, u32[]{:S(2)}, u32[]{:S(2)}) collective-permute-start(f32[18,128,128]{2,1,0:T(8,128)S(1)} %get-tuple-element.48.m1_ref), channel_id=1, source_target_pairs={{64,128},{192,256},{320,384},{128,64},{256,192},{384,320},{65,129}... | collective-permute-start | bytes 3538952 | tf_op jit(solution)/shard_map/ppermute | solution.py:321
  41.6 0.0 collective-permute-done.6.got_a_ref
  41.7 1.0 %apply3.1.part_ref = f32[128,128]{1,0:T(8,128)S(1)} custom-call(f32[136,128]{1,0:T(8,128)S(1)} %get-tuple-element.30.own_ref, f32[136,128]{1,0:T(8,128)S(1)} %collective-permute-done.below_ref, f32[128,128]{1,0:T(8,128)S(1)} %get-tuple-element.42.v_ref, f32[128,128]{1,0:T(8,128)S(1)} %collective-permute-done.6.got_a_ref, ...), custom_call_target="tpu_custom_call" | custom-call | flops 12079595520 | bytes 2760704 | tf_op jit(solution)/shard_map/apply3/pallas_call | solution.py:259
  42.7 0.0 collective-permute-done.7.got_b_ref
  42.7 0.1 finish.1
  42.8 29.4 %all_to_all.11 = f32[64,1,128]{2,1,0:T(1,128)S(1)} all-to-all(f32[64,1,128]{2,1,0:T(1,128)S(1)} %bitcast.14), channel_id=1, replica_groups={{36,37,38,39,40,41,42,43,44,45,46,47,48,49,50,51,52,53,54,55,56,57,58,5..., dimensions={0} | all-to-all | bytes 65536 | tf_op jit(solution)/shard_map/all_to_all | solution.py:334
  72.2 0.1 normalise.1
  72.4 4.0 %collective-permute-start.8 = (f32[128,128]{1,0:T(8,128)S(1)}, f32[128,128]{1,0:T(8,128)S(1)}, u32[]{:S(2)}, u32[]{:S(2)}) collective-permute-start(f32[128,128]{1,0:T(8,128)S(1)} %get-tuple-element.46), channel_id=1, source_target_pairs={{64,128},{192,256},{320,384},{128,64},{256,192},{384,320},{65,129}... | collective-permute-start | bytes 196616 | tf_op jit(solution)/shard_map/ppermute | solution.py:336
  76.4 1.9 %collective-permute-start.9 = (f32[128,128]{1,0:T(8,128)S(1)}, f32[128,128]{1,0:T(8,128)S(1)}, u32[]{:S(2)}, u32[]{:S(2)}) collective-permute-start(f32[128,128]{1,0:T(8,128)S(1)} %get-tuple-element.46), channel_id=1, source_target_pairs={{0,64},{64,0},{128,192},{192,128},{256,320},{320,256},{384,448},{4... | collective-permute-start | bytes 196616 | tf_op jit(solution)/shard_map/ppermute | solution.py:337
  78.3 0.0 collective-permute-done.10.x0_ref
  78.3 0.0 collective-permute-done.11.x1_ref
  78.3 0.7 parts.1
  79.1 0.0 collective-permute-done.8.kept1_ref
  79.1 0.5 collective-permute-done.9.kept0_ref
  79.5 2.5 %extend.1 = (f32[128,128]{1,0:T(8,128)}, f32[18,128,128]{2,1,0:T(8,128)}, f32[18,128,128]{2,1,0:T(8,128)}) custom-call(f32[128,128]{1,0:T(8,128)S(1)} %collective-permute-done.8.kept1_ref, f32[128,128]{1,0:T(8,128)S(1)} %collective-permute-done.9.kept0_ref, bf16[2304,256]{1,0:T(8,128)(2,1)S(1)} %get-tuple-element.49.p0_ref, ...), custom_call_target="tpu_custom_call" | custom-call | flops 24159191040 | bytes 4980736 | tf_op jit(solution)/shard_map/extend/pallas_call | solution.py:259
Async XLA Ops:
  3.0 7.0 %collective-permute-start = (f32[136,128]{1,0:T(8,128)S(1)}, f32[136,128]{1,0:T(8,128)S(1)}, u32[]{:S(2)}, u32[]{:S(2)}) collective-permute-start(f32[136,128]{1,0:T(8,128)S(1)} %get-tuple-element.30.own_ref), channel_id=1, source_target_pairs={{0,1},{1,2},{2,3},{3,4},{4,5},{5,6},{6,7},{7,8},{8,9},{9,10},{10,1... | collective-permute-start | bytes 208904 | tf_op jit(solution)/shard_map/ppermute | solution.py:301
  8.1 7.0 %collective-permute-start.1 = (f32[128,128]{1,0:T(8,128)S(1)}, f32[128,128]{1,0:T(8,128)S(1)}, u32[]{:S(2)}, u32[]{:S(2)}) collective-permute-start(f32[128,128]{1,0:T(8,128)S(1)} %get-tuple-element.37.b_ref), channel_id=1, source_target_pairs={{1,0},{2,1},{3,2},{4,3},{5,4},{6,5},{7,6},{8,7},{9,8},{10,9},{11,1... | collective-permute-start | bytes 196616 | tf_op jit(solution)/shard_map/ppermute | solution.py:310
  11.1 6.3 %collective-permute-start.2 = (f32[128,128]{1,0:T(8,128)S(1)}, f32[128,128]{1,0:T(8,128)S(1)}, u32[]{:S(2)}, u32[]{:S(2)}) collective-permute-start(f32[128,128]{1,0:T(8,128)S(1)} %apply0.1.a_ref), channel_id=1, source_target_pairs={{0,1},{1,2},{2,3},{3,4},{4,5},{5,6},{6,7},{7,8},{8,9},{9,10},{10,1... | collective-permute-start | bytes 196616 | tf_op jit(solution)/shard_map/ppermute | solution.py:314
  16.1 6.4 %collective-permute-start.3 = (f32[128,128]{1,0:T(8,128)S(1)}, f32[128,128]{1,0:T(8,128)S(1)}, u32[]{:S(2)}, u32[]{:S(2)}) collective-permute-start(f32[128,128]{1,0:T(8,128)S(1)} %get-tuple-element.39.b_ref), channel_id=1, source_target_pairs={{1,0},{2,1},{3,2},{4,3},{5,4},{6,5},{7,6},{8,7},{9,8},{10,9},{11,1... | collective-permute-start | bytes 196616 | tf_op jit(solution)/shard_map/ppermute | solution.py:319
  18.4 6.3 %collective-permute-start.4 = (f32[128,128]{1,0:T(8,128)S(1)}, f32[128,128]{1,0:T(8,128)S(1)}, u32[]{:S(2)}, u32[]{:S(2)}) collective-permute-start(f32[128,128]{1,0:T(8,128)S(1)} %apply1.1.a_ref), channel_id=1, source_target_pairs={{0,1},{1,2},{2,3},{3,4},{4,5},{5,6},{6,7},{7,8},{8,9},{9,10},{10,1... | collective-permute-start | bytes 196616 | tf_op jit(solution)/shard_map/ppermute | solution.py:314
  23.4 7.1 %collective-permute-start.5 = (f32[128,128]{1,0:T(8,128)S(1)}, f32[128,128]{1,0:T(8,128)S(1)}, u32[]{:S(2)}, u32[]{:S(2)}) collective-permute-start(f32[128,128]{1,0:T(8,128)S(1)} %get-tuple-element.41.b_ref), channel_id=1, source_target_pairs={{1,0},{2,1},{3,2},{4,3},{5,4},{6,5},{7,6},{8,7},{9,8},{10,9},{11,1... | collective-permute-start | bytes 196616 | tf_op jit(solution)/shard_map/ppermute | solution.py:319
  25.7 15.9 %collective-permute-start.6 = (f32[128,128]{1,0:T(8,128)S(1)}, f32[128,128]{1,0:T(8,128)S(1)}, u32[]{:S(2)}, u32[]{:S(2)}) collective-permute-start(f32[128,128]{1,0:T(8,128)S(1)} %apply2.1.a_ref), channel_id=1, source_target_pairs={{0,1},{1,2},{2,3},{3,4},{4,5},{5,6},{6,7},{7,8},{8,9},{9,10},{10,1... | collective-permute-start | bytes 196616 | tf_op jit(solution)/shard_map/ppermute | solution.py:314
  31.4 11.3 %collective-permute-start.7 = (f32[128,128]{1,0:T(8,128)S(1)}, f32[128,128]{1,0:T(8,128)S(1)}, u32[]{:S(2)}, u32[]{:S(2)}) collective-permute-start(f32[128,128]{1,0:T(8,128)S(1)} %get-tuple-element.43), channel_id=1, source_target_pairs={{1,0},{2,1},{3,2},{4,3},{5,4},{6,5},{7,6},{8,7},{9,8},{10,9},{11,1... | collective-permute-start | bytes 196616 | tf_op jit(solution)/shard_map/ppermute | solution.py:319
  32.7 45.6 %collective-permute-start.10 = (f32[18,128,128]{2,1,0:T(8,128)S(1)}, f32[18,128,128]{2,1,0:T(8,128)S(1)}, u32[]{:S(2)}, u32[]{:S(2)}) collective-permute-start(f32[18,128,128]{2,1,0:T(8,128)S(1)} %get-tuple-element.47.m0_ref), channel_id=1, source_target_pairs={{0,64},{64,0},{128,192},{192,128},{256,320},{320,256},{384,448},{4... | collective-permute-start | bytes 3538952 | tf_op jit(solution)/shard_map/ppermute | solution.py:322
  39.7 38.6 %collective-permute-start.11 = (f32[18,128,128]{2,1,0:T(8,128)S(1)}, f32[18,128,128]{2,1,0:T(8,128)S(1)}, u32[]{:S(2)}, u32[]{:S(2)}) collective-permute-start(f32[18,128,128]{2,1,0:T(8,128)S(1)} %get-tuple-element.48.m1_ref), channel_id=1, source_target_pairs={{64,128},{192,256},{320,384},{128,64},{256,192},{384,320},{65,129}... | collective-permute-start | bytes 3538952 | tf_op jit(solution)/shard_map/ppermute | solution.py:321
  72.4 6.7 %collective-permute-start.8 = (f32[128,128]{1,0:T(8,128)S(1)}, f32[128,128]{1,0:T(8,128)S(1)}, u32[]{:S(2)}, u32[]{:S(2)}) collective-permute-start(f32[128,128]{1,0:T(8,128)S(1)} %get-tuple-element.46), channel_id=1, source_target_pairs={{64,128},{192,256},{320,384},{128,64},{256,192},{384,320},{65,129}... | collective-permute-start | bytes 196616 | tf_op jit(solution)/shard_map/ppermute | solution.py:336
  76.4 3.1 %collective-permute-start.9 = (f32[128,128]{1,0:T(8,128)S(1)}, f32[128,128]{1,0:T(8,128)S(1)}, u32[]{:S(2)}, u32[]{:S(2)}) collective-permute-start(f32[128,128]{1,0:T(8,128)S(1)} %get-tuple-element.46), channel_id=1, source_target_pairs={{0,64},{64,0},{128,192},{192,128},{256,320},{320,256},{384,448},{4... | collective-permute-start | bytes 196616 | tf_op jit(solution)/shard_map/ppermute | solution.py:337

commit v7 on v6

--- a/solution.py
+++ b/solution.py
@@ -123,7 +123,7 @@
         copy.wait()
 
 
-def first_adjoint(own_ref, m0_ref, m1_ref, lt_ref, rc_ref, dlt_ref, drc_ref, b_ref):
+def first_product(own_ref, m0_ref, m1_ref, lt_ref, rc_ref, dlt_ref, drc_ref, b_ref):
     n = own_ref.shape[1]
     diags = dlt_ref.shape[0] // n
     segment = odd("seg")
@@ -135,7 +135,30 @@
     b_ref[...] = sandwich(lt_ref, rc_ref, own_ref[:n, :])
 
 
-def adjoint(own_ref, a_ref, got_b_ref, lt_ref, rc_ref, v_ref, b_ref):
+def odd_adjoint(*refs):
+    pl.when(odd("blk"))(lambda: first_product(*refs))
+
+
+def even_adjoint(own_ref, m0_ref, m1_ref, done_ref, lt_ref, rc_ref, dlt_ref, drc_ref, b_ref):
+    @pl.when(odd("blk"))
+    def _():
+        b_ref[...] = done_ref[...]
+
+    @pl.when(jnp.logical_not(odd("blk")))
+    def _():
+        first_product(own_ref, m0_ref, m1_ref, lt_ref, rc_ref, dlt_ref, drc_ref, b_ref)
+
+
+def by_parity(kernel, count):
+    def chosen(*refs):
+        odd_ops, even_ops, rest = refs[:count], refs[count : 2 * count], refs[2 * count :]
+        pl.when(odd("blk"))(lambda: kernel(*odd_ops, *rest))
+        pl.when(jnp.logical_not(odd("blk")))(lambda: kernel(*even_ops, *rest))
+
+    return chosen
+
+
+def adjoint(lt_ref, rc_ref, own_ref, a_ref, got_b_ref, v_ref, b_ref):
     n = own_ref.shape[1]
     v = a_ref[...] - where(square_mask(own_ref[n : n + 1, :]), got_b_ref[...])
     v_ref[...] = v
@@ -149,13 +172,13 @@
     return where(square_mask(own_ref[n : n + 1, :]), (hop + diag).T)
 
 
-def first_apply(own_ref, below_ref, lt_ref, rc_ref, dlt_ref, drc_ref, a_ref):
+def first_apply(lt_ref, rc_ref, dlt_ref, drc_ref, own_ref, below_ref, a_ref):
     n = own_ref.shape[1]
     v = own_ref[:n, :]
     a_ref[...] = SHIFT * v - own_part(own_ref, v, below_ref[:n, :], lt_ref, rc_ref, dlt_ref, drc_ref)
 
 
-def later_apply(last, own_ref, below_ref, v_ref, got_a_ref, b_ref, lt_ref, rc_ref, dlt_ref, drc_ref, a_ref):
+def later_apply(last, lt_ref, rc_ref, dlt_ref, drc_ref, own_ref, below_ref, v_ref, got_a_ref, b_ref, a_ref):
     n = own_ref.shape[1]
     below = where(square_mask(below_ref[n : n + 1, :]), got_a_ref[...] - b_ref[...])
     v = v_ref[...]
@@ -196,61 +219,41 @@
     kept_ref[...] = where(cols < jnp.broadcast_to(v4_ref[n : n + 1, :], (n, n)), state)
 
 
-def parts(x0_ref, x1_ref, sums_ref, p0_ref, p1_ref, energy_ref):
+def parts(x0_ref, x1_ref, sums_ref, pl_ref, pr_ref, energy_ref):
     n = x0_ref.shape[1]
     segment = odd("seg")
     for c in range(x0_ref.shape[0]):
         x, y = x0_ref[c], x1_ref[c]
-        put_parts(p0_ref, c, n, jnp.where(segment, x.T, x))
-        put_parts(p1_ref, c, n, jnp.where(segment, y, y.T))
+        put_parts(pl_ref, c, n, jnp.where(segment, x, y).T)
+        put_parts(pr_ref, c, n, jnp.where(segment, y, x))
     total = jnp.sum(sums_ref[...], axis=0, keepdims=True)
     energy_ref[0] = jnp.sum(lane_of(total, 1) / lane_of(total, 2))
 
 
-def extend(
-    kept1_ref, kept0_ref, p0_ref, p1_ref, state_ref, new_ref, left_ref, right_ref, out0, out1, sems, state_sem
-):
+def extend(kept1_ref, kept0_ref, pl_ref, pr_ref, state_ref, new_ref, left_ref, right_ref, lo, ro, sems):
     n = kept0_ref.shape[0]
-    channels = out0.shape[0]
-    step = channels // CHUNKS
+    step = lo.shape[0] // CHUNKS
+    copies = [pltpu.make_async_copy(state_ref, new_ref, sems.at[0])]
+    copies[0].start()
     segment = odd("seg")
-    even = jnp.logical_not(segment)
-    state_copy = pltpu.make_async_copy(state_ref, new_ref, state_sem)
-    state_copy.start()
-    sides = []
-    for side, (kept_ref, p_ref, out, is_left) in enumerate(
-        ((kept0_ref, p0_ref, out0, segment), (kept1_ref, p1_ref, out1, even))
-    ):
-        kept = kept_ref[...]
-        sides.append((side, p_ref, out, weight(jnp.where(is_left, kept, kept.T))))
-
-    def copy(side, target, i):
+    x, y = kept0_ref[...], kept1_ref[...]
+    sides = (
+        (pl_ref, weight(jnp.where(segment, x, y)), lo, left_ref),
+        (pr_ref, weight(jnp.where(segment, y, x).T), ro, right_ref),
+    )
+    for i in range(CHUNKS):
         at = pl.ds(i * step, step)
-        return pltpu.make_async_copy((out0, out1)[side].at[at], target.at[at], sems.at[side, i])
-
-    for i in range(CHUNKS):
-        for side, p_ref, out, w in sides:
+        for side, (p_ref, w, out, target) in enumerate(sides):
             for c in range(i * step, (i + 1) * step, 2):
                 half = folded(dot(p_ref[pl.ds(c * n, 2 * n), :], w))
                 flip = jnp.concatenate([half[:n].T, half[n:].T], 0)
-                y = folded(dot(jnp.concatenate(split(flip), 1), w)) * (1.0 / math.sqrt(n))
-                out[c] = y[:n]
-                out[c + 1] = y[n:]
-
-        @pl.when(segment)
-        def _():
-            copy(0, left_ref, i).start()
-            copy(1, right_ref, i).start()
-
-        @pl.when(even)
-        def _():
-            copy(0, right_ref, i).start()
-            copy(1, left_ref, i).start()
-
-    for i in range(CHUNKS):
-        copy(0, left_ref, i).wait()
-        copy(1, right_ref, i).wait()
-    state_copy.wait()
+                z = folded(dot(jnp.concatenate(split(flip), 1), w)) * (1.0 / math.sqrt(n))
+                out[c] = z[:n]
+                out[c + 1] = z[n:]
+            copies.append(pltpu.make_async_copy(out.at[at], target.at[at], sems.at[1 + 2 * i + side]))
+            copies[-1].start()
+    for copy in copies:
+        copy.wait()
 
 
 def call(kernel, args, specs, outs, out_specs=None, scratch=(), flops=0, limit=16, name=None):
@@ -298,32 +301,42 @@
         limit=32,
         name="load",
     )
-    below0 = lax.ppermute(own, "blk", up)
-    lt, rc, dlt, drc, b = call(
-        first_adjoint,
-        (own, m0, m1),
-        [VMEM] * 3,
-        [hop_parts, hop_parts, diag_parts, diag_parts, block],
-        flops=channel * hops,
-        name="first_adjoint",
+    products = [hop_parts, hop_parts, diag_parts, diag_parts, block]
+    *odd_ops, b = call(odd_adjoint, (own, m0, m1), [VMEM] * 3, products, flops=channel * hops, name="odd_adjoint")
+    below0 = lax.ppermute(lax.optimization_barrier((own, b))[0], "blk", up)
+    *even_ops, b = call(
+        even_adjoint, (own, m0, m1, b), [VMEM] * 4, products, flops=channel * hops, name="even_adjoint"
     )
     got_b = lax.ppermute(b, "blk", down)
-    ops = (lt, rc, dlt, drc)
-    (a,) = call(first_apply, (own, below0, *ops), [VMEM] * 6, [block], flops=channel * (hops + diags), name="apply0")
+    ops = (*odd_ops, *even_ops)
+    hop_ops = (*odd_ops[:2], *even_ops[:2])
+    (a,) = call(
+        by_parity(first_apply, 4),
+        (*ops, own, below0),
+        [VMEM] * 10,
+        [block],
+        flops=channel * (hops + diags),
+        name="apply0",
+    )
     for k in range(1, ITERS):
         got_a = lax.ppermute(a, "blk", up)
         last_b = b
         v, b = call(
-            adjoint, (own, a, got_b, lt, rc), [VMEM] * 5, [block, block], flops=channel * hops, name=f"adjoint{k}"
+            by_parity(adjoint, 2),
+            (*hop_ops, own, a, got_b),
+            [VMEM] * 7,
+            [block, block],
+            flops=channel * hops,
+            name=f"adjoint{k}",
         )
         got_b = lax.ppermute(b, "blk", down)
         if k == ITERS - 1:
             x1 = lax.ppermute(lax.optimization_barrier((m1, b))[0], "seg", across)
             x0 = lax.ppermute(lax.optimization_barrier((m0, b))[0], "seg", chip)
         (a,) = call(
-            functools.partial(later_apply, k == ITERS - 1),
-            (own, below0, v, got_a, last_b, *ops),
-            [VMEM] * 9,
+            by_parity(functools.partial(later_apply, k == ITERS - 1), 4),
+            (*ops, own, below0, v, got_a, last_b),
+            [VMEM] * 13,
             [block],
             flops=channel * (hops + diags),
             name=f"apply{k}",
@@ -354,8 +367,7 @@
         scratch=[
             pltpu.VMEM(out.shape, f32),
             pltpu.VMEM(out.shape, f32),
-            pltpu.SemaphoreType.DMA((2, CHUNKS)),
-            pltpu.SemaphoreType.DMA,
+            pltpu.SemaphoreType.DMA((1 + 2 * CHUNKS,)),
         ],
         flops=2 * channel * (hops + diags),
         name="extend",

time: 82.5 us -> 81.9 us (level)
  blocking collectives: 29.4 us -> 28.4 us
    ppermute x1, starting transfers between devices: 4.03 us -> 5.06 us  [shards(): below0 = lax.ppermute(lax.optimization_barrier((own, b))[0], 'blk', up)]
    all_to_all x1, blocking collectives: 29.4 us -> 28.4 us  [shards(): lax.all_to_all(sums, 'blk', 0, 0, tiled=True, axis_index_groups=[members])]
    pallas_call x13 -> x14, Pallas kernels: 13.2 us -> 13.2 us  [call(): pl.pallas_call(kernel, in_specs=specs, out_specs=out_specs or [VMEM] * le...]
where the time goes in v7:
time: 81.9 us; the launch traced here: 81.4 us
  starting transfers between devices  36.9 us (45%)
  blocking collectives  28.4 us (35%)
  Pallas kernels  13.2 us (16%)
  between operations  2.36 us (3%)
    all_to_all x1, blocking collectives, shards(): lax.all_to_all(sums, 'blk', 0, 0, tiled=True, axis_index_groups=[members])  28.4 us
    pallas_call x14, Pallas kernels, call(): pl.pallas_call(kernel, in_specs=specs, out_specs=out_specs or [VMEM] * le...  13.2 us
    ppermute x3, starting transfers between devices, shards(): got_a = lax.ppermute(a, 'blk', up)  12 us
    ppermute x1, starting transfers between devices, shards(): x0 = lax.ppermute(lax.optimization_barrier((m0, b))[0], 'seg', chip)  6.7 us
    ppermute x4, starting transfers between devices, shards(): got_b = lax.ppermute(b, 'blk', down)  5.17 us
    ppermute x1, starting transfers between devices, shards(): below0 = lax.ppermute(lax.optimization_barrier((own, b))[0], 'blk', up)  5.06 us
    ppermute x1, starting transfers between devices, shards(): kept1 = lax.ppermute(kept, 'seg', across)  4.03 us
    ppermute x1, starting transfers between devices, shards(): x1 = lax.ppermute(lax.optimization_barrier((m1, b))[0], 'seg', across)  2.1 us
  transfers between devices with their start and end apart: 12, of which 1 were waited for; matrix products, arithmetic and copies ran while one was open for 0% of the time, Pallas kernels for 11%

profile of v7, /device:TPU:1, one launch (start us, length us, event | category | flops | bytes accessed | tf_op | source)
XLA Modules:
  0.0 81.4 jit_solution(17536115151921035171)
XLA Ops:
  1.3 1.7 %load.1 = (f32[136,128]{1,0:T(8,128)S(1)}, f32[18,128,128]{2,1,0:T(8,128)S(1)}, f32[18,128,128]{2,1,0:T(8,128)S(1)}) custom-call(s32[1,1]{1,0:T(1,128)S(6)} %copy.12.size_ref, f32[128,128]{1,0:T(8,128)} %bitcast.19, f32[2,128,128]{2,1,0:T(8,128)} %bitcast.17, f32[16,128,128]{2,1,0:T(8,128)} %bitcast.15, f32[2,128,128]{2,1,0:T(8,128)} %bitcast.18, ...), custom_call_target="tpu_custom_call" | custom-call | bytes 4853764 | tf_op jit(solution)/shard_map/load/pallas_call | solution.py:262
  3.1 5.1 %collective-permute-start = (f32[136,128]{1,0:T(8,128)S(1)}, f32[136,128]{1,0:T(8,128)S(1)}, u32[]{:S(2)}, u32[]{:S(2)}) collective-permute-start(f32[136,128]{1,0:T(8,128)S(1)} %get-tuple-element.48.refs_0_.own_ref.refs_8_.refs_4_), channel_id=1, source_target_pairs={{0,1},{1,2},{2,3},{3,4},{4,5},{5,6},{6,7},{7,8},{8,9},{9,10},{10,1... | collective-permute-start | bytes 208904 | tf_op jit(solution)/shard_map/ppermute | solution.py:306
  8.1 1.0 %even_adjoint.1 = (bf16[2048,256]{1,0:T(8,128)(2,1)S(1)}, bf16[2048,256]{1,0:T(8,128)(2,1)S(1)}, bf16[256,256]{1,0:T(8,128)(2,1)S(1)}, bf16[256,256]{1,0:T(8,128)(2,1)S(1)}, f32[128,128]{1,0:T(8,128)S(1)}) custom-call(f32[136,128]{1,0:T(8,128)S(1)} %get-tuple-element.48.refs_0_.own_ref.refs_8_.refs_4_, f32[18,128,128]{2,1,0:T(8,128)S(1)} %get-tuple-element.59.refs_1_.m0_ref, ...), custom_call_target="tpu_custom_call" | custom-call | flops 10737418240 | bytes 4919296 | tf_op jit(solution)/shard_map/even_adjoint/pallas_call | solution.py:262
  9.2 1.3 %collective-permute-start.1 = (f32[128,128]{1,0:T(8,128)S(1)}, f32[128,128]{1,0:T(8,128)S(1)}, u32[]{:S(2)}, u32[]{:S(2)}) collective-permute-start(f32[128,128]{1,0:T(8,128)S(1)} %get-tuple-element.49.refs_12_), channel_id=1, source_target_pairs={{1,0},{2,1},{3,2},{4,3},{5,4},{6,5},{7,6},{8,7},{9,8},{10,9},{11,1... | collective-permute-start | bytes 196616 | tf_op jit(solution)/shard_map/ppermute | solution.py:310
  11.1 0.0 collective-permute-done.refs_9_
  11.1 1.1 %apply0.1.refs_5_ = f32[128,128]{1,0:T(8,128)S(1)} custom-call(bf16[2048,256]{1,0:T(8,128)(2,1)S(1)} %get-tuple-element.39.refs_0_, bf16[2048,256]{1,0:T(8,128)(2,1)S(1)} %get-tuple-element.40.refs_1_, bf16[256,256]{1,0:T(8,128)(2,1)S(1)} %get-tuple-element.44.refs_2_, bf16[256,256]{1,0:T(8,128)(2,1)S(1)} %get-tuple-element.45.refs_3_, ...), custom_call_target="tpu_custom_call" | custom-call | flops 12079595520 | bytes 4923392 | tf_op jit(solution)/shard_map/apply0/pallas_call | solution.py:262
  12.2 4.0 %collective-permute-start.2 = (f32[128,128]{1,0:T(8,128)S(1)}, f32[128,128]{1,0:T(8,128)S(1)}, u32[]{:S(2)}, u32[]{:S(2)}) collective-permute-start(f32[128,128]{1,0:T(8,128)S(1)} %apply0.1.refs_5_), channel_id=1, source_target_pairs={{0,1},{1,2},{2,3},{3,4},{4,5},{5,6},{6,7},{7,8},{8,9},{9,10},{10,1... | collective-permute-start | bytes 196616 | tf_op jit(solution)/shard_map/ppermute | solution.py:322
  16.2 0.0 collective-permute-done.1.refs_6_
  16.2 0.9 %adjoint1.1 = (f32[128,128]{1,0:T(8,128)S(1)}, f32[128,128]{1,0:T(8,128)S(1)}) custom-call(bf16[2048,256]{1,0:T(8,128)(2,1)S(1)} %get-tuple-element.39.refs_0_, bf16[2048,256]{1,0:T(8,128)(2,1)S(1)} %get-tuple-element.40.refs_1_, bf16[2048,256]{1,0:T(8,128)(2,1)S(1)} %get-tuple-element.42.refs_4_.refs_2_, ...), custom_call_target="tpu_custom_call" | custom-call | flops 10737418240 | bytes 4526080 | tf_op jit(solution)/shard_map/adjoint1/pallas_call | solution.py:262
  17.1 1.3 %collective-permute-start.3 = (f32[128,128]{1,0:T(8,128)S(1)}, f32[128,128]{1,0:T(8,128)S(1)}, u32[]{:S(2)}, u32[]{:S(2)}) collective-permute-start(f32[128,128]{1,0:T(8,128)S(1)} %get-tuple-element.51.refs_12_), channel_id=1, source_target_pairs={{1,0},{2,1},{3,2},{4,3},{5,4},{6,5},{7,6},{8,7},{9,8},{10,9},{11,1... | collective-permute-start | bytes 196616 | tf_op jit(solution)/shard_map/ppermute | solution.py:332
  18.4 0.0 collective-permute-done.2.refs_11_
  18.5 1.1 %apply1.1.refs_5_ = f32[128,128]{1,0:T(8,128)S(1)} custom-call(bf16[2048,256]{1,0:T(8,128)(2,1)S(1)} %get-tuple-element.39.refs_0_, bf16[2048,256]{1,0:T(8,128)(2,1)S(1)} %get-tuple-element.40.refs_1_, bf16[256,256]{1,0:T(8,128)(2,1)S(1)} %get-tuple-element.44.refs_2_, bf16[256,256]{1,0:T(8,128)(2,1)S(1)} %get-tuple-element.45.refs_3_, ...), custom_call_target="tpu_custom_call" | custom-call | flops 12079595520 | bytes 5120000 | tf_op jit(solution)/shard_map/apply1/pallas_call | solution.py:262
  19.5 4.0 %collective-permute-start.4 = (f32[128,128]{1,0:T(8,128)S(1)}, f32[128,128]{1,0:T(8,128)S(1)}, u32[]{:S(2)}, u32[]{:S(2)}) collective-permute-start(f32[128,128]{1,0:T(8,128)S(1)} %apply1.1.refs_5_), channel_id=1, source_target_pairs={{0,1},{1,2},{2,3},{3,4},{4,5},{5,6},{6,7},{7,8},{8,9},{9,10},{10,1... | collective-permute-start | bytes 196616 | tf_op jit(solution)/shard_map/ppermute | solution.py:322
  23.5 0.0 collective-permute-done.3.refs_6_
  23.5 0.9 %adjoint2.1 = (f32[128,128]{1,0:T(8,128)S(1)}, f32[128,128]{1,0:T(8,128)S(1)}) custom-call(bf16[2048,256]{1,0:T(8,128)(2,1)S(1)} %get-tuple-element.39.refs_0_, bf16[2048,256]{1,0:T(8,128)(2,1)S(1)} %get-tuple-element.40.refs_1_, bf16[2048,256]{1,0:T(8,128)(2,1)S(1)} %get-tuple-element.42.refs_4_.refs_2_, ...), custom_call_target="tpu_custom_call" | custom-call | flops 10737418240 | bytes 4526080 | tf_op jit(solution)/shard_map/adjoint2/pallas_call | solution.py:262
  24.5 1.3 %collective-permute-start.5 = (f32[128,128]{1,0:T(8,128)S(1)}, f32[128,128]{1,0:T(8,128)S(1)}, u32[]{:S(2)}, u32[]{:S(2)}) collective-permute-start(f32[128,128]{1,0:T(8,128)S(1)} %get-tuple-element.53.refs_12_), channel_id=1, source_target_pairs={{1,0},{2,1},{3,2},{4,3},{5,4},{6,5},{7,6},{8,7},{9,8},{10,9},{11,1... | collective-permute-start | bytes 196616 | tf_op jit(solution)/shard_map/ppermute | solution.py:332
  25.8 0.0 collective-permute-done.4.refs_11_
  25.8 1.1 %apply2.1.refs_5_ = f32[128,128]{1,0:T(8,128)S(1)} custom-call(bf16[2048,256]{1,0:T(8,128)(2,1)S(1)} %get-tuple-element.39.refs_0_, bf16[2048,256]{1,0:T(8,128)(2,1)S(1)} %get-tuple-element.40.refs_1_, bf16[256,256]{1,0:T(8,128)(2,1)S(1)} %get-tuple-element.44.refs_2_, bf16[256,256]{1,0:T(8,128)(2,1)S(1)} %get-tuple-element.45.refs_3_, ...), custom_call_target="tpu_custom_call" | custom-call | flops 12079595520 | bytes 5120000 | tf_op jit(solution)/shard_map/apply2/pallas_call | solution.py:262
  26.9 4.0 %collective-permute-start.6 = (f32[128,128]{1,0:T(8,128)S(1)}, f32[128,128]{1,0:T(8,128)S(1)}, u32[]{:S(2)}, u32[]{:S(2)}) collective-permute-start(f32[128,128]{1,0:T(8,128)S(1)} %apply2.1.refs_5_), channel_id=1, source_target_pairs={{0,1},{1,2},{2,3},{3,4},{4,5},{5,6},{6,7},{7,8},{8,9},{9,10},{10,1... | collective-permute-start | bytes 196616 | tf_op jit(solution)/shard_map/ppermute | solution.py:322
  30.9 0.0 collective-permute-done.5.refs_6_
  30.9 0.9 %adjoint3.1 = (f32[128,128]{1,0:T(8,128)S(1)}, f32[128,128]{1,0:T(8,128)S(1)}) custom-call(bf16[2048,256]{1,0:T(8,128)(2,1)S(1)} %get-tuple-element.39.refs_0_, bf16[2048,256]{1,0:T(8,128)(2,1)S(1)} %get-tuple-element.40.refs_1_, bf16[2048,256]{1,0:T(8,128)(2,1)S(1)} %get-tuple-element.42.refs_4_.refs_2_, ...), custom_call_target="tpu_custom_call" | custom-call | flops 10737418240 | bytes 4526080 | tf_op jit(solution)/shard_map/adjoint3/pallas_call | solution.py:262
  31.8 1.3 %collective-permute-start.7 = (f32[128,128]{1,0:T(8,128)S(1)}, f32[128,128]{1,0:T(8,128)S(1)}, u32[]{:S(2)}, u32[]{:S(2)}) collective-permute-start(f32[128,128]{1,0:T(8,128)S(1)} %get-tuple-element.55), channel_id=1, source_target_pairs={{1,0},{2,1},{3,2},{4,3},{5,4},{6,5},{7,6},{8,7},{9,8},{10,9},{11,1... | collective-permute-start | bytes 196616 | tf_op jit(solution)/shard_map/ppermute | solution.py:332
  33.1 6.7 %collective-permute-start.10 = (f32[18,128,128]{2,1,0:T(8,128)S(1)}, f32[18,128,128]{2,1,0:T(8,128)S(1)}, u32[]{:S(2)}, u32[]{:S(2)}) collective-permute-start(f32[18,128,128]{2,1,0:T(8,128)S(1)} %get-tuple-element.59.refs_1_.m0_ref), channel_id=1, source_target_pairs={{0,64},{64,0},{128,192},{192,128},{256,320},{320,256},{384,448},{4... | collective-permute-start | bytes 3538952 | tf_op jit(solution)/shard_map/ppermute | solution.py:335
  39.9 2.1 %collective-permute-start.11 = (f32[18,128,128]{2,1,0:T(8,128)S(1)}, f32[18,128,128]{2,1,0:T(8,128)S(1)}, u32[]{:S(2)}, u32[]{:S(2)}) collective-permute-start(f32[18,128,128]{2,1,0:T(8,128)S(1)} %get-tuple-element.60.refs_2_.m1_ref), channel_id=1, source_target_pairs={{64,128},{192,256},{320,384},{128,64},{256,192},{384,320},{65,129}... | collective-permute-start | bytes 3538952 | tf_op jit(solution)/shard_map/ppermute | solution.py:334
  42.0 0.0 collective-permute-done.6.refs_11_
  42.0 1.1 %apply3.1.part_ref = f32[128,128]{1,0:T(8,128)S(1)} custom-call(bf16[2048,256]{1,0:T(8,128)(2,1)S(1)} %get-tuple-element.39.refs_0_, bf16[2048,256]{1,0:T(8,128)(2,1)S(1)} %get-tuple-element.40.refs_1_, bf16[256,256]{1,0:T(8,128)(2,1)S(1)} %get-tuple-element.44.refs_2_, bf16[256,256]{1,0:T(8,128)(2,1)S(1)} %get-tuple-element.45.refs_3_, ...), custom_call_target="tpu_custom_call" | custom-call | flops 12079595520 | bytes 5120000 | tf_op jit(solution)/shard_map/apply3/pallas_call | solution.py:262
  43.0 0.0 collective-permute-done.7.got_b_ref
  43.1 0.1 finish.1
  43.2 28.4 %all_to_all.11 = f32[64,1,128]{2,1,0:T(1,128)S(1)} all-to-all(f32[64,1,128]{2,1,0:T(1,128)S(1)} %bitcast.14), channel_id=1, replica_groups={{36,37,38,39,40,41,42,43,44,45,46,47,48,49,50,51,52,53,54,55,56,57,58,5..., dimensions={0} | all-to-all | bytes 65536 | tf_op jit(solution)/shard_map/all_to_all | solution.py:347
  71.6 0.1 normalise.1
  71.7 4.0 %collective-permute-start.8 = (f32[128,128]{1,0:T(8,128)S(1)}, f32[128,128]{1,0:T(8,128)S(1)}, u32[]{:S(2)}, u32[]{:S(2)}) collective-permute-start(f32[128,128]{1,0:T(8,128)S(1)} %get-tuple-element.58), channel_id=1, source_target_pairs={{64,128},{192,256},{320,384},{128,64},{256,192},{384,320},{65,129}... | collective-permute-start | bytes 196616 | tf_op jit(solution)/shard_map/ppermute | solution.py:349
  75.7 1.9 %collective-permute-start.9 = (f32[128,128]{1,0:T(8,128)S(1)}, f32[128,128]{1,0:T(8,128)S(1)}, u32[]{:S(2)}, u32[]{:S(2)}) collective-permute-start(f32[128,128]{1,0:T(8,128)S(1)} %get-tuple-element.58), channel_id=1, source_target_pairs={{0,64},{64,0},{128,192},{192,128},{256,320},{320,256},{384,448},{4... | collective-permute-start | bytes 196616 | tf_op jit(solution)/shard_map/ppermute | solution.py:350
  77.7 0.0 collective-permute-done.10.x0_ref
  77.7 0.0 collective-permute-done.11.x1_ref
  77.7 0.7 parts.1
  78.4 0.0 collective-permute-done.8.kept1_ref
  78.4 0.5 collective-permute-done.9.kept0_ref
  78.9 2.4 %extend.1 = (f32[128,128]{1,0:T(8,128)}, f32[18,128,128]{2,1,0:T(8,128)}, f32[18,128,128]{2,1,0:T(8,128)}) custom-call(f32[128,128]{1,0:T(8,128)S(1)} %collective-permute-done.8.kept1_ref, f32[128,128]{1,0:T(8,128)S(1)} %collective-permute-done.9.kept0_ref, bf16[2304,256]{1,0:T(8,128)(2,1)S(1)} %get-tuple-element.61.pl_ref, ...), custom_call_target="tpu_custom_call" | custom-call | flops 24159191040 | bytes 4980736 | tf_op jit(solution)/shard_map/extend/pallas_call | solution.py:262
  (1 shorter events, 0.0 us)
Async XLA Ops:
  3.1 8.1 %collective-permute-start = (f32[136,128]{1,0:T(8,128)S(1)}, f32[136,128]{1,0:T(8,128)S(1)}, u32[]{:S(2)}, u32[]{:S(2)}) collective-permute-start(f32[136,128]{1,0:T(8,128)S(1)} %get-tuple-element.48.refs_0_.own_ref.refs_8_.refs_4_), channel_id=1, source_target_pairs={{0,1},{1,2},{2,3},{3,4},{4,5},{5,6},{6,7},{7,8},{8,9},{9,10},{10,1... | collective-permute-start | bytes 208904 | tf_op jit(solution)/shard_map/ppermute | solution.py:306
  9.2 7.0 %collective-permute-start.1 = (f32[128,128]{1,0:T(8,128)S(1)}, f32[128,128]{1,0:T(8,128)S(1)}, u32[]{:S(2)}, u32[]{:S(2)}) collective-permute-start(f32[128,128]{1,0:T(8,128)S(1)} %get-tuple-element.49.refs_12_), channel_id=1, source_target_pairs={{1,0},{2,1},{3,2},{4,3},{5,4},{6,5},{7,6},{8,7},{9,8},{10,9},{11,1... | collective-permute-start | bytes 196616 | tf_op jit(solution)/shard_map/ppermute | solution.py:310
  12.2 6.3 %collective-permute-start.2 = (f32[128,128]{1,0:T(8,128)S(1)}, f32[128,128]{1,0:T(8,128)S(1)}, u32[]{:S(2)}, u32[]{:S(2)}) collective-permute-start(f32[128,128]{1,0:T(8,128)S(1)} %apply0.1.refs_5_), channel_id=1, source_target_pairs={{0,1},{1,2},{2,3},{3,4},{4,5},{5,6},{6,7},{7,8},{8,9},{9,10},{10,1... | collective-permute-start | bytes 196616 | tf_op jit(solution)/shard_map/ppermute | solution.py:322
  17.1 6.4 %collective-permute-start.3 = (f32[128,128]{1,0:T(8,128)S(1)}, f32[128,128]{1,0:T(8,128)S(1)}, u32[]{:S(2)}, u32[]{:S(2)}) collective-permute-start(f32[128,128]{1,0:T(8,128)S(1)} %get-tuple-element.51.refs_12_), channel_id=1, source_target_pairs={{1,0},{2,1},{3,2},{4,3},{5,4},{6,5},{7,6},{8,7},{9,8},{10,9},{11,1... | collective-permute-start | bytes 196616 | tf_op jit(solution)/shard_map/ppermute | solution.py:332
  19.5 6.3 %collective-permute-start.4 = (f32[128,128]{1,0:T(8,128)S(1)}, f32[128,128]{1,0:T(8,128)S(1)}, u32[]{:S(2)}, u32[]{:S(2)}) collective-permute-start(f32[128,128]{1,0:T(8,128)S(1)} %apply1.1.refs_5_), channel_id=1, source_target_pairs={{0,1},{1,2},{2,3},{3,4},{4,5},{5,6},{6,7},{7,8},{8,9},{9,10},{10,1... | collective-permute-start | bytes 196616 | tf_op jit(solution)/shard_map/ppermute | solution.py:322
  24.5 6.4 %collective-permute-start.5 = (f32[128,128]{1,0:T(8,128)S(1)}, f32[128,128]{1,0:T(8,128)S(1)}, u32[]{:S(2)}, u32[]{:S(2)}) collective-permute-start(f32[128,128]{1,0:T(8,128)S(1)} %get-tuple-element.53.refs_12_), channel_id=1, source_target_pairs={{1,0},{2,1},{3,2},{4,3},{5,4},{6,5},{7,6},{8,7},{9,8},{10,9},{11,1... | collective-permute-start | bytes 196616 | tf_op jit(solution)/shard_map/ppermute | solution.py:332
  26.9 15.1 %collective-permute-start.6 = (f32[128,128]{1,0:T(8,128)S(1)}, f32[128,128]{1,0:T(8,128)S(1)}, u32[]{:S(2)}, u32[]{:S(2)}) collective-permute-start(f32[128,128]{1,0:T(8,128)S(1)} %apply2.1.refs_5_), channel_id=1, source_target_pairs={{0,1},{1,2},{2,3},{3,4},{4,5},{5,6},{6,7},{7,8},{8,9},{9,10},{10,1... | collective-permute-start | bytes 196616 | tf_op jit(solution)/shard_map/ppermute | solution.py:322
  31.8 11.2 %collective-permute-start.7 = (f32[128,128]{1,0:T(8,128)S(1)}, f32[128,128]{1,0:T(8,128)S(1)}, u32[]{:S(2)}, u32[]{:S(2)}) collective-permute-start(f32[128,128]{1,0:T(8,128)S(1)} %get-tuple-element.55), channel_id=1, source_target_pairs={{1,0},{2,1},{3,2},{4,3},{5,4},{6,5},{7,6},{8,7},{9,8},{10,9},{11,1... | collective-permute-start | bytes 196616 | tf_op jit(solution)/shard_map/ppermute | solution.py:332
  33.1 44.5 %collective-permute-start.10 = (f32[18,128,128]{2,1,0:T(8,128)S(1)}, f32[18,128,128]{2,1,0:T(8,128)S(1)}, u32[]{:S(2)}, u32[]{:S(2)}) collective-permute-start(f32[18,128,128]{2,1,0:T(8,128)S(1)} %get-tuple-element.59.refs_1_.m0_ref), channel_id=1, source_target_pairs={{0,64},{64,0},{128,192},{192,128},{256,320},{320,256},{384,448},{4... | collective-permute-start | bytes 3538952 | tf_op jit(solution)/shard_map/ppermute | solution.py:335
  39.9 37.8 %collective-permute-start.11 = (f32[18,128,128]{2,1,0:T(8,128)S(1)}, f32[18,128,128]{2,1,0:T(8,128)S(1)}, u32[]{:S(2)}, u32[]{:S(2)}) collective-permute-start(f32[18,128,128]{2,1,0:T(8,128)S(1)} %get-tuple-element.60.refs_2_.m1_ref), channel_id=1, source_target_pairs={{64,128},{192,256},{320,384},{128,64},{256,192},{384,320},{65,129}... | collective-permute-start | bytes 3538952 | tf_op jit(solution)/shard_map/ppermute | solution.py:334
  71.7 6.7 %collective-permute-start.8 = (f32[128,128]{1,0:T(8,128)S(1)}, f32[128,128]{1,0:T(8,128)S(1)}, u32[]{:S(2)}, u32[]{:S(2)}) collective-permute-start(f32[128,128]{1,0:T(8,128)S(1)} %get-tuple-element.58), channel_id=1, source_target_pairs={{64,128},{192,256},{320,384},{128,64},{256,192},{384,320},{65,129}... | collective-permute-start | bytes 196616 | tf_op jit(solution)/shard_map/ppermute | solution.py:349
  75.7 3.1 %collective-permute-start.9 = (f32[128,128]{1,0:T(8,128)S(1)}, f32[128,128]{1,0:T(8,128)S(1)}, u32[]{:S(2)}, u32[]{:S(2)}) collective-permute-start(f32[128,128]{1,0:T(8,128)S(1)} %get-tuple-element.58), channel_id=1, source_target_pairs={{0,64},{64,0},{128,192},{192,128},{256,320},{320,256},{384,448},{4... | collective-permute-start | bytes 196616 | tf_op jit(solution)/shard_map/ppermute | solution.py:350

commit v8 on v7

--- a/solution.py
+++ b/solution.py
@@ -85,53 +85,39 @@
     return lax.rem(lax.axis_index(axis), 2) == 1
 
 
-def load(size_ref, x_ref, dl_ref, hl_ref, dr_ref, hr_ref, own_ref, m0_ref, m1_ref, x, sems):
+def first_message(size_ref, x_ref, own_ref, x, sem):
     n = x.shape[0]
-    diags, hops = dl_ref.shape[0], hl_ref.shape[0]
-    first = pltpu.make_async_copy(x_ref, x, sems.at[0])
-    first.start()
-    part = hops // PARTS
-    left, right = (dl_ref, hl_ref), (dr_ref, hr_ref)
-
-    def loads(sides):
-        copies = []
-        for side, ((diag, hop), out) in enumerate(zip(sides, (m0_ref, m1_ref))):
-            sem = 1 + side * (1 + PARTS)
-            copies.append(pltpu.make_async_copy(diag, out.at[pl.ds(0, diags)], sems.at[sem]))
-            for i in range(PARTS):
-                source, target = pl.ds(i * part, part), pl.ds(diags + i * part, part)
-                copies.append(pltpu.make_async_copy(hop.at[source], out.at[target], sems.at[sem + 1 + i]))
-        return copies
-
-    segment = odd("seg")
-
-    @pl.when(segment)
-    def _():
-        for copy in loads((right, left)):
-            copy.start()
-
-    @pl.when(jnp.logical_not(segment))
-    def _():
-        for copy in loads((left, right)):
-            copy.start()
-
-    first.wait()
+    copy = pltpu.make_async_copy(x_ref, x, sem)
+    copy.start()
+    copy.wait()
     live = jnp.full((1, n), size_ref[0, 0].astype(f32), f32)
     own_ref[:n, :] = where(square_mask(live), x[...])
     own_ref[n:, :] = jnp.broadcast_to(live, (8, n))
-    for copy in loads((left, right)):
+
+
+def joined(sides, outs, sems):
+    copies = []
+    for side, ((diag, hop), out) in enumerate(zip(sides, outs)):
+        diags, part = diag.shape[0], hop.shape[0] // PARTS
+        copies.append(pltpu.make_async_copy(diag, out.at[pl.ds(0, diags)], sems.at[side, PARTS]))
+        for i in range(PARTS):
+            source, target = pl.ds(i * part, part), pl.ds(diags + i * part, part)
+            copies.append(pltpu.make_async_copy(hop.at[source], out.at[target], sems.at[side, i]))
+    return copies
+
+
+def first_product(own_ref, dl_ref, hl_ref, dr_ref, hr_ref, lt_ref, rc_ref, dlt_ref, drc_ref, b_ref, left, right, sems):
+    n = own_ref.shape[1]
+    diags = dl_ref.shape[0]
+    copies = joined(((dl_ref, hl_ref), (dr_ref, hr_ref)), (left, right), sems)
+    for copy in copies:
+        copy.start()
+    for copy in copies:
         copy.wait()
-
-
-def first_product(own_ref, m0_ref, m1_ref, lt_ref, rc_ref, dlt_ref, drc_ref, b_ref):
-    n = own_ref.shape[1]
-    diags = dlt_ref.shape[0] // n
-    segment = odd("seg")
-    for c in range(m0_ref.shape[0]):
-        x, y = m0_ref[c], m1_ref[c]
+    for c in range(left.shape[0]):
         k = c if c < diags else c - diags
-        put_parts(dlt_ref if c < diags else lt_ref, k, n, jnp.where(segment, y, x).T)
-        put_parts(drc_ref if c < diags else rc_ref, k, n, jnp.where(segment, x, y))
+        put_parts(dlt_ref if c < diags else lt_ref, k, n, left[c].T)
+        put_parts(drc_ref if c < diags else rc_ref, k, n, right[c])
     b_ref[...] = sandwich(lt_ref, rc_ref, own_ref[:n, :])
 
 
@@ -139,50 +125,82 @@
     pl.when(odd("blk"))(lambda: first_product(*refs))
 
 
-def even_adjoint(own_ref, m0_ref, m1_ref, done_ref, lt_ref, rc_ref, dlt_ref, drc_ref, b_ref):
+def even_adjoint(done_ref, own_ref, dl_ref, hl_ref, dr_ref, hr_ref, lt_ref, rc_ref, dlt_ref, drc_ref, b_ref, d_ref, *scratch):
+    n = own_ref.shape[1]
+
     @pl.when(odd("blk"))
     def _():
         b_ref[...] = done_ref[...]
 
     @pl.when(jnp.logical_not(odd("blk")))
     def _():
-        first_product(own_ref, m0_ref, m1_ref, lt_ref, rc_ref, dlt_ref, drc_ref, b_ref)
-
-
-def by_parity(kernel, count):
+        first_product(own_ref, dl_ref, hl_ref, dr_ref, hr_ref, lt_ref, rc_ref, dlt_ref, drc_ref, b_ref, *scratch)
+        d_ref[...] = sandwich(drc_ref, dlt_ref, own_ref[:n, :].T)
+
+
+def gather(dl_ref, hl_ref, dr_ref, hr_ref, outs, sems):
+    left, right = (dl_ref, hl_ref), (dr_ref, hr_ref)
+    segment = odd("seg")
+
+    @pl.when(segment)
+    def _():
+        for copy in joined((right, left), outs, sems):
+            copy.start()
+
+    @pl.when(jnp.logical_not(segment))
+    def _():
+        for copy in joined((left, right), outs, sems):
+            copy.start()
+
+    for copy in joined((left, right), outs, sems):
+        copy.wait()
+
+
+def odd_gather(after_ref, dl_ref, hl_ref, dr_ref, hr_ref, m0_ref, m1_ref, sems):
+    pl.when(odd("blk"))(lambda: gather(dl_ref, hl_ref, dr_ref, hr_ref, (m0_ref, m1_ref), sems))
+
+
+def even_gather(after_ref, dl_ref, hl_ref, dr_ref, hr_ref, m0_in, m1_in, m0_ref, m1_ref, sems):
+    even = jnp.logical_not(odd("blk"))
+    pl.when(even)(lambda: gather(dl_ref, hl_ref, dr_ref, hr_ref, (m0_ref, m1_ref), sems))
+
+
+def by_parity(kernel):
     def chosen(*refs):
-        odd_ops, even_ops, rest = refs[:count], refs[count : 2 * count], refs[2 * count :]
-        pl.when(odd("blk"))(lambda: kernel(*odd_ops, *rest))
-        pl.when(jnp.logical_not(odd("blk")))(lambda: kernel(*even_ops, *rest))
+        pl.when(odd("blk"))(lambda: kernel(True, refs[:4], *refs[8:]))
+        pl.when(jnp.logical_not(odd("blk")))(lambda: kernel(False, refs[4:8], *refs[8:]))
 
     return chosen
 
 
-def adjoint(lt_ref, rc_ref, own_ref, a_ref, got_b_ref, v_ref, b_ref):
+def adjoint(is_odd, ops, own_ref, a_ref, got_b_ref, v_ref, b_ref, d_ref):
+    lt_ref, rc_ref, dlt_ref, drc_ref = ops
     n = own_ref.shape[1]
     v = a_ref[...] - where(square_mask(own_ref[n : n + 1, :]), got_b_ref[...])
     v_ref[...] = v
     b_ref[...] = sandwich(lt_ref, rc_ref, v)
-
-
-def own_part(own_ref, v, below, lt_ref, rc_ref, dlt_ref, drc_ref):
-    n = own_ref.shape[1]
-    hop = sandwich(rc_ref, lt_ref, below.T)
-    diag = sandwich(drc_ref, dlt_ref, v.T)
-    return where(square_mask(own_ref[n : n + 1, :]), (hop + diag).T)
-
-
-def first_apply(lt_ref, rc_ref, dlt_ref, drc_ref, own_ref, below_ref, a_ref):
+    if not is_odd:
+        d_ref[...] = sandwich(drc_ref, dlt_ref, v.T)
+
+
+def own_part(is_odd, ops, own_ref, v, below, d_ref):
+    lt_ref, rc_ref, dlt_ref, drc_ref = ops
+    n = own_ref.shape[1]
+    diag = sandwich(drc_ref, dlt_ref, v.T) if is_odd else d_ref[...]
+    return where(square_mask(own_ref[n : n + 1, :]), (sandwich(rc_ref, lt_ref, below.T) + diag).T)
+
+
+def first_apply(is_odd, ops, own_ref, below_ref, d_ref, a_ref):
     n = own_ref.shape[1]
     v = own_ref[:n, :]
-    a_ref[...] = SHIFT * v - own_part(own_ref, v, below_ref[:n, :], lt_ref, rc_ref, dlt_ref, drc_ref)
-
-
-def later_apply(last, lt_ref, rc_ref, dlt_ref, drc_ref, own_ref, below_ref, v_ref, got_a_ref, b_ref, a_ref):
+    a_ref[...] = SHIFT * v - own_part(is_odd, ops, own_ref, v, below_ref[:n, :], d_ref)
+
+
+def later_apply(last, is_odd, ops, own_ref, below_ref, v_ref, d_ref, got_a_ref, b_ref, a_ref):
     n = own_ref.shape[1]
     below = where(square_mask(below_ref[n : n + 1, :]), got_a_ref[...] - b_ref[...])
     v = v_ref[...]
-    part = own_part(own_ref, v, below, lt_ref, rc_ref, dlt_ref, drc_ref)
+    part = own_part(is_odd, ops, own_ref, v, below, d_ref)
     a_ref[...] = part if last else SHIFT * v - part
 
 
@@ -256,7 +274,7 @@
         copy.wait()
 
 
-def call(kernel, args, specs, outs, out_specs=None, scratch=(), flops=0, limit=16, name=None):
+def call(kernel, args, specs, outs, out_specs=None, scratch=(), flops=0, limit=16, aliases=None, name=None):
     moved = sum(math.prod(a.shape) * a.dtype.itemsize for a in (*args, *outs))
     args = [pltpu.with_memory_space_constraint(a, pltpu.HBM) if spec is HBM else a for a, spec in zip(args, specs)]
     return pl.pallas_call(
@@ -265,6 +283,7 @@
         out_specs=out_specs or [VMEM] * len(outs),
         out_shape=outs,
         scratch_shapes=list(scratch),
+        input_output_aliases=aliases or {},
         compiler_params=pltpu.CompilerParams(vmem_limit_bytes=limit << 20),
         cost_estimate=pl.CostEstimate(flops=flops, bytes_accessed=moved, transcendentals=0),
         name=name,
@@ -289,43 +308,82 @@
     out = SDS((diags + hops, n, n), f32)
     channel = 20 * 8 * 2 * n**3
 
-    own, m0, m1 = call(
-        load,
-        (sector_sizes, x0, dl, hl, dr, hr),
-        [SMEM] + [HBM] * 5,
-        [message, out, out],
-        scratch=[
-            pltpu.VMEM((n, n), f32),
-            pltpu.SemaphoreType.DMA((3 + 2 * PARTS,)),
-        ],
+    (own,) = call(
+        first_message,
+        (sector_sizes, x0),
+        [SMEM, HBM],
+        [message],
+        scratch=[pltpu.VMEM((n, n), f32), pltpu.SemaphoreType.DMA],
         limit=32,
-        name="load",
-    )
+        name="first_message",
+    )
+    operators = (dl, hl, dr, hr)
     products = [hop_parts, hop_parts, diag_parts, diag_parts, block]
-    *odd_ops, b = call(odd_adjoint, (own, m0, m1), [VMEM] * 3, products, flops=channel * hops, name="odd_adjoint")
+    arrivals = pltpu.SemaphoreType.DMA((2, PARTS + 1))
+    rooms = [pltpu.VMEM(out.shape, f32), pltpu.VMEM(out.shape, f32), arrivals]
+    *odd_ops, b = call(
+        odd_adjoint,
+        (own, *operators),
+        [VMEM] + [HBM] * 4,
+        products,
+        scratch=rooms,
+        flops=channel * hops,
+        limit=32,
+        name="odd_adjoint",
+    )
     below0 = lax.ppermute(lax.optimization_barrier((own, b))[0], "blk", up)
-    *even_ops, b = call(
-        even_adjoint, (own, m0, m1, b), [VMEM] * 4, products, flops=channel * hops, name="even_adjoint"
+    *even_ops, b, d = call(
+        even_adjoint,
+        (b, own, *operators),
+        [VMEM] * 2 + [HBM] * 4,
+        [*products, block],
+        scratch=rooms,
+        flops=channel * hops,
+        limit=32,
+        name="even_adjoint",
     )
     got_b = lax.ppermute(b, "blk", down)
     ops = (*odd_ops, *even_ops)
-    hop_ops = (*odd_ops[:2], *even_ops[:2])
+    m0, m1 = call(
+        odd_gather,
+        (below0, *operators),
+        [VMEM] + [HBM] * 4,
+        [out, out],
+        out_specs=[ANY] * 2,
+        scratch=[arrivals],
+        limit=32,
+        name="odd_gather",
+    )
+    below0 = lax.optimization_barrier((below0, m0))[0]
     (a,) = call(
-        by_parity(first_apply, 4),
-        (*ops, own, below0),
-        [VMEM] * 10,
+        by_parity(first_apply),
+        (*ops, own, below0, d),
+        [VMEM] * 11,
         [block],
         flops=channel * (hops + diags),
         name="apply0",
     )
     for k in range(1, ITERS):
         got_a = lax.ppermute(a, "blk", up)
+        if k == 1:
+            m0, m1 = call(
+                even_gather,
+                (lax.optimization_barrier((got_b, a))[0], *operators, m0, m1),
+                [VMEM] + [HBM] * 4 + [ANY] * 2,
+                [out, out],
+                out_specs=[ANY] * 2,
+                scratch=[arrivals],
+                limit=32,
+                aliases={5: 0, 6: 1},
+                name="even_gather",
+            )
+            got_b = lax.optimization_barrier((got_b, m0))[0]
         last_b = b
-        v, b = call(
-            by_parity(adjoint, 2),
-            (*hop_ops, own, a, got_b),
-            [VMEM] * 7,
-            [block, block],
+        v, b, d = call(
+            by_parity(adjoint),
+            (*ops, own, a, got_b),
+            [VMEM] * 11,
+            [block, block, block],
             flops=channel * hops,
             name=f"adjoint{k}",
         )
@@ -334,9 +392,9 @@
             x1 = lax.ppermute(lax.optimization_barrier((m1, b))[0], "seg", across)
             x0 = lax.ppermute(lax.optimization_barrier((m0, b))[0], "seg", chip)
         (a,) = call(
-            by_parity(functools.partial(later_apply, k == ITERS - 1), 4),
-            (*ops, own, below0, v, got_a, last_b),
-            [VMEM] * 13,
+            by_parity(functools.partial(later_apply, k == ITERS - 1)),
+            (*ops, own, below0, v, d, got_a, last_b),
+            [VMEM] * 14,
             [block],
             flops=channel * (hops + diags),
             name=f"apply{k}",

time: 81.9 us -> 84.5 us (1.032)
  blocking collectives: 28.4 us -> 24.6 us
  starting transfers between devices: 36.9 us -> 40.5 us
  Pallas kernels: 13.2 us -> 15.9 us
    ppermute x1, starting transfers between devices: 6.7 us -> 1.92 us  [shards(): x0 = lax.ppermute(lax.optimization_barrier((m0, b))[0], 'seg', chip)]
    all_to_all x1, blocking collectives: 28.4 us -> 24.6 us  [shards(): lax.all_to_all(sums, 'blk', 0, 0, tiled=True, axis_index_groups=[members])]
    ppermute x1, starting transfers between devices: 2.1 us -> 5.65 us  [shards(): x1 = lax.ppermute(lax.optimization_barrier((m1, b))[0], 'seg', across)]
    pallas_call x14 -> x16, Pallas kernels: 13.2 us -> 15.9 us  [call(): pl.pallas_call(kernel, in_specs=specs, out_specs=out_specs or [VMEM] * le...]
    ppermute x3, starting transfers between devices: 12 us -> 14 us  [shards(): got_a = lax.ppermute(a, 'blk', up)]
    ppermute x1, starting transfers between devices: 5.06 us -> 6.66 us  [shards(): below0 = lax.ppermute(lax.optimization_barrier((own, b))[0], 'blk', up)]
    ppermute x1, starting transfers between devices: 4.03 us -> 4.93 us  [shards(): kept1 = lax.ppermute(kept, 'seg', across)]
  transfers between devices with their start and end apart: 12 -> 12, of which waited for: 1 -> 1; matrix products, arithmetic and copies ran while one was open for 0% -> 0% of each run, Pallas kernels for 11% -> 15%
where the time goes in v8:
time: 84.5 us; the launch traced here: 84 us
  starting transfers between devices  40.5 us (48%)
  blocking collectives  24.6 us (29%)
  Pallas kernels  15.9 us (19%)
  between operations  2.38 us (3%)
    all_to_all x1, blocking collectives, shards(): lax.all_to_all(sums, 'blk', 0, 0, tiled=True, axis_index_groups=[members])  24.6 us
    pallas_call x16, Pallas kernels, call(): pl.pallas_call(kernel, in_specs=specs, out_specs=out_specs or [VMEM] * le...  15.9 us
    ppermute x3, starting transfers between devices, shards(): got_a = lax.ppermute(a, 'blk', up)  14 us
    ppermute x1, starting transfers between devices, shards(): below0 = lax.ppermute(lax.optimization_barrier((own, b))[0], 'blk', up)  6.66 us
    ppermute x1, starting transfers between devices, shards(): x1 = lax.ppermute(lax.optimization_barrier((m1, b))[0], 'seg', across)  5.65 us
    ppermute x4, starting transfers between devices, shards(): got_b = lax.ppermute(b, 'blk', down)  5.35 us
    ppermute x1, starting transfers between devices, shards(): kept1 = lax.ppermute(kept, 'seg', across)  4.93 us
    ppermute x1, starting transfers between devices, shards(): x0 = lax.ppermute(lax.optimization_barrier((m0, b))[0], 'seg', chip)  1.92 us
  transfers between devices with their start and end apart: 12, of which 1 were waited for; matrix products, arithmetic and copies ran while one was open for 0% of the time, Pallas kernels for 15%

profile of v8, /device:TPU:1, one launch (start us, length us, event | category | flops | bytes accessed | tf_op | source)
XLA Modules:
  0.0 84.0 jit_solution(8885206789330657410)
XLA Ops:
  1.3 0.9 %first_message.1.refs_0_.own_ref.refs_8_ = f32[136,128]{1,0:T(8,128)S(1)} custom-call(s32[1,1]{1,0:T(1,128)S(6)} %copy.16.size_ref, f32[128,128]{1,0:T(8,128)} %bitcast.31), custom_call_target="tpu_custom_call" | custom-call | bytes 135172 | tf_op jit(solution)/shard_map/first_message/pallas_call | solution.py:280
  2.1 0.1 odd_adjoint.1
  2.3 6.7 %collective-permute-start = (f32[136,128]{1,0:T(8,128)S(1)}, f32[136,128]{1,0:T(8,128)S(1)}, u32[]{:S(2)}, u32[]{:S(2)}) collective-permute-start(f32[136,128]{1,0:T(8,128)S(1)} %first_message.1.refs_0_.own_ref.refs_8_), channel_id=1, source_target_pairs={{0,1},{1,2},{2,3},{3,4},{4,5},{5,6},{6,7},{7,8},{8,9},{9,10},{10,1... | collective-permute-start | bytes 208904 | tf_op jit(solution)/shard_map/ppermute | solution.py:334
  8.9 2.7 %even_adjoint.1 = (bf16[2048,256]{1,0:T(8,128)(2,1)S(1)}, bf16[2048,256]{1,0:T(8,128)(2,1)S(1)}, bf16[256,256]{1,0:T(8,128)(2,1)S(1)}, bf16[256,256]{1,0:T(8,128...) custom-call(f32[128,128]{1,0:T(8,128)S(1)} %get-tuple-element.48.done_ref, ...), custom_call_target="tpu_custom_call" | custom-call | flops 10737418240 | bytes 4984832 | tf_op jit(solution)/shard_map/even_adjoint/pallas_call | solution.py:280
  11.7 1.3 %collective-permute-start.1 = (f32[128,128]{1,0:T(8,128)S(1)}, f32[128,128]{1,0:T(8,128)S(1)}, u32[]{:S(2)}, u32[]{:S(2)}) collective-permute-start(f32[128,128]{1,0:T(8,128)S(1)} %get-tuple-element.57.refs_13_), channel_id=1, source_target_pairs={{1,0},{2,1},{3,2},{4,3},{5,4},{6,5},{7,6},{8,7},{9,8},{10,9},{11,1... | collective-permute-start | bytes 196616 | tf_op jit(solution)/shard_map/ppermute | solution.py:345
  13.6 0.0 collective-permute-done.after_ref.refs_9_
  13.6 0.1 odd_gather.1
  13.8 1.1 %apply0.1.refs_9_ = f32[128,128]{1,0:T(8,128)S(1)} custom-call(bf16[2048,256]{1,0:T(8,128)(2,1)S(1)} %get-tuple-element.44.refs_0_, bf16[2048,256]{1,0:T(8,128)(2,1)S(1)} %get-tuple-element.45.refs_1_, bf16[256,256]{1,0:T(8,128)(2,1)S(1)} %get-tuple-element.46.refs_2_, bf16[256,256]{1,0:T(8,128)(2,1)S(1)} %get-tuple-element.47.refs_3_, ...), custom_call_target="tpu_custom_call" | custom-call | flops 12079595520 | bytes 4988928 | tf_op jit(solution)/shard_map/apply0/pallas_call | solution.py:280
  14.9 5.7 %collective-permute-start.2 = (f32[128,128]{1,0:T(8,128)S(1)}, f32[128,128]{1,0:T(8,128)S(1)}, u32[]{:S(2)}, u32[]{:S(2)}) collective-permute-start(f32[128,128]{1,0:T(8,128)S(1)} %apply0.1.refs_9_), channel_id=1, source_target_pairs={{0,1},{1,2},{2,3},{3,4},{4,5},{5,6},{6,7},{7,8},{8,9},{9,10},{10,1... | collective-permute-start | bytes 196616 | tf_op jit(solution)/shard_map/ppermute | solution.py:367
  20.6 0.0 collective-permute-done.1.after_ref.refs_10_
  20.6 1.7 %even_gather.1 = (f32[18,128,128]{2,1,0:T(8,128)S(1)}, f32[18,128,128]{2,1,0:T(8,128)S(1)}) custom-call(f32[128,128]{1,0:T(8,128)S(1)} %collective-permute-done.1.after_ref.refs_10_, f32[2,128,128]{2,1,0:T(8,128)} %bitcast.26, f32[16,128,128]{2,1,0:T(8,128)} %bitcast.18, f32[2,128,128]{2,1,0:T(8,128)} %bitcast.30, ...), custom_call_target="tpu_custom_call", output_to_operand_aliasing={{0}: (5, {}), {1}: (6, {})} | custom-call | bytes 7143424 | tf_op jit(solution)/shard_map/even_gather/pallas_call | solution.py:280
  22.3 0.9 %adjoint1.1 = (f32[128,128]{1,0:T(8,128)S(1)}, f32[128,128]{1,0:T(8,128)S(1)}, f32[128,128]{1,0:T(8,128)S(1)}) custom-call(bf16[2048,256]{1,0:T(8,128)(2,1)S(1)} %get-tuple-element.44.refs_0_, bf16[2048,256]{1,0:T(8,128)(2,1)S(1)} %get-tuple-element.45.refs_1_, bf16[256,256]{1,0:T(8,128)(2,1)S(1)} %get-tuple-element.46.refs_2_, ...), custom_call_target="tpu_custom_call" | custom-call | flops 10737418240 | bytes 5115904 | tf_op jit(solution)/shard_map/adjoint1/pallas_call | solution.py:280
  23.2 1.3 %collective-permute-start.3 = (f32[128,128]{1,0:T(8,128)S(1)}, f32[128,128]{1,0:T(8,128)S(1)}, u32[]{:S(2)}, u32[]{:S(2)}) collective-permute-start(f32[128,128]{1,0:T(8,128)S(1)} %get-tuple-element.64.refs_13_), channel_id=1, source_target_pairs={{1,0},{2,1},{3,2},{4,3},{5,4},{6,5},{7,6},{8,7},{9,8},{10,9},{11,1... | collective-permute-start | bytes 196616 | tf_op jit(solution)/shard_map/ppermute | solution.py:390
  24.5 0.0 collective-permute-done.2.refs_12_
  24.6 1.1 %apply1.1.refs_9_ = f32[128,128]{1,0:T(8,128)S(1)} custom-call(bf16[2048,256]{1,0:T(8,128)(2,1)S(1)} %get-tuple-element.44.refs_0_, bf16[2048,256]{1,0:T(8,128)(2,1)S(1)} %get-tuple-element.45.refs_1_, bf16[256,256]{1,0:T(8,128)(2,1)S(1)} %get-tuple-element.46.refs_2_, bf16[256,256]{1,0:T(8,128)(2,1)S(1)} %get-tuple-element.47.refs_3_, ...), custom_call_target="tpu_custom_call" | custom-call | flops 12079595520 | bytes 5185536 | tf_op jit(solution)/shard_map/apply1/pallas_call | solution.py:280
  25.7 4.1 %collective-permute-start.4 = (f32[128,128]{1,0:T(8,128)S(1)}, f32[128,128]{1,0:T(8,128)S(1)}, u32[]{:S(2)}, u32[]{:S(2)}) collective-permute-start(f32[128,128]{1,0:T(8,128)S(1)} %apply1.1.refs_9_), channel_id=1, source_target_pairs={{0,1},{1,2},{2,3},{3,4},{4,5},{5,6},{6,7},{7,8},{8,9},{9,10},{10,1... | collective-permute-start | bytes 196616 | tf_op jit(solution)/shard_map/ppermute | solution.py:367
  29.8 0.0 collective-permute-done.3.refs_10_
  29.8 0.9 %adjoint2.1 = (f32[128,128]{1,0:T(8,128)S(1)}, f32[128,128]{1,0:T(8,128)S(1)}, f32[128,128]{1,0:T(8,128)S(1)}) custom-call(bf16[2048,256]{1,0:T(8,128)(2,1)S(1)} %get-tuple-element.44.refs_0_, bf16[2048,256]{1,0:T(8,128)(2,1)S(1)} %get-tuple-element.45.refs_1_, bf16[256,256]{1,0:T(8,128)(2,1)S(1)} %get-tuple-element.46.refs_2_, ...), custom_call_target="tpu_custom_call" | custom-call | flops 10737418240 | bytes 5115904 | tf_op jit(solution)/shard_map/adjoint2/pallas_call | solution.py:280
  30.7 1.3 %collective-permute-start.5 = (f32[128,128]{1,0:T(8,128)S(1)}, f32[128,128]{1,0:T(8,128)S(1)}, u32[]{:S(2)}, u32[]{:S(2)}) collective-permute-start(f32[128,128]{1,0:T(8,128)S(1)} %get-tuple-element.67.refs_13_), channel_id=1, source_target_pairs={{1,0},{2,1},{3,2},{4,3},{5,4},{6,5},{7,6},{8,7},{9,8},{10,9},{11,1... | collective-permute-start | bytes 196616 | tf_op jit(solution)/shard_map/ppermute | solution.py:390
  32.0 0.0 collective-permute-done.4.refs_12_
  32.0 1.1 %apply2.1.refs_9_ = f32[128,128]{1,0:T(8,128)S(1)} custom-call(bf16[2048,256]{1,0:T(8,128)(2,1)S(1)} %get-tuple-element.44.refs_0_, bf16[2048,256]{1,0:T(8,128)(2,1)S(1)} %get-tuple-element.45.refs_1_, bf16[256,256]{1,0:T(8,128)(2,1)S(1)} %get-tuple-element.46.refs_2_, bf16[256,256]{1,0:T(8,128)(2,1)S(1)} %get-tuple-element.47.refs_3_, ...), custom_call_target="tpu_custom_call" | custom-call | flops 12079595520 | bytes 5185536 | tf_op jit(solution)/shard_map/apply2/pallas_call | solution.py:280
  33.2 4.1 %collective-permute-start.6 = (f32[128,128]{1,0:T(8,128)S(1)}, f32[128,128]{1,0:T(8,128)S(1)}, u32[]{:S(2)}, u32[]{:S(2)}) collective-permute-start(f32[128,128]{1,0:T(8,128)S(1)} %apply2.1.refs_9_), channel_id=1, source_target_pairs={{0,1},{1,2},{2,3},{3,4},{4,5},{5,6},{6,7},{7,8},{8,9},{9,10},{10,1... | collective-permute-start | bytes 196616 | tf_op jit(solution)/shard_map/ppermute | solution.py:367
  37.3 0.0 collective-permute-done.5.refs_10_
  37.3 0.9 %adjoint3.1 = (f32[128,128]{1,0:T(8,128)S(1)}, f32[128,128]{1,0:T(8,128)S(1)}, f32[128,128]{1,0:T(8,128)S(1)}) custom-call(bf16[2048,256]{1,0:T(8,128)(2,1)S(1)} %get-tuple-element.44.refs_0_, bf16[2048,256]{1,0:T(8,128)(2,1)S(1)} %get-tuple-element.45.refs_1_, bf16[256,256]{1,0:T(8,128)(2,1)S(1)} %get-tuple-element.46.refs_2_, ...), custom_call_target="tpu_custom_call" | custom-call | flops 10737418240 | bytes 5115904 | tf_op jit(solution)/shard_map/adjoint3/pallas_call | solution.py:280
  38.2 1.5 %collective-permute-start.7 = (f32[128,128]{1,0:T(8,128)S(1)}, f32[128,128]{1,0:T(8,128)S(1)}, u32[]{:S(2)}, u32[]{:S(2)}) collective-permute-start(f32[128,128]{1,0:T(8,128)S(1)} %get-tuple-element.70), channel_id=1, source_target_pairs={{1,0},{2,1},{3,2},{4,3},{5,4},{6,5},{7,6},{8,7},{9,8},{10,9},{11,1... | collective-permute-start | bytes 196616 | tf_op jit(solution)/shard_map/ppermute | solution.py:390
  39.7 5.7 %collective-permute-start.11 = (f32[18,128,128]{2,1,0:T(8,128)S(1)}, f32[18,128,128]{2,1,0:T(8,128)S(1)}, u32[]{:S(2)}, u32[]{:S(2)}) collective-permute-start(f32[18,128,128]{2,1,0:T(8,128)S(1)} %get-tuple-element.76), channel_id=1, source_target_pairs={{64,128},{192,256},{320,384},{128,64},{256,192},{384,320},{65,129}... | collective-permute-start | bytes 3538952 | tf_op jit(solution)/shard_map/ppermute | solution.py:392
  45.4 1.9 %collective-permute-start.10 = (f32[18,128,128]{2,1,0:T(8,128)S(1)}, f32[18,128,128]{2,1,0:T(8,128)S(1)}, u32[]{:S(2)}, u32[]{:S(2)}) collective-permute-start(f32[18,128,128]{2,1,0:T(8,128)S(1)} %get-tuple-element.74), channel_id=1, source_target_pairs={{0,64},{64,0},{128,192},{192,128},{256,320},{320,256},{384,448},{4... | collective-permute-start | bytes 3538952 | tf_op jit(solution)/shard_map/ppermute | solution.py:393
  47.3 0.0 collective-permute-done.6.refs_12_
  47.3 1.1 %apply3.1.part_ref = f32[128,128]{1,0:T(8,128)S(1)} custom-call(bf16[2048,256]{1,0:T(8,128)(2,1)S(1)} %get-tuple-element.44.refs_0_, bf16[2048,256]{1,0:T(8,128)(2,1)S(1)} %get-tuple-element.45.refs_1_, bf16[256,256]{1,0:T(8,128)(2,1)S(1)} %get-tuple-element.46.refs_2_, bf16[256,256]{1,0:T(8,128)(2,1)S(1)} %get-tuple-element.47.refs_3_, ...), custom_call_target="tpu_custom_call" | custom-call | flops 12079595520 | bytes 5185536 | tf_op jit(solution)/shard_map/apply3/pallas_call | solution.py:280
  48.4 0.0 collective-permute-done.7.got_b_ref
  48.4 0.1 finish.1
  48.6 24.6 %all_to_all.11 = f32[64,1,128]{2,1,0:T(1,128)S(1)} all-to-all(f32[64,1,128]{2,1,0:T(1,128)S(1)} %bitcast.14), channel_id=1, replica_groups={{36,37,38,39,40,41,42,43,44,45,46,47,48,49,50,51,52,53,54,55,56,57,58,5..., dimensions={0} | all-to-all | bytes 65536 | tf_op jit(solution)/shard_map/all_to_all | solution.py:405
  73.2 0.1 normalise.1
  73.3 4.9 %collective-permute-start.8 = (f32[128,128]{1,0:T(8,128)S(1)}, f32[128,128]{1,0:T(8,128)S(1)}, u32[]{:S(2)}, u32[]{:S(2)}) collective-permute-start(f32[128,128]{1,0:T(8,128)S(1)} %get-tuple-element.73), channel_id=1, source_target_pairs={{64,128},{192,256},{320,384},{128,64},{256,192},{384,320},{65,129}... | collective-permute-start | bytes 196616 | tf_op jit(solution)/shard_map/ppermute | solution.py:407
  78.3 1.9 %collective-permute-start.9 = (f32[128,128]{1,0:T(8,128)S(1)}, f32[128,128]{1,0:T(8,128)S(1)}, u32[]{:S(2)}, u32[]{:S(2)}) collective-permute-start(f32[128,128]{1,0:T(8,128)S(1)} %get-tuple-element.73), channel_id=1, source_target_pairs={{0,64},{64,0},{128,192},{192,128},{256,320},{320,256},{384,448},{4... | collective-permute-start | bytes 196616 | tf_op jit(solution)/shard_map/ppermute | solution.py:408
  80.2 0.0 collective-permute-done.11.x1_ref
  80.2 0.0 collective-permute-done.10.x0_ref
  80.2 0.7 parts.1
  80.9 0.0 collective-permute-done.8.kept1_ref
  80.9 0.5 collective-permute-done.9.kept0_ref
  81.4 2.4 %extend.1 = (f32[128,128]{1,0:T(8,128)}, f32[18,128,128]{2,1,0:T(8,128)}, f32[18,128,128]{2,1,0:T(8,128)}) custom-call(f32[128,128]{1,0:T(8,128)S(1)} %collective-permute-done.8.kept1_ref, f32[128,128]{1,0:T(8,128)S(1)} %collective-permute-done.9.kept0_ref, bf16[2304,256]{1,0:T(8,128)(2,1)S(1)} %get-tuple-element.77.pl_ref, ...), custom_call_target="tpu_custom_call" | custom-call | flops 24159191040 | bytes 4980736 | tf_op jit(solution)/shard_map/extend/pallas_call | solution.py:280
Async XLA Ops:
  2.3 11.3 %collective-permute-start = (f32[136,128]{1,0:T(8,128)S(1)}, f32[136,128]{1,0:T(8,128)S(1)}, u32[]{:S(2)}, u32[]{:S(2)}) collective-permute-start(f32[136,128]{1,0:T(8,128)S(1)} %first_message.1.refs_0_.own_ref.refs_8_), channel_id=1, source_target_pairs={{0,1},{1,2},{2,3},{3,4},{4,5},{5,6},{6,7},{7,8},{8,9},{9,10},{10,1... | collective-permute-start | bytes 208904 | tf_op jit(solution)/shard_map/ppermute | solution.py:334
  11.7 8.9 %collective-permute-start.1 = (f32[128,128]{1,0:T(8,128)S(1)}, f32[128,128]{1,0:T(8,128)S(1)}, u32[]{:S(2)}, u32[]{:S(2)}) collective-permute-start(f32[128,128]{1,0:T(8,128)S(1)} %get-tuple-element.57.refs_13_), channel_id=1, source_target_pairs={{1,0},{2,1},{3,2},{4,3},{5,4},{6,5},{7,6},{8,7},{9,8},{10,9},{11,1... | collective-permute-start | bytes 196616 | tf_op jit(solution)/shard_map/ppermute | solution.py:345
  14.9 9.7 %collective-permute-start.2 = (f32[128,128]{1,0:T(8,128)S(1)}, f32[128,128]{1,0:T(8,128)S(1)}, u32[]{:S(2)}, u32[]{:S(2)}) collective-permute-start(f32[128,128]{1,0:T(8,128)S(1)} %apply0.1.refs_9_), channel_id=1, source_target_pairs={{0,1},{1,2},{2,3},{3,4},{4,5},{5,6},{6,7},{7,8},{8,9},{9,10},{10,1... | collective-permute-start | bytes 196616 | tf_op jit(solution)/shard_map/ppermute | solution.py:367
  23.2 6.6 %collective-permute-start.3 = (f32[128,128]{1,0:T(8,128)S(1)}, f32[128,128]{1,0:T(8,128)S(1)}, u32[]{:S(2)}, u32[]{:S(2)}) collective-permute-start(f32[128,128]{1,0:T(8,128)S(1)} %get-tuple-element.64.refs_13_), channel_id=1, source_target_pairs={{1,0},{2,1},{3,2},{4,3},{5,4},{6,5},{7,6},{8,7},{9,8},{10,9},{11,1... | collective-permute-start | bytes 196616 | tf_op jit(solution)/shard_map/ppermute | solution.py:390
  25.7 6.4 %collective-permute-start.4 = (f32[128,128]{1,0:T(8,128)S(1)}, f32[128,128]{1,0:T(8,128)S(1)}, u32[]{:S(2)}, u32[]{:S(2)}) collective-permute-start(f32[128,128]{1,0:T(8,128)S(1)} %apply1.1.refs_9_), channel_id=1, source_target_pairs={{0,1},{1,2},{2,3},{3,4},{4,5},{5,6},{6,7},{7,8},{8,9},{9,10},{10,1... | collective-permute-start | bytes 196616 | tf_op jit(solution)/shard_map/ppermute | solution.py:367
  30.7 6.6 %collective-permute-start.5 = (f32[128,128]{1,0:T(8,128)S(1)}, f32[128,128]{1,0:T(8,128)S(1)}, u32[]{:S(2)}, u32[]{:S(2)}) collective-permute-start(f32[128,128]{1,0:T(8,128)S(1)} %get-tuple-element.67.refs_13_), channel_id=1, source_target_pairs={{1,0},{2,1},{3,2},{4,3},{5,4},{6,5},{7,6},{8,7},{9,8},{10,9},{11,1... | collective-permute-start | bytes 196616 | tf_op jit(solution)/shard_map/ppermute | solution.py:390
  33.2 14.1 %collective-permute-start.6 = (f32[128,128]{1,0:T(8,128)S(1)}, f32[128,128]{1,0:T(8,128)S(1)}, u32[]{:S(2)}, u32[]{:S(2)}) collective-permute-start(f32[128,128]{1,0:T(8,128)S(1)} %apply2.1.refs_9_), channel_id=1, source_target_pairs={{0,1},{1,2},{2,3},{3,4},{4,5},{5,6},{6,7},{7,8},{8,9},{9,10},{10,1... | collective-permute-start | bytes 196616 | tf_op jit(solution)/shard_map/ppermute | solution.py:367
  38.2 10.2 %collective-permute-start.7 = (f32[128,128]{1,0:T(8,128)S(1)}, f32[128,128]{1,0:T(8,128)S(1)}, u32[]{:S(2)}, u32[]{:S(2)}) collective-permute-start(f32[128,128]{1,0:T(8,128)S(1)} %get-tuple-element.70), channel_id=1, source_target_pairs={{1,0},{2,1},{3,2},{4,3},{5,4},{6,5},{7,6},{8,7},{9,8},{10,9},{11,1... | collective-permute-start | bytes 196616 | tf_op jit(solution)/shard_map/ppermute | solution.py:390
  39.7 40.5 %collective-permute-start.11 = (f32[18,128,128]{2,1,0:T(8,128)S(1)}, f32[18,128,128]{2,1,0:T(8,128)S(1)}, u32[]{:S(2)}, u32[]{:S(2)}) collective-permute-start(f32[18,128,128]{2,1,0:T(8,128)S(1)} %get-tuple-element.76), channel_id=1, source_target_pairs={{64,128},{192,256},{320,384},{128,64},{256,192},{384,320},{65,129}... | collective-permute-start | bytes 3538952 | tf_op jit(solution)/shard_map/ppermute | solution.py:392
  45.4 34.8 %collective-permute-start.10 = (f32[18,128,128]{2,1,0:T(8,128)S(1)}, f32[18,128,128]{2,1,0:T(8,128)S(1)}, u32[]{:S(2)}, u32[]{:S(2)}) collective-permute-start(f32[18,128,128]{2,1,0:T(8,128)S(1)} %get-tuple-element.74), channel_id=1, source_target_pairs={{0,64},{64,0},{128,192},{192,128},{256,320},{320,256},{384,448},{4... | collective-permute-start | bytes 3538952 | tf_op jit(solution)/shard_map/ppermute | solution.py:393
  73.3 7.6 %collective-permute-start.8 = (f32[128,128]{1,0:T(8,128)S(1)}, f32[128,128]{1,0:T(8,128)S(1)}, u32[]{:S(2)}, u32[]{:S(2)}) collective-permute-start(f32[128,128]{1,0:T(8,128)S(1)} %get-tuple-element.73), channel_id=1, source_target_pairs={{64,128},{192,256},{320,384},{128,64},{256,192},{384,320},{65,129}... | collective-permute-start | bytes 196616 | tf_op jit(solution)/shard_map/ppermute | solution.py:407
  78.3 3.1 %collective-permute-start.9 = (f32[128,128]{1,0:T(8,128)S(1)}, f32[128,128]{1,0:T(8,128)S(1)}, u32[]{:S(2)}, u32[]{:S(2)}) collective-permute-start(f32[128,128]{1,0:T(8,128)S(1)} %get-tuple-element.73), channel_id=1, source_target_pairs={{0,64},{64,0},{128,192},{192,128},{256,320},{320,256},{384,448},{4... | collective-permute-start | bytes 196616 | tf_op jit(solution)/shard_map/ppermute | solution.py:408

commit v9 on v7

--- a/solution.py
+++ b/solution.py
@@ -219,7 +219,7 @@
     kept_ref[...] = where(cols < jnp.broadcast_to(v4_ref[n : n + 1, :], (n, n)), state)
 
 
-def parts(x0_ref, x1_ref, sums_ref, pl_ref, pr_ref, energy_ref):
+def parts(x1_ref, x0_ref, sums_ref, pl_ref, pr_ref, energy_ref):
     n = x0_ref.shape[1]
     segment = odd("seg")
     for c in range(x0_ref.shape[0]):
@@ -351,7 +351,7 @@
     all_parts = SDS(((diags + hops) * n, 2 * n), bf16)
     p0, p1, energy = call(
         parts,
-        (x0, x1, sums),
+        (x1, x0, sums),
         [VMEM] * 3,
         [all_parts, all_parts, SDS((1,), f32)],
         out_specs=[VMEM, VMEM, SMEM],

time: 81.9 us -> 82.9 us (1.012)
  blocking collectives: 28.4 us -> 29.5 us
    ppermute x1, starting transfers between devices: 6.7 us -> 2.1 us  [shards(): x0 = lax.ppermute(lax.optimization_barrier((m0, b))[0], 'seg', chip)]
    ppermute x1, starting transfers between devices: 2.1 us -> 5.64 us  [shards(): x1 = lax.ppermute(lax.optimization_barrier((m1, b))[0], 'seg', across)]
    all_to_all x1, blocking collectives: 28.4 us -> 29.5 us  [shards(): lax.all_to_all(sums, 'blk', 0, 0, tiled=True, axis_index_groups=[members])]
    ppermute x1, starting transfers between devices: 4.03 us -> 4.93 us  [shards(): kept1 = lax.ppermute(kept, 'seg', across)]
where the time goes in v9:
time: 82.9 us; the launch traced here: 82.3 us
  starting transfers between devices  36.8 us (44%)
  blocking collectives  29.5 us (36%)
  Pallas kernels  13.2 us (16%)
  between operations  2.36 us (3%)
    all_to_all x1, blocking collectives, shards(): lax.all_to_all(sums, 'blk', 0, 0, tiled=True, axis_index_groups=[members])  29.5 us
    pallas_call x14, Pallas kernels, call(): pl.pallas_call(kernel, in_specs=specs, out_specs=out_specs or [VMEM] * le...  13.2 us
    ppermute x3, starting transfers between devices, shards(): got_a = lax.ppermute(a, 'blk', up)  12 us
    ppermute x1, starting transfers between devices, shards(): x1 = lax.ppermute(lax.optimization_barrier((m1, b))[0], 'seg', across)  5.64 us
    ppermute x4, starting transfers between devices, shards(): got_b = lax.ppermute(b, 'blk', down)  5.17 us
    ppermute x1, starting transfers between devices, shards(): below0 = lax.ppermute(lax.optimization_barrier((own, b))[0], 'blk', up)  5.06 us
    ppermute x1, starting transfers between devices, shards(): kept1 = lax.ppermute(kept, 'seg', across)  4.93 us
    ppermute x1, starting transfers between devices, shards(): x0 = lax.ppermute(lax.optimization_barrier((m0, b))[0], 'seg', chip)  2.1 us
  transfers between devices with their start and end apart: 12, of which 1 were waited for; matrix products, arithmetic and copies ran while one was open for 0% of the time, Pallas kernels for 11%

profile of v9, /device:TPU:1, one launch (start us, length us, event | category | flops | bytes accessed | tf_op | source)
XLA Modules:
  0.0 82.3 jit_solution(6656473453625775814)
XLA Ops:
  1.3 1.7 %load.1 = (f32[136,128]{1,0:T(8,128)S(1)}, f32[18,128,128]{2,1,0:T(8,128)S(1)}, f32[18,128,128]{2,1,0:T(8,128)S(1)}) custom-call(s32[1,1]{1,0:T(1,128)S(6)} %copy.12.size_ref, f32[128,128]{1,0:T(8,128)} %bitcast.19, f32[2,128,128]{2,1,0:T(8,128)} %bitcast.17, f32[16,128,128]{2,1,0:T(8,128)} %bitcast.15, f32[2,128,128]{2,1,0:T(8,128)} %bitcast.18, ...), custom_call_target="tpu_custom_call" | custom-call | bytes 4853764 | tf_op jit(solution)/shard_map/load/pallas_call | solution.py:262
  3.1 5.1 %collective-permute-start = (f32[136,128]{1,0:T(8,128)S(1)}, f32[136,128]{1,0:T(8,128)S(1)}, u32[]{:S(2)}, u32[]{:S(2)}) collective-permute-start(f32[136,128]{1,0:T(8,128)S(1)} %get-tuple-element.48.refs_0_.own_ref.refs_8_.refs_4_), channel_id=1, source_target_pairs={{0,1},{1,2},{2,3},{3,4},{4,5},{5,6},{6,7},{7,8},{8,9},{9,10},{10,1... | collective-permute-start | bytes 208904 | tf_op jit(solution)/shard_map/ppermute | solution.py:306
  8.1 1.0 %even_adjoint.1 = (bf16[2048,256]{1,0:T(8,128)(2,1)S(1)}, bf16[2048,256]{1,0:T(8,128)(2,1)S(1)}, bf16[256,256]{1,0:T(8,128)(2,1)S(1)}, bf16[256,256]{1,0:T(8,128)(2,1)S(1)}, f32[128,128]{1,0:T(8,128)S(1)}) custom-call(f32[136,128]{1,0:T(8,128)S(1)} %get-tuple-element.48.refs_0_.own_ref.refs_8_.refs_4_, f32[18,128,128]{2,1,0:T(8,128)S(1)} %get-tuple-element.60.refs_1_.m0_ref, ...), custom_call_target="tpu_custom_call" | custom-call | flops 10737418240 | bytes 4919296 | tf_op jit(solution)/shard_map/even_adjoint/pallas_call | solution.py:262
  9.2 1.3 %collective-permute-start.1 = (f32[128,128]{1,0:T(8,128)S(1)}, f32[128,128]{1,0:T(8,128)S(1)}, u32[]{:S(2)}, u32[]{:S(2)}) collective-permute-start(f32[128,128]{1,0:T(8,128)S(1)} %get-tuple-element.49.refs_12_), channel_id=1, source_target_pairs={{1,0},{2,1},{3,2},{4,3},{5,4},{6,5},{7,6},{8,7},{9,8},{10,9},{11,1... | collective-permute-start | bytes 196616 | tf_op jit(solution)/shard_map/ppermute | solution.py:310
  11.1 0.0 collective-permute-done.refs_9_
  11.1 1.1 %apply0.1.refs_5_ = f32[128,128]{1,0:T(8,128)S(1)} custom-call(bf16[2048,256]{1,0:T(8,128)(2,1)S(1)} %get-tuple-element.39.refs_0_, bf16[2048,256]{1,0:T(8,128)(2,1)S(1)} %get-tuple-element.40.refs_1_, bf16[256,256]{1,0:T(8,128)(2,1)S(1)} %get-tuple-element.44.refs_2_, bf16[256,256]{1,0:T(8,128)(2,1)S(1)} %get-tuple-element.45.refs_3_, ...), custom_call_target="tpu_custom_call" | custom-call | flops 12079595520 | bytes 4923392 | tf_op jit(solution)/shard_map/apply0/pallas_call | solution.py:262
  12.2 4.0 %collective-permute-start.2 = (f32[128,128]{1,0:T(8,128)S(1)}, f32[128,128]{1,0:T(8,128)S(1)}, u32[]{:S(2)}, u32[]{:S(2)}) collective-permute-start(f32[128,128]{1,0:T(8,128)S(1)} %apply0.1.refs_5_), channel_id=1, source_target_pairs={{0,1},{1,2},{2,3},{3,4},{4,5},{5,6},{6,7},{7,8},{8,9},{9,10},{10,1... | collective-permute-start | bytes 196616 | tf_op jit(solution)/shard_map/ppermute | solution.py:322
  16.2 0.0 collective-permute-done.1.refs_6_
  16.2 0.9 %adjoint1.1 = (f32[128,128]{1,0:T(8,128)S(1)}, f32[128,128]{1,0:T(8,128)S(1)}) custom-call(bf16[2048,256]{1,0:T(8,128)(2,1)S(1)} %get-tuple-element.39.refs_0_, bf16[2048,256]{1,0:T(8,128)(2,1)S(1)} %get-tuple-element.40.refs_1_, bf16[2048,256]{1,0:T(8,128)(2,1)S(1)} %get-tuple-element.42.refs_4_.refs_2_, ...), custom_call_target="tpu_custom_call" | custom-call | flops 10737418240 | bytes 4526080 | tf_op jit(solution)/shard_map/adjoint1/pallas_call | solution.py:262
  17.1 1.3 %collective-permute-start.3 = (f32[128,128]{1,0:T(8,128)S(1)}, f32[128,128]{1,0:T(8,128)S(1)}, u32[]{:S(2)}, u32[]{:S(2)}) collective-permute-start(f32[128,128]{1,0:T(8,128)S(1)} %get-tuple-element.51.refs_12_), channel_id=1, source_target_pairs={{1,0},{2,1},{3,2},{4,3},{5,4},{6,5},{7,6},{8,7},{9,8},{10,9},{11,1... | collective-permute-start | bytes 196616 | tf_op jit(solution)/shard_map/ppermute | solution.py:332
  18.4 0.0 collective-permute-done.2.refs_11_
  18.5 1.1 %apply1.1.refs_5_ = f32[128,128]{1,0:T(8,128)S(1)} custom-call(bf16[2048,256]{1,0:T(8,128)(2,1)S(1)} %get-tuple-element.39.refs_0_, bf16[2048,256]{1,0:T(8,128)(2,1)S(1)} %get-tuple-element.40.refs_1_, bf16[256,256]{1,0:T(8,128)(2,1)S(1)} %get-tuple-element.44.refs_2_, bf16[256,256]{1,0:T(8,128)(2,1)S(1)} %get-tuple-element.45.refs_3_, ...), custom_call_target="tpu_custom_call" | custom-call | flops 12079595520 | bytes 5120000 | tf_op jit(solution)/shard_map/apply1/pallas_call | solution.py:262
  19.5 4.0 %collective-permute-start.4 = (f32[128,128]{1,0:T(8,128)S(1)}, f32[128,128]{1,0:T(8,128)S(1)}, u32[]{:S(2)}, u32[]{:S(2)}) collective-permute-start(f32[128,128]{1,0:T(8,128)S(1)} %apply1.1.refs_5_), channel_id=1, source_target_pairs={{0,1},{1,2},{2,3},{3,4},{4,5},{5,6},{6,7},{7,8},{8,9},{9,10},{10,1... | collective-permute-start | bytes 196616 | tf_op jit(solution)/shard_map/ppermute | solution.py:322
  23.5 0.0 collective-permute-done.3.refs_6_
  23.5 0.9 %adjoint2.1 = (f32[128,128]{1,0:T(8,128)S(1)}, f32[128,128]{1,0:T(8,128)S(1)}) custom-call(bf16[2048,256]{1,0:T(8,128)(2,1)S(1)} %get-tuple-element.39.refs_0_, bf16[2048,256]{1,0:T(8,128)(2,1)S(1)} %get-tuple-element.40.refs_1_, bf16[2048,256]{1,0:T(8,128)(2,1)S(1)} %get-tuple-element.42.refs_4_.refs_2_, ...), custom_call_target="tpu_custom_call" | custom-call | flops 10737418240 | bytes 4526080 | tf_op jit(solution)/shard_map/adjoint2/pallas_call | solution.py:262
  24.5 1.3 %collective-permute-start.5 = (f32[128,128]{1,0:T(8,128)S(1)}, f32[128,128]{1,0:T(8,128)S(1)}, u32[]{:S(2)}, u32[]{:S(2)}) collective-permute-start(f32[128,128]{1,0:T(8,128)S(1)} %get-tuple-element.53.refs_12_), channel_id=1, source_target_pairs={{1,0},{2,1},{3,2},{4,3},{5,4},{6,5},{7,6},{8,7},{9,8},{10,9},{11,1... | collective-permute-start | bytes 196616 | tf_op jit(solution)/shard_map/ppermute | solution.py:332
  25.8 0.0 collective-permute-done.4.refs_11_
  25.8 1.1 %apply2.1.refs_5_ = f32[128,128]{1,0:T(8,128)S(1)} custom-call(bf16[2048,256]{1,0:T(8,128)(2,1)S(1)} %get-tuple-element.39.refs_0_, bf16[2048,256]{1,0:T(8,128)(2,1)S(1)} %get-tuple-element.40.refs_1_, bf16[256,256]{1,0:T(8,128)(2,1)S(1)} %get-tuple-element.44.refs_2_, bf16[256,256]{1,0:T(8,128)(2,1)S(1)} %get-tuple-element.45.refs_3_, ...), custom_call_target="tpu_custom_call" | custom-call | flops 12079595520 | bytes 5120000 | tf_op jit(solution)/shard_map/apply2/pallas_call | solution.py:262
  26.9 4.0 %collective-permute-start.6 = (f32[128,128]{1,0:T(8,128)S(1)}, f32[128,128]{1,0:T(8,128)S(1)}, u32[]{:S(2)}, u32[]{:S(2)}) collective-permute-start(f32[128,128]{1,0:T(8,128)S(1)} %apply2.1.refs_5_), channel_id=1, source_target_pairs={{0,1},{1,2},{2,3},{3,4},{4,5},{5,6},{6,7},{7,8},{8,9},{9,10},{10,1... | collective-permute-start | bytes 196616 | tf_op jit(solution)/shard_map/ppermute | solution.py:322
  30.9 0.0 collective-permute-done.5.refs_6_
  30.9 0.9 %adjoint3.1 = (f32[128,128]{1,0:T(8,128)S(1)}, f32[128,128]{1,0:T(8,128)S(1)}) custom-call(bf16[2048,256]{1,0:T(8,128)(2,1)S(1)} %get-tuple-element.39.refs_0_, bf16[2048,256]{1,0:T(8,128)(2,1)S(1)} %get-tuple-element.40.refs_1_, bf16[2048,256]{1,0:T(8,128)(2,1)S(1)} %get-tuple-element.42.refs_4_.refs_2_, ...), custom_call_target="tpu_custom_call" | custom-call | flops 10737418240 | bytes 4526080 | tf_op jit(solution)/shard_map/adjoint3/pallas_call | solution.py:262
  31.8 1.3 %collective-permute-start.7 = (f32[128,128]{1,0:T(8,128)S(1)}, f32[128,128]{1,0:T(8,128)S(1)}, u32[]{:S(2)}, u32[]{:S(2)}) collective-permute-start(f32[128,128]{1,0:T(8,128)S(1)} %get-tuple-element.55), channel_id=1, source_target_pairs={{1,0},{2,1},{3,2},{4,3},{5,4},{6,5},{7,6},{8,7},{9,8},{10,9},{11,1... | collective-permute-start | bytes 196616 | tf_op jit(solution)/shard_map/ppermute | solution.py:332
  33.1 5.6 %collective-permute-start.10 = (f32[18,128,128]{2,1,0:T(8,128)S(1)}, f32[18,128,128]{2,1,0:T(8,128)S(1)}, u32[]{:S(2)}, u32[]{:S(2)}) collective-permute-start(f32[18,128,128]{2,1,0:T(8,128)S(1)} %get-tuple-element.59.refs_2_.m1_ref), channel_id=1, source_target_pairs={{64,128},{192,256},{320,384},{128,64},{256,192},{384,320},{65,129}... | collective-permute-start | bytes 3538952 | tf_op jit(solution)/shard_map/ppermute | solution.py:334
  38.8 2.1 %collective-permute-start.11 = (f32[18,128,128]{2,1,0:T(8,128)S(1)}, f32[18,128,128]{2,1,0:T(8,128)S(1)}, u32[]{:S(2)}, u32[]{:S(2)}) collective-permute-start(f32[18,128,128]{2,1,0:T(8,128)S(1)} %get-tuple-element.60.refs_1_.m0_ref), channel_id=1, source_target_pairs={{0,64},{64,0},{128,192},{192,128},{256,320},{320,256},{384,448},{4... | collective-permute-start | bytes 3538952 | tf_op jit(solution)/shard_map/ppermute | solution.py:335
  40.9 0.0 collective-permute-done.6.refs_11_
  40.9 1.1 %apply3.1.part_ref = f32[128,128]{1,0:T(8,128)S(1)} custom-call(bf16[2048,256]{1,0:T(8,128)(2,1)S(1)} %get-tuple-element.39.refs_0_, bf16[2048,256]{1,0:T(8,128)(2,1)S(1)} %get-tuple-element.40.refs_1_, bf16[256,256]{1,0:T(8,128)(2,1)S(1)} %get-tuple-element.44.refs_2_, bf16[256,256]{1,0:T(8,128)(2,1)S(1)} %get-tuple-element.45.refs_3_, ...), custom_call_target="tpu_custom_call" | custom-call | flops 12079595520 | bytes 5120000 | tf_op jit(solution)/shard_map/apply3/pallas_call | solution.py:262
  42.0 0.0 collective-permute-done.7.got_b_ref
  42.0 0.1 finish.1
  42.1 29.5 %all_to_all.11 = f32[64,1,128]{2,1,0:T(1,128)S(1)} all-to-all(f32[64,1,128]{2,1,0:T(1,128)S(1)} %bitcast.14), channel_id=1, replica_groups={{36,37,38,39,40,41,42,43,44,45,46,47,48,49,50,51,52,53,54,55,56,57,58,5..., dimensions={0} | all-to-all | bytes 65536 | tf_op jit(solution)/shard_map/all_to_all | solution.py:347
  71.6 0.1 normalise.1
  71.7 4.9 %collective-permute-start.8 = (f32[128,128]{1,0:T(8,128)S(1)}, f32[128,128]{1,0:T(8,128)S(1)}, u32[]{:S(2)}, u32[]{:S(2)}) collective-permute-start(f32[128,128]{1,0:T(8,128)S(1)} %get-tuple-element.58), channel_id=1, source_target_pairs={{64,128},{192,256},{320,384},{128,64},{256,192},{384,320},{65,129}... | collective-permute-start | bytes 196616 | tf_op jit(solution)/shard_map/ppermute | solution.py:349
  76.6 1.9 %collective-permute-start.9 = (f32[128,128]{1,0:T(8,128)S(1)}, f32[128,128]{1,0:T(8,128)S(1)}, u32[]{:S(2)}, u32[]{:S(2)}) collective-permute-start(f32[128,128]{1,0:T(8,128)S(1)} %get-tuple-element.58), channel_id=1, source_target_pairs={{0,64},{64,0},{128,192},{192,128},{256,320},{320,256},{384,448},{4... | collective-permute-start | bytes 196616 | tf_op jit(solution)/shard_map/ppermute | solution.py:350
  78.6 0.0 collective-permute-done.10.x1_ref
  78.6 0.0 collective-permute-done.11.x0_ref
  78.6 0.7 parts.1
  79.3 0.0 collective-permute-done.8.kept1_ref
  79.3 0.5 collective-permute-done.9.kept0_ref
  79.8 2.4 %extend.1 = (f32[128,128]{1,0:T(8,128)}, f32[18,128,128]{2,1,0:T(8,128)}, f32[18,128,128]{2,1,0:T(8,128)}) custom-call(f32[128,128]{1,0:T(8,128)S(1)} %collective-permute-done.8.kept1_ref, f32[128,128]{1,0:T(8,128)S(1)} %collective-permute-done.9.kept0_ref, bf16[2304,256]{1,0:T(8,128)(2,1)S(1)} %get-tuple-element.61.pl_ref, ...), custom_call_target="tpu_custom_call" | custom-call | flops 24159191040 | bytes 4980736 | tf_op jit(solution)/shard_map/extend/pallas_call | solution.py:262
  (1 shorter events, 0.0 us)
Async XLA Ops:
  3.1 8.1 %collective-permute-start = (f32[136,128]{1,0:T(8,128)S(1)}, f32[136,128]{1,0:T(8,128)S(1)}, u32[]{:S(2)}, u32[]{:S(2)}) collective-permute-start(f32[136,128]{1,0:T(8,128)S(1)} %get-tuple-element.48.refs_0_.own_ref.refs_8_.refs_4_), channel_id=1, source_target_pairs={{0,1},{1,2},{2,3},{3,4},{4,5},{5,6},{6,7},{7,8},{8,9},{9,10},{10,1... | collective-permute-start | bytes 208904 | tf_op jit(solution)/shard_map/ppermute | solution.py:306
  9.2 7.0 %collective-permute-start.1 = (f32[128,128]{1,0:T(8,128)S(1)}, f32[128,128]{1,0:T(8,128)S(1)}, u32[]{:S(2)}, u32[]{:S(2)}) collective-permute-start(f32[128,128]{1,0:T(8,128)S(1)} %get-tuple-element.49.refs_12_), channel_id=1, source_target_pairs={{1,0},{2,1},{3,2},{4,3},{5,4},{6,5},{7,6},{8,7},{9,8},{10,9},{11,1... | collective-permute-start | bytes 196616 | tf_op jit(solution)/shard_map/ppermute | solution.py:310
  12.2 6.3 %collective-permute-start.2 = (f32[128,128]{1,0:T(8,128)S(1)}, f32[128,128]{1,0:T(8,128)S(1)}, u32[]{:S(2)}, u32[]{:S(2)}) collective-permute-start(f32[128,128]{1,0:T(8,128)S(1)} %apply0.1.refs_5_), channel_id=1, source_target_pairs={{0,1},{1,2},{2,3},{3,4},{4,5},{5,6},{6,7},{7,8},{8,9},{9,10},{10,1... | collective-permute-start | bytes 196616 | tf_op jit(solution)/shard_map/ppermute | solution.py:322
  17.1 6.4 %collective-permute-start.3 = (f32[128,128]{1,0:T(8,128)S(1)}, f32[128,128]{1,0:T(8,128)S(1)}, u32[]{:S(2)}, u32[]{:S(2)}) collective-permute-start(f32[128,128]{1,0:T(8,128)S(1)} %get-tuple-element.51.refs_12_), channel_id=1, source_target_pairs={{1,0},{2,1},{3,2},{4,3},{5,4},{6,5},{7,6},{8,7},{9,8},{10,9},{11,1... | collective-permute-start | bytes 196616 | tf_op jit(solution)/shard_map/ppermute | solution.py:332
  19.5 6.3 %collective-permute-start.4 = (f32[128,128]{1,0:T(8,128)S(1)}, f32[128,128]{1,0:T(8,128)S(1)}, u32[]{:S(2)}, u32[]{:S(2)}) collective-permute-start(f32[128,128]{1,0:T(8,128)S(1)} %apply1.1.refs_5_), channel_id=1, source_target_pairs={{0,1},{1,2},{2,3},{3,4},{4,5},{5,6},{6,7},{7,8},{8,9},{9,10},{10,1... | collective-permute-start | bytes 196616 | tf_op jit(solution)/shard_map/ppermute | solution.py:322
  24.5 6.4 %collective-permute-start.5 = (f32[128,128]{1,0:T(8,128)S(1)}, f32[128,128]{1,0:T(8,128)S(1)}, u32[]{:S(2)}, u32[]{:S(2)}) collective-permute-start(f32[128,128]{1,0:T(8,128)S(1)} %get-tuple-element.53.refs_12_), channel_id=1, source_target_pairs={{1,0},{2,1},{3,2},{4,3},{5,4},{6,5},{7,6},{8,7},{9,8},{10,9},{11,1... | collective-permute-start | bytes 196616 | tf_op jit(solution)/shard_map/ppermute | solution.py:332
  26.9 14.0 %collective-permute-start.6 = (f32[128,128]{1,0:T(8,128)S(1)}, f32[128,128]{1,0:T(8,128)S(1)}, u32[]{:S(2)}, u32[]{:S(2)}) collective-permute-start(f32[128,128]{1,0:T(8,128)S(1)} %apply2.1.refs_5_), channel_id=1, source_target_pairs={{0,1},{1,2},{2,3},{3,4},{4,5},{5,6},{6,7},{7,8},{8,9},{9,10},{10,1... | collective-permute-start | bytes 196616 | tf_op jit(solution)/shard_map/ppermute | solution.py:322
  31.8 10.1 %collective-permute-start.7 = (f32[128,128]{1,0:T(8,128)S(1)}, f32[128,128]{1,0:T(8,128)S(1)}, u32[]{:S(2)}, u32[]{:S(2)}) collective-permute-start(f32[128,128]{1,0:T(8,128)S(1)} %get-tuple-element.55), channel_id=1, source_target_pairs={{1,0},{2,1},{3,2},{4,3},{5,4},{6,5},{7,6},{8,7},{9,8},{10,9},{11,1... | collective-permute-start | bytes 196616 | tf_op jit(solution)/shard_map/ppermute | solution.py:332
  33.1 45.4 %collective-permute-start.10 = (f32[18,128,128]{2,1,0:T(8,128)S(1)}, f32[18,128,128]{2,1,0:T(8,128)S(1)}, u32[]{:S(2)}, u32[]{:S(2)}) collective-permute-start(f32[18,128,128]{2,1,0:T(8,128)S(1)} %get-tuple-element.59.refs_2_.m1_ref), channel_id=1, source_target_pairs={{64,128},{192,256},{320,384},{128,64},{256,192},{384,320},{65,129}... | collective-permute-start | bytes 3538952 | tf_op jit(solution)/shard_map/ppermute | solution.py:334
  38.8 39.8 %collective-permute-start.11 = (f32[18,128,128]{2,1,0:T(8,128)S(1)}, f32[18,128,128]{2,1,0:T(8,128)S(1)}, u32[]{:S(2)}, u32[]{:S(2)}) collective-permute-start(f32[18,128,128]{2,1,0:T(8,128)S(1)} %get-tuple-element.60.refs_1_.m0_ref), channel_id=1, source_target_pairs={{0,64},{64,0},{128,192},{192,128},{256,320},{320,256},{384,448},{4... | collective-permute-start | bytes 3538952 | tf_op jit(solution)/shard_map/ppermute | solution.py:335
  71.7 7.6 %collective-permute-start.8 = (f32[128,128]{1,0:T(8,128)S(1)}, f32[128,128]{1,0:T(8,128)S(1)}, u32[]{:S(2)}, u32[]{:S(2)}) collective-permute-start(f32[128,128]{1,0:T(8,128)S(1)} %get-tuple-element.58), channel_id=1, source_target_pairs={{64,128},{192,256},{320,384},{128,64},{256,192},{384,320},{65,129}... | collective-permute-start | bytes 196616 | tf_op jit(solution)/shard_map/ppermute | solution.py:349
  76.6 3.1 %collective-permute-start.9 = (f32[128,128]{1,0:T(8,128)S(1)}, f32[128,128]{1,0:T(8,128)S(1)}, u32[]{:S(2)}, u32[]{:S(2)}) collective-permute-start(f32[128,128]{1,0:T(8,128)S(1)} %get-tuple-element.58), channel_id=1, source_target_pairs={{0,64},{64,0},{128,192},{192,128},{256,320},{320,256},{384,448},{4... | collective-permute-start | bytes 196616 | tf_op jit(solution)/shard_map/ppermute | solution.py:350
